TPU v7x, 32 devices: a whole 2x2x4 slice. The times are simulated.
32 devices in a mesh: boxes: 2 (over y), gx: 4 (over z), gy: 2 (over x), gz: 2 (over core).
Axes of the slice: x: 2, y: 2, z: 4, core: 2. Of those that a mesh axis runs over, the one named last changes fastest.
Arguments:
- density: float32 [64, 8, 256], P(('boxes', 'gx'), 'gy', 'gz'), parts along dimension 0, may hold values from 0.2 to 7, as said below
- external: float32 [64, 8, 256], P(('boxes', 'gx'), 'gy', 'gz'), parts along dimension 0, may hold values from -4 to 4
- w_first: bfloat16 [27, 32], replicated, may hold values from -1.25 to 1.25
- w_second: bfloat16 [27, 32, 32], replicated, may hold values from -0.21875 to 0.21875
- w_third: bfloat16 [27, 32, 32], replicated, may hold values from -0.21875 to 0.21875
- w_last: bfloat16 [27, 32], replicated, may hold values from -0.21875 to 0.21875
Outputs:
- new_density: float32 [64, 8, 256], P(('boxes', 'gx'), 'gy', 'gz'), parts along dimension 0
- potential: float32 [64, 8, 256], P(('boxes', 'gx'), 'gy', 'gz'), parts along dimension 0
- chem_potential: float32 [4], P('boxes'), parts along dimension 0
- stress: float32 [4, 3, 3], P('boxes'), parts along dimension 0
There are 2 independent parts, one for each index of `boxes`. A program takes and returns all parts, laid end to end along the dimension named above; an argument that names none is the same for every part. Nothing has to cross between parts.
Inputs may be any that keep to these rules, and one draw needn't show every extreme that they name: Electron density of each cell, positive.
All inputs are finite; a program needn't handle non-finite values.
Results may differ from a plain program's by a relative error of at most 0.0024.
Values may be sent and summed in bfloat16 or wider, within the bound.
No kernel may reach another device: no remote copies, remote signals or barrier semaphores. Data moves between devices by JAX's collectives and lax.ppermute only.
A program may use at most 64 MiB of HBM per device.

v0:
```python
import jax
import jax.numpy as jnp
from jax import lax
from jax.sharding import PartitionSpec as P

STEPS = 2


C_TF = 2.871234
C_X = 0.7385588
TAU = 0.1
OFFSETS = [
    (along_x - 1, along_y - 1, along_z - 1)
    for along_x in range(3)
    for along_y in range(3)
    for along_z in range(3)
]


def padded_2(cells, sides, width):
    for axis, dim in sides:
        count = lax.axis_size(axis)
        head = lax.slice_in_dim(cells, 0, width, axis=dim)
        tail = lax.slice_in_dim(cells, cells.shape[dim] - width, cells.shape[dim], axis=dim)
        cells = jnp.concatenate(
            [
                lax.ppermute(tail, axis, [(i, (i + 1) % count) for i in range(count)]),
                cells,
                lax.ppermute(head, axis, [((i + 1) % count, i) for i in range(count)]),
            ],
            axis=dim,
        )
    return cells


def silu_slope(argument):
    logistic = jax.nn.sigmoid(argument)
    return logistic * (1.0 + argument * (1.0 - logistic))


def start_of(offset, direction):
    return (1 + direction * offset[0], 1 + direction * offset[1], 1 + direction * offset[2])


def pad_field(field):
    return padded_2(field, (("gx", 0), ("gy", 1), ("gz", 2)), 1)


def pad_channels(activity):
    return padded_2(activity, (("gx", 1), ("gy", 2), ("gz", 3)), 1)


def dense_apply(padded, weights, direction):
    kernel_taps = weights.reshape(3, 3, 3, weights.shape[1], weights.shape[2])
    if direction > 0:
        kernel_block = jnp.transpose(kernel_taps, (3, 4, 0, 1, 2))
    else:
        kernel_block = jnp.transpose(kernel_taps[::-1, ::-1, ::-1], (4, 3, 0, 1, 2))
    convolved = lax.conv_general_dilated(
        padded[None],
        kernel_block,
        (1, 1, 1),
        "VALID",
        dimension_numbers=("NCDHW", "OIDHW", "NCDHW"),
        preferred_element_type=jnp.float32,
    )
    return convolved[0]


def single_apply(padded, weights, direction):
    inner = tuple((extent - 2 for extent in padded.shape))
    pieces = []
    for offset in OFFSETS:
        begin = start_of(offset, direction)
        pieces.append(
            padded[
                begin[0] : begin[0] + inner[0],
                begin[1] : begin[1] + inner[1],
                begin[2] : begin[2] + inner[2],
            ]
        )
    stacked = jnp.stack(pieces)
    return jnp.einsum(
        "dc,dxyz->cxyz",
        weights.astype(jnp.float32),
        stacked,
        precision=lax.Precision.HIGHEST,
        preferred_element_type=jnp.float32,
    )


def narrow_planes(padded, weights):
    return jnp.einsum("dc,cxyz->dxyz", weights, padded, preferred_element_type=jnp.float32)


def fold_planes(planes, factors, direction):
    inner = tuple((extent - 2 for extent in planes.shape[1:]))
    summed = jnp.zeros(inner, jnp.float32)
    for ordinal, offset in enumerate(OFFSETS):
        if factors[ordinal] != 0.0:
            begin = start_of(offset, direction)
            summed = (
                summed
                + factors[ordinal]
                * planes[
                    ordinal,
                    begin[0] : begin[0] + inner[0],
                    begin[1] : begin[1] + inner[1],
                    begin[2] : begin[2] + inner[2],
                ]
            )
    return summed


def evaluate(current, external, w_first, w_second, w_third, w_last):
    cube = jnp.cbrt(current)
    act_three_pad = None
    cube_pad = pad_field(cube)
    pre_one = single_apply(cube_pad, w_first, 1)
    act_one = jax.nn.silu(pre_one).astype(jnp.bfloat16)
    pre_two = dense_apply(pad_channels(act_one), w_second, 1)
    act_two = jax.nn.silu(pre_two).astype(jnp.bfloat16)
    pre_three = dense_apply(pad_channels(act_two), w_third, 1)
    act_three = jax.nn.silu(pre_three).astype(jnp.bfloat16)
    act_three_pad = pad_channels(act_three)
    enhance = fold_planes(narrow_planes(act_three_pad, w_last), [1.0] * 27, 1)
    source = current * cube * cube
    back_three = single_apply(pad_field(source), w_last, -1)
    delta_three = (back_three * silu_slope(pre_three)).astype(jnp.bfloat16)
    back_two = dense_apply(pad_channels(delta_three), w_third, -1)
    delta_two = (back_two * silu_slope(pre_two)).astype(jnp.bfloat16)
    back_one = dense_apply(pad_channels(delta_two), w_second, -1)
    delta_one = (back_one * silu_slope(pre_one)).astype(jnp.bfloat16)
    lever_factors = [[float(offset[axis_no]) for offset in OFFSETS] for axis_no in range(3)]
    planes_one = narrow_planes(pad_channels(delta_one), w_first)
    cotangent = fold_planes(planes_one, [1.0] * 27, -1)
    levers = [fold_planes(planes_one, factors, -1) for factors in lever_factors]
    potential = (
        5.0 / 3.0 * cube * cube * (C_TF + enhance)
        + cotangent / (3.0 * cube * cube)
        + external
        - 4.0 / 3.0 * C_X * cube
    )
    energy_part = jnp.sum(source * (C_TF + enhance) + external * current - C_X * current * cube)
    virial_part = jnp.sum(current * potential)
    slopes = [
        (cube_pad[2:, 1:-1, 1:-1] - cube_pad[:-2, 1:-1, 1:-1]) * 0.5,
        (cube_pad[1:-1, 2:, 1:-1] - cube_pad[1:-1, :-2, 1:-1]) * 0.5,
        (cube_pad[1:-1, 1:-1, 2:] - cube_pad[1:-1, 1:-1, :-2]) * 0.5,
    ]
    moment_parts = [
        jnp.sum(slopes[row_no] * levers[col_no]) for row_no in range(3) for col_no in range(3)
    ]
    stress_part = jnp.stack([energy_part - virial_part] + moment_parts)
    weighted = current * jnp.exp(-TAU * potential)
    norm_part = jnp.sum(weighted)
    return (potential, weighted, norm_part, stress_part)


def on_device(density, external, w_first, w_second, w_third, w_last):
    cells_x, cells_y, cells_z = density.shape
    cell_count = (
        cells_x
        * lax.axis_size("gx")
        * cells_y
        * lax.axis_size("gy")
        * cells_z
        * lax.axis_size("gz")
    )
    mass_part = jnp.sum(density)
    current = density
    potential = density
    chem_list = []
    stress_rows = []
    for repeat_count in range(STEPS):
        potential, weighted, norm_part, stress_part = evaluate(
            current, external, w_first, w_second, w_third, w_last
        )
        totals = lax.psum((jnp.stack([norm_part, mass_part]), stress_part), ("gx", "gy", "gz"))
        norm = totals[0][0]
        total_mass = totals[0][1]
        stress_rows.append(totals[1])
        chem_list.append(jnp.log(total_mass / norm) / TAU)
        current = weighted * (total_mass / norm)
    stress_all = jnp.stack(stress_rows)
    moments = stress_all[:, 1:].reshape(stress_all.shape[0], 3, 3)
    stress = (
        moments + jnp.eye(3, dtype=jnp.float32)[None] * stress_all[:, 0][:, None, None]
    ) / cell_count
    return (current, potential, jnp.stack(chem_list), stress)


def solution(mesh):
    in_specs = (P(("boxes", "gx"), "gy", "gz"), P(("boxes", "gx"), "gy", "gz"), P(), P(), P(), P())
    out_specs = (
        P(("boxes", "gx"), "gy", "gz"),
        P(("boxes", "gx"), "gy", "gz"),
        P("boxes"),
        P("boxes", None, None),
    )
    return jax.shard_map(
        on_device, mesh=mesh, in_specs=in_specs, out_specs=out_specs, check_vma=False
    )
```

profile of v0, /device:TPU:0, one launch (start us, length us, event | category | flops | bytes accessed | tf_op | source)
XLA Modules:
  0.0 437.4 jit_solution(16269450500948980255)
XLA Ops:
  1.5 3.1 collective-permute-start
  6.6 3.8 collective-permute-start.25
  22.2 4.0 collective-permute-start.7
  30.0 2.4 collective-permute-done.8
  37.1 4.1 reshape.81
  41.2 5.1 %copy.100 = bf16[32,10,6,1,8,17]{0,4,5,2,1,3:T(8,128)(2,1)S(1)} copy(bf16[32,10,6,1,8,17]{5,4,0,2,1,3:T(8,128)(2,1)} %reshape.81) | data formatting | bytes 1044480 | tf_op jit(solution)/shard_map/conv_general_dilated | solution.py:59
  46.4 4.1 fusion.85
  53.7 3.4 collective-permute-start.13
  68.4 4.1 reshape.88
  72.4 5.1 %copy.104 = bf16[32,10,6,1,8,17]{0,4,5,2,1,3:T(8,128)(2,1)S(1)} copy(bf16[32,10,6,1,8,17]{5,4,0,2,1,3:T(8,128)(2,1)} %reshape.88) | data formatting | bytes 1044480 | tf_op jit(solution)/shard_map/conv_general_dilated | solution.py:59
  77.6 4.1 fusion.82
  87.0 3.3 collective-permute-start.31
  94.0 2.5 collective-permute-done.32
  101.2 4.1 reshape.95
  105.3 5.1 %copy.111 = bf16[32,10,6,1,8,17]{0,4,5,2,1,3:T(8,128)(2,1)S(1)} copy(bf16[32,10,6,1,8,17]{5,4,0,2,1,3:T(8,128)(2,1)} %reshape.95) | data formatting | bytes 1044480 | tf_op jit(solution)/shard_map/conv_general_dilated | solution.py:59
  110.4 4.4 %fusion.79 = f32[8,4,8,17,32]{4,2,3,1,0:T(8,128)S(1)} fusion(bf16[3,3,3,32,32]{4,3,2,1,0:T(8,128)(2,1)S(1)} %bitcast.1625, bf16[32,10,6,1,7,2]{0,4,5,2,1,3:T(8,128)(2,1)S(1)} %slice.1599, bf16[32,10,6,1,8,17]{0,4,5,2,1,3:T(8,128)(2,1)S(1)} %copy.111, pred[8,17]{0,1:T(8,128)(4,1)S(1)} %copy-done.33), kind=kOutput, calls=%fused_computation.66 | convolution fusion | flops 242538496 | bytes 1188488 | tf_op jit(solution)/shard_map/conv_general_dilated | solution.py:59
  120.4 2.7 collective-permute-start.37
  128.4 2.8 collective-permute-start.19
  136.5 4.1 reshape.102
  140.6 5.1 %copy.115 = bf16[32,10,6,1,8,17]{0,4,5,2,1,3:T(8,128)(2,1)S(1)} copy(bf16[32,10,6,1,8,17]{5,4,0,2,1,3:T(8,128)(2,1)} %reshape.102) | data formatting | bytes 1044480 | tf_op jit(solution)/shard_map/conv_general_dilated | solution.py:59
  145.8 4.4 fusion.76
  155.0 2.9 collective-permute-start.43
  174.2 33.6 %psum.28 = f32[2]{0:T(128)S(1)} all-reduce(f32[2]{0:T(128)S(1)} %pad_maximum_fusion.81), channel_id=1, replica_groups=mesh['boxes'=2,'gx'=4,'gy'=2,'gz'=2] {'gx','gy','gz'}, use_global_device_ids=true, to_apply=%region_2.3 | all-reduce | flops 2 | bytes 16 | tf_op jit(solution)/shard_map/psum | solution.py:179
  209.9 3.8 collective-permute-start.49
  213.8 3.8 collective-permute-start.73
  228.2 4.2 collective-permute-start.55
  236.1 3.2 collective-permute-done.56
  244.3 4.1 reshape.109
  248.4 5.1 %copy.122 = bf16[32,10,6,1,8,17]{0,4,5,2,1,3:T(8,128)(2,1)S(1)} copy(bf16[32,10,6,1,8,17]{5,4,0,2,1,3:T(8,128)(2,1)} %reshape.109) | data formatting | bytes 1044480 | tf_op jit(solution)/shard_map/conv_general_dilated | solution.py:59
  253.6 4.1 fusion.73
  260.9 3.4 collective-permute-start.61
  275.4 4.1 reshape.116
  279.5 5.1 %copy.126 = bf16[32,10,6,1,8,17]{0,4,5,2,1,3:T(8,128)(2,1)S(1)} copy(bf16[32,10,6,1,8,17]{5,4,0,2,1,3:T(8,128)(2,1)} %reshape.116) | data formatting | bytes 1044480 | tf_op jit(solution)/shard_map/conv_general_dilated | solution.py:59
  284.6 4.1 fusion.70
  294.0 2.9 collective-permute-start.79
  305.9 2.4 multiply_reduce_fusion.16
  309.6 6.4 %stack.566 = f32[10]{0:T(128)} concatenate(f32[1]{0:T(128)} %bitcast.273, f32[1]{0:T(128)} %bitcast.277, f32[1]{0:T(128)} %bitcast.278, f32[1]{0:T(128)} %bitcast.280, f32[1]{0:T(128)} %bitcast.281, f32[1]{0:T(128)} %bitcast.282, f32[1]{0:T(128)} %bitcast.283, f32[1]{0:T(128)} %bitcast.284, f32[1]{0:T(128)} %bitcast.285, f32[1]{0:T(128)} %bitcast.286), dimensions={0} | concatenate | bytes 80 | tf_op jit(solution)/shard_map/stack | solution.py:154
  317.9 4.1 reshape.123
  322.0 5.1 %copy.133 = bf16[32,10,6,1,8,17]{0,4,5,2,1,3:T(8,128)(2,1)S(1)} copy(bf16[32,10,6,1,8,17]{5,4,0,2,1,3:T(8,128)(2,1)} %reshape.123) | data formatting | bytes 1044480 | tf_op jit(solution)/shard_map/conv_general_dilated | solution.py:59
  327.2 4.4 fusion.67
  337.1 2.7 collective-permute-start.85
  345.0 2.9 collective-permute-start.67
  353.2 4.1 reshape.130
  357.3 5.1 %copy.137 = bf16[32,10,6,1,8,17]{0,4,5,2,1,3:T(8,128)(2,1)S(1)} copy(bf16[32,10,6,1,8,17]{5,4,0,2,1,3:T(8,128)(2,1)} %reshape.130) | data formatting | bytes 1044480 | tf_op jit(solution)/shard_map/conv_general_dilated | solution.py:59
  362.5 4.4 fusion.64
  371.8 3.0 collective-permute-start.91
  393.0 5.9 %stack.578 = f32[10]{0:T(128)S(1)} concatenate(f32[1]{0:T(128)} %bitcast.288, f32[1]{0:T(128)} %bitcast.292, f32[1]{0:T(128)} %bitcast.293, f32[1]{0:T(128)} %bitcast.295, f32[1]{0:T(128)} %bitcast.296, f32[1]{0:T(128)} %bitcast.297, f32[1]{0:T(128)} %bitcast.298, f32[1]{0:T(128)} %bitcast.299, f32[1]{0:T(128)} %bitcast.300, f32[1]{0:T(128)} %bitcast.301), dimensions={0} | concatenate | bytes 80 | tf_op jit(solution)/shard_map/stack | solution.py:154
  398.9 33.9 %all-reduce = (f32[2]{0:T(128)S(1)}, f32[1,10]{1,0:T(1,128)S(1)}, f32[1,10]{1,0:T(1,128)S(1)}) all-reduce(f32[2]{0:T(128)S(1)} %pad_maximum_fusion.82, f32[1,10]{1,0:T(1,128)S(1)} %bitcast.1700, f32[1,10]{1,0:T(1,128)S(1)} %bitcast.1699), channel_id=1, replica_groups=mesh['boxes'=2,'gx'=4,'gy'=2,'gz'=2] {'gx','gy','gz'}, use_global_device_ids=true, to_apply=%region_4.5 | all-reduce | flops 22 | bytes 176 | tf_op jit(solution)/shard_map/psum | solution.py:179
  (493 shorter events, 179.1 us)
Async XLA Ops:
  1.5 9.0 %collective-permute-start = (f32[1,4,128]{2,1,0:T(4,128)S(1)}, f32[1,4,128]{2,1,0:T(4,128)S(1)}, u32[]{:S(2)}, u32[]{:S(2)}) collective-permute-start(f32[1,4,128]{2,1,0:T(4,128)S(1)} %get-tuple-element.200), channel_id=1, source_target_pairs={{0,4},{4,8},{8,12},{12,0},{1,5},{5,9},{9,13},{13,1},{2,6},{6,10},{... | collective-permute-start | bytes 6152 | tf_op jit(solution)/shard_map/ppermute | solution.py:27
  4.5 5.9 %collective-permute-start.1 = (f32[1,4,128]{2,1,0:T(4,128)S(1)}, f32[1,4,128]{2,1,0:T(4,128)S(1)}, u32[]{:S(2)}, u32[]{:S(2)}) collective-permute-start(f32[1,4,128]{2,1,0:T(4,128)S(1)} %get-tuple-element.201), channel_id=1, source_target_pairs={{4,0},{8,4},{12,8},{0,12},{5,1},{9,5},{13,9},{1,13},{6,2},{10,6},{... | collective-permute-start | bytes 6152 | tf_op jit(solution)/shard_map/ppermute | solution.py:29
  6.6 5.9 %collective-permute-start.24 = (f32[1,4,128]{2,1,0:T(4,128)S(1)}, f32[1,4,128]{2,1,0:T(4,128)S(1)}, u32[]{:S(2)}, u32[]{:S(2)}) collective-permute-start(f32[1,4,128]{2,1,0:T(4,128)S(1)} %get-tuple-element.194), channel_id=1, source_target_pairs={{0,4},{4,8},{8,12},{12,0},{1,5},{5,9},{9,13},{13,1},{2,6},{6,10},{... | collective-permute-start | bytes 6152 | tf_op jit(solution)/shard_map/ppermute | solution.py:27
  6.6 5.9 %collective-permute-start.25 = (f32[1,4,128]{2,1,0:T(4,128)S(1)}, f32[1,4,128]{2,1,0:T(4,128)S(1)}, u32[]{:S(2)}, u32[]{:S(2)}) collective-permute-start(f32[1,4,128]{2,1,0:T(4,128)S(1)} %get-tuple-element.195), channel_id=1, source_target_pairs={{4,0},{8,4},{12,8},{0,12},{5,1},{9,5},{13,9},{1,13},{6,2},{10,6},{... | collective-permute-start | bytes 6152 | tf_op jit(solution)/shard_map/ppermute | solution.py:29
  18.0 8.1 %collective-permute-start.28 = (f32[10,6,1]{2,1,0:T(8,128)S(1)}, f32[10,6,1]{2,1,0:T(8,128)S(1)}, u32[]{:S(2)}, u32[]{:S(2)}) collective-permute-start(f32[10,6,1]{2,1,0:T(8,128)S(1)} %get-tuple-element.153), channel_id=1, source_target_pairs={{1,0},{0,1},{3,2},{2,3},{5,4},{4,5},{7,6},{6,7},{9,8},{8,9},{11,10... | collective-permute-start | bytes 728 | tf_op jit(solution)/shard_map/ppermute | solution.py:29
  18.1 8.1 %collective-permute-start.29 = (f32[10,6,1]{2,1,0:T(8,128)S(1)}, f32[10,6,1]{2,1,0:T(8,128)S(1)}, u32[]{:S(2)}, u32[]{:S(2)}) collective-permute-start(f32[10,6,1]{2,1,0:T(8,128)S(1)} %get-tuple-element.152), channel_id=1, source_target_pairs={{0,1},{1,0},{2,3},{3,2},{4,5},{5,4},{6,7},{7,6},{8,9},{9,8},{10,11... | collective-permute-start | bytes 728 | tf_op jit(solution)/shard_map/ppermute | solution.py:27
  22.1 5.8 %collective-permute-start.6 = (bf16[32,1,4,128]{3,0,2,1:T(8,128)(2,1)S(1)}, bf16[32,1,4,128]{3,0,2,1:T(8,128)(2,1)S(1)}, u32[]{:S(2)}, u32[]{:S(2)}) collective-permute-start(bf16[32,1,4,128]{3,0,2,1:T(8,128)(2,1)S(1)} %get-tuple-element.128), channel_id=1, source_target_pairs={{0,4},{4,8},{8,12},{12,0},{1,5},{5,9},{9,13},{13,1},{2,6},{6,10},{... | collective-permute-start | bytes 98312 | tf_op jit(solution)/shard_map/ppermute | solution.py:27
  22.2 5.7 %collective-permute-start.7 = (bf16[32,1,4,128]{3,0,2,1:T(8,128)(2,1)S(1)}, bf16[32,1,4,128]{3,0,2,1:T(8,128)(2,1)S(1)}, u32[]{:S(2)}, u32[]{:S(2)}) collective-permute-start(bf16[32,1,4,128]{3,0,2,1:T(8,128)(2,1)S(1)} %get-tuple-element.129), channel_id=1, source_target_pairs={{4,0},{8,4},{12,8},{0,12},{5,1},{9,5},{13,9},{1,13},{6,2},{10,6},{... | collective-permute-start | bytes 98312 | tf_op jit(solution)/shard_map/ppermute | solution.py:29
  28.3 5.0 %collective-permute-start.9 = (bf16[32,10,1,128]{3,0,2,1:T(8,128)(2,1)S(1)}, bf16[32,10,1,128]{3,0,2,1:T(8,128)(2,1)S(1)}, u32[]{:S(2)}, u32[]{:S(2)}) collective-permute-start(bf16[32,10,1,128]{3,0,2,1:T(8,128)(2,1)S(1)} %get-tuple-element.105), channel_id=1, source_target_pairs={{2,0},{0,2},{3,1},{1,3},{6,4},{4,6},{7,5},{5,7},{10,8},{8,10},{11,... | collective-permute-start | bytes 245768 | tf_op jit(solution)/shard_map/ppermute | solution.py:29
  52.8 6.1 %collective-permute-start.12 = (bf16[32,1,4,128]{3,0,2,1:T(8,128)(2,1)S(1)}, bf16[32,1,4,128]{3,0,2,1:T(8,128)(2,1)S(1)}, u32[]{:S(2)}, u32[]{:S(2)}) collective-permute-start(bf16[32,1,4,128]{3,0,2,1:T(8,128)(2,1)S(1)} %get-tuple-element.126), channel_id=1, source_target_pairs={{0,4},{4,8},{8,12},{12,0},{1,5},{5,9},{9,13},{13,1},{2,6},{6,10},{... | collective-permute-start | bytes 98312 | tf_op jit(solution)/shard_map/ppermute | solution.py:27
  53.7 5.1 %collective-permute-start.13 = (bf16[32,1,4,128]{3,0,2,1:T(8,128)(2,1)S(1)}, bf16[32,1,4,128]{3,0,2,1:T(8,128)(2,1)S(1)}, u32[]{:S(2)}, u32[]{:S(2)}) collective-permute-start(bf16[32,1,4,128]{3,0,2,1:T(8,128)(2,1)S(1)} %get-tuple-element.127), channel_id=1, source_target_pairs={{4,0},{8,4},{12,8},{0,12},{5,1},{9,5},{13,9},{1,13},{6,2},{10,6},{... | collective-permute-start | bytes 98312 | tf_op jit(solution)/shard_map/ppermute | solution.py:29
  85.7 6.0 %collective-permute-start.30 = (bf16[32,1,4,128]{3,0,2,1:T(8,128)(2,1)S(1)}, bf16[32,1,4,128]{3,0,2,1:T(8,128)(2,1)S(1)}, u32[]{:S(2)}, u32[]{:S(2)}) collective-permute-start(bf16[32,1,4,128]{3,0,2,1:T(8,128)(2,1)S(1)} %get-tuple-element.122), channel_id=1, source_target_pairs={{0,4},{4,8},{8,12},{12,0},{1,5},{5,9},{9,13},{13,1},{2,6},{6,10},{... | collective-permute-start | bytes 98312 | tf_op jit(solution)/shard_map/ppermute | solution.py:27
  87.0 4.9 %collective-permute-start.31 = (bf16[32,1,4,128]{3,0,2,1:T(8,128)(2,1)S(1)}, bf16[32,1,4,128]{3,0,2,1:T(8,128)(2,1)S(1)}, u32[]{:S(2)}, u32[]{:S(2)}) collective-permute-start(bf16[32,1,4,128]{3,0,2,1:T(8,128)(2,1)S(1)} %get-tuple-element.123), channel_id=1, source_target_pairs={{4,0},{8,4},{12,8},{0,12},{5,1},{9,5},{13,9},{1,13},{6,2},{10,6},{... | collective-permute-start | bytes 98312 | tf_op jit(solution)/shard_map/ppermute | solution.py:29
  91.9 4.6 %collective-permute-start.32 = (bf16[32,10,1,128]{3,0,2,1:T(8,128)(2,1)S(1)}, bf16[32,10,1,128]{3,0,2,1:T(8,128)(2,1)S(1)}, u32[]{:S(2)}, u32[]{:S(2)}) collective-permute-start(bf16[32,10,1,128]{3,0,2,1:T(8,128)(2,1)S(1)} %get-tuple-element.98), channel_id=1, source_target_pairs={{0,2},{2,0},{1,3},{3,1},{4,6},{6,4},{5,7},{7,5},{8,10},{10,8},{9,1... | collective-permute-start | bytes 245768 | tf_op jit(solution)/shard_map/ppermute | solution.py:27
  119.0 6.0 %collective-permute-start.36 = (bf16[32,1,4,128]{3,0,2,1:T(8,128)(2,1)S(1)}, bf16[32,1,4,128]{3,0,2,1:T(8,128)(2,1)S(1)}, u32[]{:S(2)}, u32[]{:S(2)}) collective-permute-start(bf16[32,1,4,128]{3,0,2,1:T(8,128)(2,1)S(1)} %get-tuple-element.120), channel_id=1, source_target_pairs={{0,4},{4,8},{8,12},{12,0},{1,5},{5,9},{9,13},{13,1},{2,6},{6,10},{... | collective-permute-start | bytes 98312 | tf_op jit(solution)/shard_map/ppermute | solution.py:27
  120.4 4.6 %collective-permute-start.37 = (bf16[32,1,4,128]{3,0,2,1:T(8,128)(2,1)S(1)}, bf16[32,1,4,128]{3,0,2,1:T(8,128)(2,1)S(1)}, u32[]{:S(2)}, u32[]{:S(2)}) collective-permute-start(bf16[32,1,4,128]{3,0,2,1:T(8,128)(2,1)S(1)} %get-tuple-element.121), channel_id=1, source_target_pairs={{4,0},{8,4},{12,8},{0,12},{5,1},{9,5},{13,9},{1,13},{6,2},{10,6},{... | collective-permute-start | bytes 98312 | tf_op jit(solution)/shard_map/ppermute | solution.py:29
  125.1 6.1 %collective-permute-start.38 = (bf16[32,10,1,128]{3,0,2,1:T(8,128)(2,1)S(1)}, bf16[32,10,1,128]{3,0,2,1:T(8,128)(2,1)S(1)}, u32[]{:S(2)}, u32[]{:S(2)}) collective-permute-start(bf16[32,10,1,128]{3,0,2,1:T(8,128)(2,1)S(1)} %get-tuple-element.96), channel_id=1, source_target_pairs={{0,2},{2,0},{1,3},{3,1},{4,6},{6,4},{5,7},{7,5},{8,10},{10,8},{9,1... | collective-permute-start | bytes 245768 | tf_op jit(solution)/shard_map/ppermute | solution.py:27
  126.3 4.9 %collective-permute-start.39 = (bf16[32,10,1,128]{3,0,2,1:T(8,128)(2,1)S(1)}, bf16[32,10,1,128]{3,0,2,1:T(8,128)(2,1)S(1)}, u32[]{:S(2)}, u32[]{:S(2)}) collective-permute-start(bf16[32,10,1,128]{3,0,2,1:T(8,128)(2,1)S(1)} %get-tuple-element.97), channel_id=1, source_target_pairs={{2,0},{0,2},{3,1},{1,3},{6,4},{4,6},{7,5},{5,7},{10,8},{8,10},{11,... | collective-permute-start | bytes 245768 | tf_op jit(solution)/shard_map/ppermute | solution.py:29
  127.2 5.7 %collective-permute-start.18 = (bf16[32,1,4,128]{3,0,2,1:T(8,128)(2,1)S(1)}, bf16[32,1,4,128]{3,0,2,1:T(8,128)(2,1)S(1)}, u32[]{:S(2)}, u32[]{:S(2)}) collective-permute-start(bf16[32,1,4,128]{3,0,2,1:T(8,128)(2,1)S(1)} %get-tuple-element.124), channel_id=1, source_target_pairs={{0,4},{4,8},{8,12},{12,0},{1,5},{5,9},{9,13},{13,1},{2,6},{6,10},{... | collective-permute-start | bytes 98312 | tf_op jit(solution)/shard_map/ppermute | solution.py:27
  128.4 4.5 %collective-permute-start.19 = (bf16[32,1,4,128]{3,0,2,1:T(8,128)(2,1)S(1)}, bf16[32,1,4,128]{3,0,2,1:T(8,128)(2,1)S(1)}, u32[]{:S(2)}, u32[]{:S(2)}) collective-permute-start(bf16[32,1,4,128]{3,0,2,1:T(8,128)(2,1)S(1)} %get-tuple-element.125), channel_id=1, source_target_pairs={{4,0},{8,4},{12,8},{0,12},{5,1},{9,5},{13,9},{1,13},{6,2},{10,6},{... | collective-permute-start | bytes 98312 | tf_op jit(solution)/shard_map/ppermute | solution.py:29
  133.6 24.4 %collective-permute-start.20 = (bf16[32,10,1,128]{3,0,2,1:T(8,128)(2,1)}, bf16[32,10,1,128]{3,0,2,1:T(8,128)(2,1)S(1)}, u32[]{:S(2)}, u32[]{:S(2)}) collective-permute-start(bf16[32,10,1,128]{3,0,2,1:T(8,128)(2,1)} %get-tuple-element.100), channel_id=1, source_target_pairs={{0,2},{2,0},{1,3},{3,1},{4,6},{6,4},{5,7},{7,5},{8,10},{10,8},{9,1... | collective-permute-start | bytes 245768 | tf_op jit(solution)/shard_map/ppermute | solution.py:27
  134.7 23.2 %collective-permute-start.21 = (bf16[32,10,1,128]{3,0,2,1:T(8,128)(2,1)S(1)}, bf16[32,10,1,128]{3,0,2,1:T(8,128)(2,1)S(1)}, u32[]{:S(2)}, u32[]{:S(2)}) collective-permute-start(bf16[32,10,1,128]{3,0,2,1:T(8,128)(2,1)S(1)} %get-tuple-element.101), channel_id=1, source_target_pairs={{2,0},{0,2},{3,1},{1,3},{6,4},{4,6},{7,5},{5,7},{10,8},{8,10},{11,... | collective-permute-start | bytes 245768 | tf_op jit(solution)/shard_map/ppermute | solution.py:29
  153.6 6.0 %collective-permute-start.42 = (bf16[32,1,4,128]{3,0,2,1:T(8,128)(2,1)S(1)}, bf16[32,1,4,128]{3,0,2,1:T(8,128)(2,1)S(1)}, u32[]{:S(2)}, u32[]{:S(2)}) collective-permute-start(bf16[32,1,4,128]{3,0,2,1:T(8,128)(2,1)S(1)} %get-tuple-element.118), channel_id=1, source_target_pairs={{0,4},{4,8},{8,12},{12,0},{1,5},{5,9},{9,13},{13,1},{2,6},{6,10},{... | collective-permute-start | bytes 98312 | tf_op jit(solution)/shard_map/ppermute | solution.py:27
  155.0 4.5 %collective-permute-start.43 = (bf16[32,1,4,128]{3,0,2,1:T(8,128)(2,1)S(1)}, bf16[32,1,4,128]{3,0,2,1:T(8,128)(2,1)S(1)}, u32[]{:S(2)}, u32[]{:S(2)}) collective-permute-start(bf16[32,1,4,128]{3,0,2,1:T(8,128)(2,1)S(1)} %get-tuple-element.119), channel_id=1, source_target_pairs={{4,0},{8,4},{12,8},{0,12},{5,1},{9,5},{13,9},{1,13},{6,2},{10,6},{... | collective-permute-start | bytes 98312 | tf_op jit(solution)/shard_map/ppermute | solution.py:29
  209.9 7.7 %collective-permute-start.48 = (f32[1,4,128]{2,1,0:T(4,128)S(1)}, f32[1,4,128]{2,1,0:T(4,128)S(1)}, u32[]{:S(2)}, u32[]{:S(2)}) collective-permute-start(f32[1,4,128]{2,1,0:T(4,128)S(1)} %get-tuple-element.192), channel_id=1, source_target_pairs={{0,4},{4,8},{8,12},{12,0},{1,5},{5,9},{9,13},{13,1},{2,6},{6,10},{... | collective-permute-start | bytes 6152 | tf_op jit(solution)/shard_map/ppermute | solution.py:27
  209.9 7.6 %collective-permute-start.49 = (f32[1,4,128]{2,1,0:T(4,128)S(1)}, f32[1,4,128]{2,1,0:T(4,128)S(1)}, u32[]{:S(2)}, u32[]{:S(2)}) collective-permute-start(f32[1,4,128]{2,1,0:T(4,128)S(1)} %get-tuple-element.193), channel_id=1, source_target_pairs={{4,0},{8,4},{12,8},{0,12},{5,1},{9,5},{13,9},{1,13},{6,2},{10,6},{... | collective-permute-start | bytes 6152 | tf_op jit(solution)/shard_map/ppermute | solution.py:29
  213.8 5.9 %collective-permute-start.72 = (f32[1,4,128]{2,1,0:T(4,128)S(1)}, f32[1,4,128]{2,1,0:T(4,128)S(1)}, u32[]{:S(2)}, u32[]{:S(2)}) collective-permute-start(f32[1,4,128]{2,1,0:T(4,128)S(1)} %get-tuple-element.188), channel_id=1, source_target_pairs={{0,4},{4,8},{8,12},{12,0},{1,5},{5,9},{9,13},{13,1},{2,6},{6,10},{... | collective-permute-start | bytes 6152 | tf_op jit(solution)/shard_map/ppermute | solution.py:27
  213.8 5.9 %collective-permute-start.73 = (f32[1,4,128]{2,1,0:T(4,128)S(1)}, f32[1,4,128]{2,1,0:T(4,128)S(1)}, u32[]{:S(2)}, u32[]{:S(2)}) collective-permute-start(f32[1,4,128]{2,1,0:T(4,128)S(1)} %get-tuple-element.189), channel_id=1, source_target_pairs={{4,0},{8,4},{12,8},{0,12},{5,1},{9,5},{13,9},{1,13},{6,2},{10,6},{... | collective-permute-start | bytes 6152 | tf_op jit(solution)/shard_map/ppermute | solution.py:29
  228.1 5.9 %collective-permute-start.54 = (bf16[32,1,4,128]{3,0,2,1:T(8,128)(2,1)S(1)}, bf16[32,1,4,128]{3,0,2,1:T(8,128)(2,1)S(1)}, u32[]{:S(2)}, u32[]{:S(2)}) collective-permute-start(bf16[32,1,4,128]{3,0,2,1:T(8,128)(2,1)S(1)} %get-tuple-element.116), channel_id=1, source_target_pairs={{0,4},{4,8},{8,12},{12,0},{1,5},{5,9},{9,13},{13,1},{2,6},{6,10},{... | collective-permute-start | bytes 98312 | tf_op jit(solution)/shard_map/ppermute | solution.py:27
  228.2 5.8 %collective-permute-start.55 = (bf16[32,1,4,128]{3,0,2,1:T(8,128)(2,1)S(1)}, bf16[32,1,4,128]{3,0,2,1:T(8,128)(2,1)S(1)}, u32[]{:S(2)}, u32[]{:S(2)}) collective-permute-start(bf16[32,1,4,128]{3,0,2,1:T(8,128)(2,1)S(1)} %get-tuple-element.117), channel_id=1, source_target_pairs={{4,0},{8,4},{12,8},{0,12},{5,1},{9,5},{13,9},{1,13},{6,2},{10,6},{... | collective-permute-start | bytes 98312 | tf_op jit(solution)/shard_map/ppermute | solution.py:29
  234.0 5.3 %collective-permute-start.56 = (bf16[32,10,1,128]{3,0,2,1:T(8,128)(2,1)S(1)}, bf16[32,10,1,128]{3,0,2,1:T(8,128)(2,1)S(1)}, u32[]{:S(2)}, u32[]{:S(2)}) collective-permute-start(bf16[32,10,1,128]{3,0,2,1:T(8,128)(2,1)S(1)} %get-tuple-element.92), channel_id=1, source_target_pairs={{0,2},{2,0},{1,3},{3,1},{4,6},{6,4},{5,7},{7,5},{8,10},{10,8},{9,1... | collective-permute-start | bytes 245768 | tf_op jit(solution)/shard_map/ppermute | solution.py:27
  260.0 6.1 %collective-permute-start.60 = (bf16[32,1,4,128]{3,0,2,1:T(8,128)(2,1)S(1)}, bf16[32,1,4,128]{3,0,2,1:T(8,128)(2,1)S(1)}, u32[]{:S(2)}, u32[]{:S(2)}) collective-permute-start(bf16[32,1,4,128]{3,0,2,1:T(8,128)(2,1)S(1)} %get-tuple-element.114), channel_id=1, source_target_pairs={{0,4},{4,8},{8,12},{12,0},{1,5},{5,9},{9,13},{13,1},{2,6},{6,10},{... | collective-permute-start | bytes 98312 | tf_op jit(solution)/shard_map/ppermute | solution.py:27
  260.9 5.2 %collective-permute-start.61 = (bf16[32,1,4,128]{3,0,2,1:T(8,128)(2,1)S(1)}, bf16[32,1,4,128]{3,0,2,1:T(8,128)(2,1)S(1)}, u32[]{:S(2)}, u32[]{:S(2)}) collective-permute-start(bf16[32,1,4,128]{3,0,2,1:T(8,128)(2,1)S(1)} %get-tuple-element.115), channel_id=1, source_target_pairs={{4,0},{8,4},{12,8},{0,12},{5,1},{9,5},{13,9},{1,13},{6,2},{10,6},{... | collective-permute-start | bytes 98312 | tf_op jit(solution)/shard_map/ppermute | solution.py:29
  292.7 6.0 %collective-permute-start.78 = (bf16[32,1,4,128]{3,0,2,1:T(8,128)(2,1)S(1)}, bf16[32,1,4,128]{3,0,2,1:T(8,128)(2,1)S(1)}, u32[]{:S(2)}, u32[]{:S(2)}) collective-permute-start(bf16[32,1,4,128]{3,0,2,1:T(8,128)(2,1)S(1)} %get-tuple-element.110), channel_id=1, source_target_pairs={{0,4},{4,8},{8,12},{12,0},{1,5},{5,9},{9,13},{13,1},{2,6},{6,10},{... | collective-permute-start | bytes 98312 | tf_op jit(solution)/shard_map/ppermute | solution.py:27
  294.0 4.7 %collective-permute-start.79 = (bf16[32,1,4,128]{3,0,2,1:T(8,128)(2,1)S(1)}, bf16[32,1,4,128]{3,0,2,1:T(8,128)(2,1)S(1)}, u32[]{:S(2)}, u32[]{:S(2)}) collective-permute-start(bf16[32,1,4,128]{3,0,2,1:T(8,128)(2,1)S(1)} %get-tuple-element.111), channel_id=1, source_target_pairs={{4,0},{8,4},{12,8},{0,12},{5,1},{9,5},{13,9},{1,13},{6,2},{10,6},{... | collective-permute-start | bytes 98312 | tf_op jit(solution)/shard_map/ppermute | solution.py:29
  298.7 4.5 %collective-permute-start.80 = (bf16[32,10,1,128]{3,0,2,1:T(8,128)(2,1)S(1)}, bf16[32,10,1,128]{3,0,2,1:T(8,128)(2,1)S(1)}, u32[]{:S(2)}, u32[]{:S(2)}) collective-permute-start(bf16[32,10,1,128]{3,0,2,1:T(8,128)(2,1)S(1)} %get-tuple-element.86), channel_id=1, source_target_pairs={{0,2},{2,0},{1,3},{3,1},{4,6},{6,4},{5,7},{7,5},{8,10},{10,8},{9,1... | collective-permute-start | bytes 245768 | tf_op jit(solution)/shard_map/ppermute | solution.py:27
  305.3 10.7 %collective-permute-start.82 = (bf16[32,10,6,1]{3,0,2,1:T(8,128)(2,1)S(1)}, bf16[32,10,6,1]{3,0,2,1:T(8,128)(2,1)S(1)}, u32[]{:S(2)}, u32[]{:S(2)}) collective-permute-start(bf16[32,10,6,1]{3,0,2,1:T(8,128)(2,1)S(1)} %get-tuple-element.62), channel_id=1, source_target_pairs={{0,1},{1,0},{2,3},{3,2},{4,5},{5,4},{6,7},{7,6},{8,9},{9,8},{10,11... | collective-permute-start | bytes 11528 | tf_op jit(solution)/shard_map/ppermute | solution.py:27
  305.4 10.6 %collective-permute-start.83 = (bf16[32,10,6,1]{3,0,2,1:T(8,128)(2,1)S(1)}, bf16[32,10,6,1]{3,0,2,1:T(8,128)(2,1)}, u32[]{:S(2)}, u32[]{:S(2)}) collective-permute-start(bf16[32,10,6,1]{3,0,2,1:T(8,128)(2,1)S(1)} %get-tuple-element.63), channel_id=1, source_target_pairs={{1,0},{0,1},{3,2},{2,3},{5,4},{4,5},{7,6},{6,7},{9,8},{8,9},{11,10... | collective-permute-start | bytes 11528 | tf_op jit(solution)/shard_map/ppermute | solution.py:29
  335.7 6.0 %collective-permute-start.84 = (bf16[32,1,4,128]{3,0,2,1:T(8,128)(2,1)S(1)}, bf16[32,1,4,128]{3,0,2,1:T(8,128)(2,1)S(1)}, u32[]{:S(2)}, u32[]{:S(2)}) collective-permute-start(bf16[32,1,4,128]{3,0,2,1:T(8,128)(2,1)S(1)} %get-tuple-element.108), channel_id=1, source_target_pairs={{0,4},{4,8},{8,12},{12,0},{1,5},{5,9},{9,13},{13,1},{2,6},{6,10},{... | collective-permute-start | bytes 98312 | tf_op jit(solution)/shard_map/ppermute | solution.py:27
  337.1 4.6 %collective-permute-start.85 = (bf16[32,1,4,128]{3,0,2,1:T(8,128)(2,1)S(1)}, bf16[32,1,4,128]{3,0,2,1:T(8,128)(2,1)S(1)}, u32[]{:S(2)}, u32[]{:S(2)}) collective-permute-start(bf16[32,1,4,128]{3,0,2,1:T(8,128)(2,1)S(1)} %get-tuple-element.109), channel_id=1, source_target_pairs={{4,0},{8,4},{12,8},{0,12},{5,1},{9,5},{13,9},{1,13},{6,2},{10,6},{... | collective-permute-start | bytes 98312 | tf_op jit(solution)/shard_map/ppermute | solution.py:29
  341.8 6.2 %collective-permute-start.86 = (bf16[32,10,1,128]{3,0,2,1:T(8,128)(2,1)S(1)}, bf16[32,10,1,128]{3,0,2,1:T(8,128)(2,1)S(1)}, u32[]{:S(2)}, u32[]{:S(2)}) collective-permute-start(bf16[32,10,1,128]{3,0,2,1:T(8,128)(2,1)S(1)} %get-tuple-element.84), channel_id=1, source_target_pairs={{0,2},{2,0},{1,3},{3,1},{4,6},{6,4},{5,7},{7,5},{8,10},{10,8},{9,1... | collective-permute-start | bytes 245768 | tf_op jit(solution)/shard_map/ppermute | solution.py:27
  342.7 5.3 %collective-permute-start.87 = (bf16[32,10,1,128]{3,0,2,1:T(8,128)(2,1)S(1)}, bf16[32,10,1,128]{3,0,2,1:T(8,128)(2,1)S(1)}, u32[]{:S(2)}, u32[]{:S(2)}) collective-permute-start(bf16[32,10,1,128]{3,0,2,1:T(8,128)(2,1)S(1)} %get-tuple-element.85), channel_id=1, source_target_pairs={{2,0},{0,2},{3,1},{1,3},{6,4},{4,6},{7,5},{5,7},{10,8},{8,10},{11,... | collective-permute-start | bytes 245768 | tf_op jit(solution)/shard_map/ppermute | solution.py:29
  343.9 5.7 %collective-permute-start.66 = (bf16[32,1,4,128]{3,0,2,1:T(8,128)(2,1)S(1)}, bf16[32,1,4,128]{3,0,2,1:T(8,128)(2,1)S(1)}, u32[]{:S(2)}, u32[]{:S(2)}) collective-permute-start(bf16[32,1,4,128]{3,0,2,1:T(8,128)(2,1)S(1)} %get-tuple-element.112), channel_id=1, source_target_pairs={{0,4},{4,8},{8,12},{12,0},{1,5},{5,9},{9,13},{13,1},{2,6},{6,10},{... | collective-permute-start | bytes 98312 | tf_op jit(solution)/shard_map/ppermute | solution.py:27
  345.0 4.5 %collective-permute-start.67 = (bf16[32,1,4,128]{3,0,2,1:T(8,128)(2,1)S(1)}, bf16[32,1,4,128]{3,0,2,1:T(8,128)(2,1)S(1)}, u32[]{:S(2)}, u32[]{:S(2)}) collective-permute-start(bf16[32,1,4,128]{3,0,2,1:T(8,128)(2,1)S(1)} %get-tuple-element.113), channel_id=1, source_target_pairs={{4,0},{8,4},{12,8},{0,12},{5,1},{9,5},{13,9},{1,13},{6,2},{10,6},{... | collective-permute-start | bytes 98312 | tf_op jit(solution)/shard_map/ppermute | solution.py:29
  350.2 24.5 %collective-permute-start.68 = (bf16[32,10,1,128]{3,0,2,1:T(8,128)(2,1)}, bf16[32,10,1,128]{3,0,2,1:T(8,128)(2,1)}, u32[]{:S(2)}, u32[]{:S(2)}) collective-permute-start(bf16[32,10,1,128]{3,0,2,1:T(8,128)(2,1)} %get-tuple-element.88), channel_id=1, source_target_pairs={{0,2},{2,0},{1,3},{3,1},{4,6},{6,4},{5,7},{7,5},{8,10},{10,8},{9,1... | collective-permute-start | bytes 245768 | tf_op jit(solution)/shard_map/ppermute | solution.py:27
  351.1 23.6 %collective-permute-start.69 = (bf16[32,10,1,128]{3,0,2,1:T(8,128)(2,1)}, bf16[32,10,1,128]{3,0,2,1:T(8,128)(2,1)}, u32[]{:S(2)}, u32[]{:S(2)}) collective-permute-start(bf16[32,10,1,128]{3,0,2,1:T(8,128)(2,1)} %get-tuple-element.89), channel_id=1, source_target_pairs={{2,0},{0,2},{3,1},{1,3},{6,4},{4,6},{7,5},{5,7},{10,8},{8,10},{11,... | collective-permute-start | bytes 245768 | tf_op jit(solution)/shard_map/ppermute | solution.py:29
  370.2 6.1 %collective-permute-start.90 = (bf16[32,1,4,128]{3,0,2,1:T(8,128)(2,1)S(1)}, bf16[32,1,4,128]{3,0,2,1:T(8,128)(2,1)S(1)}, u32[]{:S(2)}, u32[]{:S(2)}) collective-permute-start(bf16[32,1,4,128]{3,0,2,1:T(8,128)(2,1)S(1)} %get-tuple-element.106), channel_id=1, source_target_pairs={{0,4},{4,8},{8,12},{12,0},{1,5},{5,9},{9,13},{13,1},{2,6},{6,10},{... | collective-permute-start | bytes 98312 | tf_op jit(solution)/shard_map/ppermute | solution.py:27
  371.8 4.6 %collective-permute-start.91 = (bf16[32,1,4,128]{3,0,2,1:T(8,128)(2,1)S(1)}, bf16[32,1,4,128]{3,0,2,1:T(8,128)(2,1)S(1)}, u32[]{:S(2)}, u32[]{:S(2)}) collective-permute-start(bf16[32,1,4,128]{3,0,2,1:T(8,128)(2,1)S(1)} %get-tuple-element.107), channel_id=1, source_target_pairs={{4,0},{8,4},{12,8},{0,12},{5,1},{9,5},{13,9},{1,13},{6,2},{10,6},{... | collective-permute-start | bytes 98312 | tf_op jit(solution)/shard_map/ppermute | solution.py:29
  (86 other events, 554.6 us)
where the time goes:
time: 442 us; the launch traced here: 437 us
  local copies, waits for them, and re-layouts  126 us (29%)
  starting transfers between devices  110 us (25%)
  blocking collectives  67.5 us (15%)
  waiting for transfers between devices  52.9 us (12%)
  matrix products  44 us (10%)
  other arithmetic  28.5 us (6%)
  between operations  8.16 us (2%)
    conv_general_dilated x40, local copies, waits for them, and re-layouts, dense_apply(): lax.conv_general_dilated(padded[None], kernel_block, (1, 1, 1), 'VALID',...  85.4 us
    ppermute x48, starting transfers between devices, padded_2(): lax.ppermute(head, axis, [((i + 1) % count, i) for i in range(count)])  75.4 us
    psum x2, blocking collectives, on_device(): lax.psum((jnp.stack([norm_part, mass_part]), stress_part), ('gx', 'gy', '...  67.5 us
    ppermute x48, waiting for transfers between devices, padded_2(): lax.ppermute(tail, axis, [(i, (i + 1) % count) for i in range(count)])  37.8 us
    ppermute x48, starting transfers between devices, padded_2(): lax.ppermute(tail, axis, [(i, (i + 1) % count) for i in range(count)])  34.6 us
    conv_general_dilated x8, matrix products, dense_apply(): lax.conv_general_dilated(padded[None], kernel_block, (1, 1, 1), 'VALID',...  33.8 us
    unnamed x154, local copies, waits for them, and re-layouts  16 us
    ppermute x48, waiting for transfers between devices, padded_2(): lax.ppermute(head, axis, [((i + 1) % count, i) for i in range(count)])  15 us
  transfers between devices with their start and end apart: 96, of which 46 were waited for; matrix products, arithmetic and copies ran while one was open for 14% of the time, Pallas kernels for 0%

commit v1 on v0

v1 whole, which is shorter than its diff:
```python
import functools

import jax
import jax.numpy as jnp
from jax import lax
from jax.experimental import pallas as pl
from jax.experimental.pallas import tpu as pltpu
from jax.sharding import PartitionSpec as P

STEPS = 2
C_TF = 2.871234
C_X = 0.7385588
TAU = 0.1
REACH = 6
STRIPS = 16
GROUP = 4
SUMS = 16
LIMIT = 60 << 20
BF = jnp.bfloat16
F32 = jnp.float32
VM = pl.BlockSpec(memory_space=pltpu.VMEM)
SM = pl.BlockSpec(memory_space=pltpu.SMEM)


def up(number, unit):
    return -(-number // unit) * unit


def iota(shape, dim):
    return lax.broadcasted_iota(jnp.int32, shape, dim)


def dot(a, b):
    return jnp.dot(a, b, preferred_element_type=F32)


def dot_tn(a, b):
    return lax.dot_general(a, b, (((0,), (0,)), ((), ())), preferred_element_type=F32)


def dot_nt(a, b):
    return lax.dot_general(a, b, (((1,), (1,)), ((), ())), preferred_element_type=F32)


class Plan:
    def __init__(self, xo, yw, own_y, ny, zo, ch):
        self.xo, self.yw, self.own_y, self.ny, self.zo, self.ch = xo, yw, own_y, ny, zo, ch
        self.xe = xo + 2 * REACH
        self.ze = up(zo + 2 * REACH, STRIPS)
        self.zh = (self.ze - zo) // 2
        self.lo = self.ze // STRIPS
        self.zp = up(self.ze, 128)
        self.zq = up(zo, 128)
        self.lanes = yw * ch
        self.fields = 4 * yw
        self.narrow = up(GROUP * self.fields, 128)


def tap_no(tx, ty, tz, direction):
    number = 9 * tx + 3 * ty + tz
    return number if direction > 0 else 26 - number


def weights_kernel(p, dense_in, single_in, dense_out, first_out, last_out):
    ch, yw, lanes = p.ch, p.yw, p.lanes

    for ref_in, ref_out, direction in zip(dense_in, dense_out, (1, 1, -1, -1)):
        taps = []
        for ty in range(3):
            taps.append(
                jnp.concatenate(
                    [ref_in[tap_no(t // 3, ty, t % 3, direction)] for t in range(9)], axis=0
                )
            )
        for yi in range(yw):
            spread = None
            for ty in range(3):
                yo = (yi - ty + 1) % yw
                place = (iota((ch, lanes), 1) == iota((ch, lanes), 0) + yo * ch).astype(F32)
                part = dot(taps[ty], place.astype(BF))
                spread = part if spread is None else spread + part
            ref_out[:, yi * ch : (yi + 1) * ch, :] = spread.astype(BF).reshape(9, ch, lanes)

    tile = (
        jnp.bitwise_and(iota((ch, lanes), 1), ch - 1) == iota((ch, lanes), 0)
    ).astype(F32).astype(BF)
    tiled = [dot(ref[...], tile).astype(BF) for ref in single_in]

    rows = 18 * yw
    row = iota((rows, 1), 0)
    yi = lax.rem(row, yw)
    tx = lax.rem(lax.div(row, yw), 3)
    tz = lax.rem(lax.div(row, 3 * yw), 3)
    yo = lax.div(iota((rows, lanes), 1), ch)
    for wide, ref_out, direction in zip(tiled, first_out, (1, -1)):
        total = jnp.zeros((rows, lanes), F32)
        for ty in range(3):
            number = 9 * tx + 3 * ty + tz
            number = number if direction > 0 else 26 - number
            pick = (iota((rows, 27), 1) == number).astype(F32).astype(BF)
            here = lax.rem(yo + (ty - 1 + yw), yw) == yi
            total = total + jnp.where(here, dot(pick, wide), 0.0)
        ref_out[...] = total.astype(BF)

    rows = p.narrow
    row = iota((rows, 1), 0)
    yo = lax.rem(row, yw)
    field = lax.rem(lax.div(row, yw), 4)
    tx = lax.div(row, 4 * yw)
    yi = lax.div(iota((rows, lanes), 1), ch)
    for wide, ref_out, direction in zip(tiled[::-1], last_out, (1, -1)):
        for tz in range(3):
            total = jnp.zeros((rows, lanes), F32)
            for ty in range(3):
                number = 9 * tx + 3 * ty + tz
                number = number if direction > 0 else 26 - number
                if direction > 0:
                    factor = jnp.where(field == 0, 1, 0)
                else:
                    factor = jnp.where(
                        field == 0,
                        1,
                        jnp.where(field == 1, 1 - tx, jnp.where(field == 2, 1 - ty, 1 - tz)),
                    )
                factor = jnp.where(tx < 3, factor, 0).astype(F32)
                pick = (iota((rows, 27), 1) == number).astype(F32).astype(BF)
                here = lax.rem(yo + (ty - 1 + yw), yw) == yi
                total = total + jnp.where(here, dot(pick, wide), 0.0) * factor
            ref_out[tz] = total.astype(BF)


def spread_weights(p, w_first, w_second, w_third, w_last):
    def body(a, b, c, d, first, last, oa, ob, oc, od, o_first, o_back, o_last, o_cot):
        weights_kernel(
            p, (a, b, c, d), (first, last), (oa, ob, oc, od), (o_first, o_back), (o_last, o_cot)
        )

    dense = jax.ShapeDtypeStruct((9, p.lanes, p.lanes), BF)
    single = jax.ShapeDtypeStruct((18 * p.yw, p.lanes), BF)
    narrow = jax.ShapeDtypeStruct((3, p.narrow, p.lanes), BF)
    flops = 2 * 4 * 9 * 3 * p.lanes * p.lanes * p.lanes
    return pl.pallas_call(
        body,
        name="spread_weights",
        out_shape=(dense,) * 4 + (single,) * 2 + (narrow,) * 2,
        in_specs=[VM] * 6,
        out_specs=(VM,) * 8,
        compiler_params=pltpu.CompilerParams(vmem_limit_bytes=LIMIT),
        cost_estimate=pl.CostEstimate(flops=flops, bytes_accessed=6 << 20, transcendentals=0),
    )(
        jnp.swapaxes(w_second, 1, 2),
        jnp.swapaxes(w_third, 1, 2),
        w_third,
        w_second,
        w_first,
        w_last,
    )


def cube_root(value):
    guess = jnp.exp(jnp.log(value) * (1.0 / 3.0))
    return guess - (guess - value / (guess * guess)) * (1.0 / 3.0)


def store_edges(p, ref, place, value):
    tiles = value.reshape(p.lo, STRIPS, p.lanes)
    ref[place, 1 : p.lo + 1] = tiles.astype(BF)
    ref[place, 0] = pltpu.roll(tiles[p.lo - 1], 1, 0).astype(BF)
    ref[place, p.lo + 1] = pltpu.roll(tiles[0], STRIPS - 1, 0).astype(BF)


def blocks(total, size):
    return [(start, min(size, total - start)) for start in range(0, total, size)]


def dense_planes(p, ref, w_ref, start, count):
    total = None
    for t in range(9):
        tx, tz = divmod(t, 3)
        rows = ref[start + tx : start + tx + count, tz : tz + p.lo]
        part = dot(rows.reshape(count * p.ze, p.lanes), w_ref[t])
        total = part if total is None else total + part
    return total


def gate(value):
    logistic = 0.5 * jnp.tanh(0.5 * value) + 0.5
    act = value * logistic
    return logistic, act


def slope_of(value, logistic, act):
    return logistic * (1.0 + value - act)


def to_planes(p, field, spread, planes_ref):
    high = field.astype(BF)
    low = (field - high.astype(F32)).astype(BF)
    flat = jnp.concatenate(
        [high.reshape(p.xe * p.yw, p.zp), low.reshape(p.xe * p.yw, p.zp)], axis=0
    )
    planes_ref[...] = dot(flat, spread).reshape(2, p.xe, p.yw, 3 * p.zp)


def single_plane(p, planes_ref, place, w_ref):
    pieces = []
    for half in range(2):
        for tz in range(3):
            piece = planes_ref[half, place : place + 3, :, tz * p.zp : (tz + 1) * p.zp]
            pieces.append(piece.reshape(3 * p.yw, p.zp))
    window = jnp.concatenate(pieces, axis=0).astype(BF)
    return dot_tn(window, w_ref[...])[: p.ze]


def narrow_fold(p, ref, w_ref, planes_ref, back):
    for start, count in blocks(p.xo + 2, 5):
        total = None
        for tz in range(3):
            rows = ref[start : start + count, tz : tz + p.lo].reshape(count * p.ze, p.lanes)
            part = dot_nt(rows, w_ref[tz])
            total = part if total is None else total + part
        planes_ref[start : start + count] = total.reshape(count, p.ze, p.narrow)
    lane = lax.div(iota((p.ze, p.narrow), 1), p.fields)
    fields = []
    for first in range(0, p.xo, GROUP):
        joined = jnp.zeros((p.ze, p.narrow), F32)
        for k in range(GROUP):
            total = None
            for tx in range(3):
                part = planes_ref[first + k + tx]
                shift = (k - tx) * p.fields % p.narrow
                part = pltpu.roll(part, shift, 1) if shift else part
                total = part if total is None else total + part
            joined = jnp.where(lane == k, total, joined)
        high = joined.astype(BF)
        rest = joined - high.astype(F32)
        mid = rest.astype(BF)
        low = (rest - mid.astype(F32)).astype(BF)
        parts = jnp.concatenate([high, mid, low], axis=0)
        natural = dot_tn(parts, back)[: GROUP * p.fields]
        fields.append(natural.reshape(GROUP, 4, p.yw, p.zq))
    return jnp.concatenate(fields, axis=0)


def update_kernel(p, current, external, weights, scratch):
    w_two, w_three, w_three_back, w_two_back, w_one, w_source, w_enhance, w_lever = weights
    planes, act_a, act_b, act_c, slope_one, slope_two, slope_three, narrow = scratch

    current = jnp.where(iota(current.shape, 2) < p.ze, current, 1.0)
    cube = cube_root(current)
    source = current * cube * cube

    shape = (p.zp, 3 * p.zp)
    lane = iota(shape, 1)
    tz = lax.div(lane, p.zp)
    row = lane - tz * p.zp
    cell = p.lo * jnp.bitwise_and(row, STRIPS - 1) + lax.div(row, STRIPS) + tz - 1
    spread = jnp.where((cell == iota(shape, 0)) & (row < p.ze), 1.0, 0.0).astype(BF)
    shape = (3 * p.ze, p.zq)
    row = lax.rem(iota(shape, 0), p.ze)
    cell = p.lo * jnp.bitwise_and(row, STRIPS - 1) + lax.div(row, STRIPS) - p.zh
    back = jnp.where((cell == iota(shape, 1)) & (cell < p.zo), 1.0, 0.0).astype(BF)

    to_planes(p, cube, spread, planes)
    for x in range(p.xo + 10):
        value = single_plane(p, planes, x, w_one)
        logistic, act = gate(value)
        store_edges(p, act_a, x, act)
        if 4 <= x < p.xo + 6:
            slope_one[x - 4] = slope_of(value, logistic, act)

    for start, count in blocks(p.xo + 8, 4):
        values = dense_planes(p, act_a, w_two, start, count)
        for k in range(count):
            x = start + k
            value = values[k * p.ze : (k + 1) * p.ze]
            logistic, act = gate(value)
            store_edges(p, act_b, x, act)
            if 2 <= x < p.xo + 6:
                slope_two[x - 2] = slope_of(value, logistic, act)

    to_planes(p, source, spread, planes)
    for start, count in blocks(p.xo + 6, 7):
        values = dense_planes(p, act_b, w_three, start, count)
        for k in range(count):
            x = start + k
            value = values[k * p.ze : (k + 1) * p.ze]
            logistic, act = gate(value)
            if 2 <= x < p.xo + 4:
                store_edges(p, act_c, x - 2, act)
            slope = slope_of(value, logistic, act)
            store_edges(p, act_a, x, single_plane(p, planes, x + 2, w_source) * slope)

    enhance = narrow_fold(p, act_c, w_enhance, narrow, back)[:, 0]

    for start, count in blocks(p.xo + 4, 4):
        values = dense_planes(p, act_a, w_three_back, start, count)
        for k in range(count):
            x = start + k
            store_edges(p, act_b, x, values[k * p.ze : (k + 1) * p.ze] * slope_two[x])

    for start, count in blocks(p.xo + 2, 5):
        values = dense_planes(p, act_b, w_two_back, start, count)
        for k in range(count):
            x = start + k
            store_edges(p, act_c, x, values[k * p.ze : (k + 1) * p.ze] * slope_one[x])

    levers = narrow_fold(p, act_c, w_lever, narrow, back)

    def natural(field, step):
        return pltpu.roll(field, (p.zp - p.zh - step) % p.zp, 2)[:, :, : p.zq]

    inner = cube[REACH : REACH + p.xo]
    here = natural(inner, 0)
    density = natural(current[REACH : REACH + p.xo], 0)
    source_here = natural(source[REACH : REACH + p.xo], 0)
    squared = here * here
    potential = (
        5.0 / 3.0 * squared * (C_TF + enhance)
        + levers[:, 0] / (3.0 * squared)
        + external
        - 4.0 / 3.0 * C_X * here
    )
    slopes = [
        natural(cube[REACH + 1 : REACH + 1 + p.xo], 0) - natural(cube[REACH - 1 : REACH - 1 + p.xo], 0),
        pltpu.roll(here, p.yw - 1, 1) - pltpu.roll(here, 1, 1),
        natural(inner, 1) - natural(inner, -1),
    ]
    weighted = density * jnp.exp(-TAU * potential)
    energy = source_here * (C_TF + enhance) + external * density - C_X * density * here
    terms = [weighted, density, energy - density * potential]
    for slope in slopes:
        for axis in range(3):
            terms.append(0.5 * slope * levers[:, 1 + axis])
    lane = iota((p.yw, p.zq), 1)
    y = iota((p.yw, p.zq), 0)
    own = (lane < p.zo) & (y >= p.own_y) & (y < p.own_y + p.ny)
    rows = []
    for term in terms:
        rows.append(jnp.sum(jnp.where(own, jnp.sum(term, axis=0), 0.0), axis=0, keepdims=True))
    rows.append(jnp.zeros((SUMS - len(rows), p.zq), F32))
    sums = jnp.sum(jnp.concatenate(rows, axis=0), axis=1, keepdims=True)
    return potential, weighted, jnp.broadcast_to(sums, (SUMS, 128))


def update_scratch(p):
    def acts(planes):
        return pltpu.VMEM((planes, p.lo + 2, STRIPS, p.lanes), BF)

    return [
        pltpu.VMEM((2, p.xe, p.yw, 3 * p.zp), F32),
        acts(p.xo + 10),
        acts(p.xo + 8),
        acts(p.xo + 2),
        pltpu.VMEM((p.xo + 2, p.ze, p.lanes), F32),
        pltpu.VMEM((p.xo + 4, p.ze, p.lanes), F32),
        pltpu.VMEM((8, 128), F32),
        pltpu.VMEM((p.xo + 2, p.ze, p.narrow), F32),
    ]


def update_cost(p):
    flops = 2 * 9 * p.lanes * p.lanes * p.ze * (4 * p.xo + 20)
    return pl.CostEstimate(flops=flops, bytes_accessed=6 << 20, transcendentals=0)


def kernel_call(name, body, out_shape, n_smem, n_vmem, scratch=(), cost=None):
    return pl.pallas_call(
        body,
        name=name,
        out_shape=out_shape,
        in_specs=[SM] * n_smem + [VM] * n_vmem,
        out_specs=jax.tree.map(lambda _: VM, out_shape),
        scratch_shapes=list(scratch),
        compiler_params=pltpu.CompilerParams(vmem_limit_bytes=LIMIT),
        cost_estimate=cost,
    )


def f32(*shape):
    return jax.ShapeDtypeStruct(shape, F32)


def widen(cells, axis, dim, before, after):
    size = cells.shape[dim]
    count = lax.axis_size(axis)

    def fetch(step, start, stop):
        piece = lax.slice_in_dim(cells, start, stop, axis=dim)
        if step % count == 0:
            return piece
        return lax.ppermute(piece, axis, [(i, (i + step) % count) for i in range(count)])

    pieces = [cells]
    left = before
    step = 1
    while left > 0:
        take = min(left, size)
        pieces.insert(0, fetch(step, size - take, size))
        left -= take
        step += 1
    left = after
    step = 1
    while left > 0:
        take = min(left, size)
        pieces.append(fetch(-step, 0, take))
        left -= take
        step += 1
    return jnp.concatenate(pieces, axis=dim)


def any_mesh(density, external, w_first, w_second, w_third, w_last):
    nx, ny, nz = density.shape
    ch = w_first.shape[1]
    yw = up(ny + 2 * REACH, 8)
    own_y = (yw - ny) // 2
    xo = up(nx, GROUP)
    p = Plan(xo, yw, own_y, ny, nz, ch)
    weights = spread_weights(p, w_first, w_second, w_third, w_last)
    axes = ("gx", "gy", "gz")
    count = nx * ny * nz * lax.axis_size("gx") * lax.axis_size("gy") * lax.axis_size("gz")
    total_mass = lax.psum(jnp.sum(density), axes)

    def body(cur, ext, *refs):
        weight_refs, (o_pot, o_weighted, o_sums), scratch = refs[:8], refs[8:11], refs[11:]
        pot, weighted, sums = update_kernel(p, cur[...], ext[...], weight_refs, scratch)
        o_pot[...] = pot
        o_weighted[...] = weighted
        o_sums[...] = sums

    call = kernel_call(
        "update",
        body,
        (f32(xo, yw, p.zq), f32(xo, yw, p.zq), f32(SUMS, 128)),
        0,
        10,
        update_scratch(p),
        update_cost(p),
    )
    ext = jnp.pad(
        external, ((0, xo - nx), (own_y, yw - ny - own_y), (0, p.zq - nz))
    )
    current = density
    chem, stress = [], []
    for _ in range(STEPS):
        tile = widen(current, "gz", 2, p.zh, p.ze - nz - p.zh)
        tile = widen(tile, "gy", 1, own_y, yw - ny - own_y)
        tile = widen(tile, "gx", 0, REACH, REACH)
        tile = jnp.pad(tile, ((0, 0), (0, 0), (0, p.zp - p.ze)), constant_values=1.0)
        pot, weighted, sums = call(tile, ext, *weights)
        totals = lax.psum(sums[:, 0], axes)
        chem.append(jnp.log(total_mass / totals[0]) / TAU)
        moments = totals[3:12].reshape(3, 3)
        stress.append((moments + jnp.eye(3, dtype=F32) * totals[2]) / count)
        current = weighted[:nx, own_y : own_y + ny, :nz] * (total_mass / totals[0])
        potential = pot[:nx, own_y : own_y + ny, :nz]
    return current, potential, jnp.stack(chem), jnp.stack(stress)


def split_pairs(density, external, w_first, w_second, w_third, w_last):
    nx, ny, nz = density.shape
    ch = w_first.shape[1]
    half = nz // 2
    p = Plan(nx, 2 * ny, 0, 2 * ny, half, ch)
    lanes = p.zp
    gy = lax.axis_index("gy")
    where = gy.astype(jnp.int32).reshape(1)
    cells = nx * ny * nz * 16
    axes = ("gx", "gy", "gz")

    def along_x(cells_out, step):
        return lax.ppermute(cells_out, "gx", [(i, (i + step) % 4) for i in range(4)])

    def quarter(number):
        return (number % 2) * 2 + number // 2

    def along_z(cells_out, step):
        pairs = [(quarter(q), quarter((q + step) % 4)) for q in range(4)]
        return lax.ppermute(cells_out, ("gy", "gz"), pairs)

    weights = spread_weights(p, w_first, w_second, w_third, w_last)

    wide = jnp.concatenate(
        [
            along_x(density[nx - REACH :], 1),
            density,
            along_x(density[:REACH], -1),
            external,
        ],
        axis=0,
    )
    from_y = lax.ppermute(wide, "gy", [(0, 1), (1, 0)])
    from_z = lax.ppermute(wide, "gz", [(0, 1), (1, 0)])
    from_yz = lax.ppermute(wide, ("gy", "gz"), [(i, 3 - i) for i in range(4)])
    planes = p.xe + nx

    def emit(weighted, sums, o_own, o_low, o_high):
        extra = sums.reshape(2, 8, 128)
        o_own[...] = weighted
        o_low[:REACH] = weighted[:REACH]
        o_low[REACH:] = extra
        o_high[:REACH] = weighted[nx - REACH :]
        o_high[REACH:] = extra

    def first_body(where_ref, own, y, z, yz, *refs):
        weight_refs, outs, tile, scratch = refs[:8], refs[8:12], refs[12], refs[13:]
        second = where_ref[0] == 1
        shift = jnp.where(second, nz - half + p.zh, p.zh)
        lane = iota((planes, p.yw, lanes), 2)
        for ref, other in ((own, y), (z, yz)):
            mine, theirs = ref[...], other[...]
            lower = jnp.where(second, theirs, mine)
            upper = jnp.where(second, mine, theirs)
            cells_here = jnp.concatenate([lower, upper], axis=1)
            moved = pltpu.roll(cells_here, shift, 2)
            if ref is own:
                tile[...] = moved
            else:
                begin = jnp.where(second, half + p.zh, 0)
                end = jnp.where(second, lanes, p.zh)
                tile[...] = jnp.where((lane >= begin) & (lane < end), moved, tile[...])
        cur = tile[: p.xe]
        ext = pltpu.roll(tile[p.xe :], lanes - p.zh, 2)
        _, weighted, sums = update_kernel(p, cur, ext, weight_refs, scratch)
        emit(weighted, sums, *outs[:3])
        outs[3][...] = ext

    message = f32(REACH + 2, p.yw, lanes)
    own, low, high, ext = kernel_call(
        "update_one",
        first_body,
        (f32(nx, p.yw, lanes), message, message, f32(nx, p.yw, lanes)),
        1,
        12,
        [pltpu.VMEM((planes, p.yw, lanes), F32)] + update_scratch(p),
        update_cost(p),
    )(where, wide, from_y, from_z, from_yz, *weights)

    left = along_x(high, 1)
    right = along_x(low, -1)
    far = along_x(low[REACH:], 2)

    packs = up(p.xe, 8) // 8

    def join_body(own_ref, low_ref, left_ref, right_ref, far_ref, o_tile, o_down, o_up, o_sums):
        tile = jnp.concatenate([left_ref[:REACH], own_ref[...], right_ref[:REACH]], axis=0)
        sums = low_ref[REACH:] + left_ref[REACH:] + right_ref[REACH:] + far_ref[...]
        o_tile[...] = tile
        o_sums[...] = sums
        lane = lax.div(iota((p.yw, lanes), 1), p.zh)
        for ref, start in ((o_down, 0), (o_up, half - p.zh)):
            for pack in range(packs):
                joined = jnp.zeros((p.yw, lanes), F32)
                for k in range(min(8, p.xe - 8 * pack)):
                    moved = pltpu.roll(tile[8 * pack + k], (k * p.zh - start) % lanes, 1)
                    joined = jnp.where(lane == k, moved, joined)
                ref[pack] = joined
            ref[packs:] = sums

    edge = f32(packs + 2, p.yw, lanes)
    tile, down, upper, sums = kernel_call(
        "join",
        join_body,
        (f32(p.xe, p.yw, lanes), edge, edge, f32(2, 8, 128)),
        0,
        5,
    )(own, low, left, right, far)
    below = along_z(upper, 1)
    above = along_z(down, -1)
    across = lax.ppermute(sums, "gz", [(0, 1), (1, 0)])

    def second_body(where_ref, tile_ref, below_ref, above_ref, sums_ref, across_ref, ext_ref, *refs):
        weight_refs, outs, cur, scratch = refs[:8], refs[8:12], refs[12], refs[13:]
        o_keep, o_send, o_sums, o_totals = outs
        totals = sums_ref[...] + across_ref[...] + below_ref[packs:] + above_ref[packs:]
        o_totals[...] = totals
        scale = totals[0, 1:2, :] / totals[0, 0:1, :]
        lane = iota((p.yw, lanes), 1)
        for x in range(p.xe):
            pack, k = divmod(x, 8)
            lower = pltpu.roll(below_ref[pack], -k * p.zh % lanes, 1)
            top = pltpu.roll(above_ref[pack], (p.zh + half - k * p.zh) % lanes, 1)
            middle = pltpu.roll(tile_ref[x], p.zh, 1)
            joined = jnp.where(lane < p.zh, lower, jnp.where(lane < p.zh + half, middle, top))
            cur[x] = joined * scale
        pot, weighted, sums_here = update_kernel(p, cur[...], ext_ref[...], weight_refs, scratch)
        o_sums[...] = sums_here
        both = jnp.where(
            iota(pot.shape, 2) < half, pot, pltpu.roll(weighted, half, 2)
        )
        second = where_ref[0] == 1
        lower, top = both[:, :ny], both[:, ny:]
        o_keep[...] = jnp.where(second, top, lower)
        o_send[...] = jnp.where(second, lower, top)

    share = f32(nx, ny, lanes)
    keep, send, sums, totals = kernel_call(
        "update_two",
        second_body,
        (share, share, f32(SUMS, 128), f32(2, 8, 128)),
        1,
        14,
        [pltpu.VMEM((p.xe, p.yw, lanes), F32)] + update_scratch(p),
        update_cost(p),
    )(where, tile, below, above, sums, across, ext, *weights)

    other = lax.ppermute(send, "gy", [(0, 1), (1, 0)])
    gathered = lax.all_to_all(
        jnp.broadcast_to(sums[None], (16, SUMS, 128)), axes, 0, 0, tiled=True
    )

    def last_body(where_ref, keep_ref, other_ref, all_ref, totals_ref, o_new, o_pot, o_chem, o_stress):
        first = totals_ref[...].reshape(SUMS, 128)
        last = jnp.sum(all_ref[...], axis=0)
        mass = first[1:2]
        scale = mass / last[0:1]
        second = where_ref[0] == 1
        mine, theirs = keep_ref[...], other_ref[...]
        lower = jnp.where(second, theirs, mine)
        top = jnp.where(second, mine, theirs)
        lane = iota((nx, ny, nz), 2)
        o_pot[...] = jnp.where(lane < half, lower, pltpu.roll(top, half, 2))
        o_new[...] = jnp.where(lane < half, pltpu.roll(lower, half, 2), top) * scale
        row, column = iota((8, 128), 0), iota((8, 128), 1)
        for step, total in enumerate((first, last)):
            o_chem[step : step + 1] = jnp.log(mass / total[0:1]) * (1.0 / TAU)
            stress = jnp.where(row == column, total[2:3], 0.0)
            for a in range(3):
                for b in range(3):
                    k = 3 + 3 * a + b
                    stress = stress + jnp.where((row == a) & (column == b), total[k : k + 1], 0.0)
            o_stress[step] = stress[:3, :3] * (1.0 / cells)

    new, potential, chem, stress = kernel_call(
        "finish",
        last_body,
        (f32(nx, ny, nz), f32(nx, ny, nz), f32(STEPS, 128), f32(STEPS, 3, 3)),
        1,
        4,
    )(where, keep, other, gathered, totals)
    return new, potential, chem[:, 0], stress


def on_device(density, external, w_first, w_second, w_third, w_last):
    mesh = tuple(lax.axis_size(axis) for axis in ("gx", "gy", "gz"))
    if mesh == (4, 2, 2) and density.shape == (8, 4, 128):
        return split_pairs(density, external, w_first, w_second, w_third, w_last)
    return any_mesh(density, external, w_first, w_second, w_third, w_last)


def solution(mesh):
    cells = P(("boxes", "gx"), "gy", "gz")
    return jax.shard_map(
        on_device,
        mesh=mesh,
        in_specs=(cells, cells, P(), P(), P(), P()),
        out_specs=(cells, cells, P("boxes"), P("boxes", None, None)),
        check_vma=False,
    )
```

time: 442 us -> 78.2 us (0.18)
  local copies, waits for them, and re-layouts: 126 us -> 12.8 us
  starting transfers between devices: 110 us -> 18.4 us
  blocking collectives: 67.5 us -> 0 us
  matrix products: 44 us -> 0 us
  waiting for transfers between devices: 52.9 us -> 14.3 us
  Pallas kernels: 0 us -> 31.1 us
  other arithmetic: 28.5 us -> 0 us
  between operations: 8.16 us -> 0.72 us
    ppermute x96 -> x12, starting transfers between devices: 110 us -> 14.8 us  [the longest x5 8.88 us: along_x(): lax.ppermute(cells_out, 'gx', [(i, (i + step) % 4) for i in range(4)])]
    conv_general_dilated x40 -> x0, local copies, waits for them, and re-layouts: 85.4 us -> none  [dense_apply(): lax.conv_general_dilated(padded[None], kernel_block, (1, 1, 1), 'VALID',...]
    psum x2 -> x0, blocking collectives: 67.5 us -> none  [on_device(): lax.psum((jnp.stack([norm_part, mass_part]), stress_part), ('gx', 'gy', '...]
    ppermute x96 -> x12, waiting for transfers between devices: 52.9 us -> 10.5 us  [the longest x5 4.56 us: along_x(): lax.ppermute(cells_out, 'gx', [(i, (i + step) % 4) for i in range(4)])]
    conv_general_dilated x8 -> x0, matrix products: 33.8 us -> none  [dense_apply(): lax.conv_general_dilated(padded[None], kernel_block, (1, 1, 1), 'VALID',...]
    pallas_call x0 -> x5, Pallas kernels: none -> 31.1 us  [the longest x1 11.1 us: split_pairs(): kernel_call('update_two', second_body, (share, share, f32(SUMS, 128), f32...]
    another operation x6 -> x0, local copies, waits for them, and re-layouts: 14.2 us -> none  [the longest x2 12.2 us: evaluate(): stress_part = jnp.stack([energy_part - virial_part] + moment_parts)]
    dot_general x8 -> x0, matrix products: 10.2 us -> none  [the longest x4 6.43 us: single_apply(): jnp.einsum('dc,dxyz->cxyz', weights.astype(jnp.float32), stacked, precisi...]
  transfers between devices with their start and end apart: 96 -> 13, of which waited for: 46 -> 6; matrix products, arithmetic and copies ran while one was open for 14% -> 6% of each run, Pallas kernels for 0% -> 8%
where the time goes in v1:
time: 78.2 us; the launch traced here: 77.4 us
  Pallas kernels  31.1 us (40%)
  starting transfers between devices  18.4 us (24%)
  waiting for transfers between devices  14.3 us (18%)
  local copies, waits for them, and re-layouts  12.8 us (16%)
    pallas_call x1, Pallas kernels, split_pairs(): kernel_call('update_two', second_body, (share, share, f32(SUMS, 128), f32...  11.1 us
    pallas_call x1, Pallas kernels, split_pairs(): kernel_call('update_one', first_body, (f32(nx, p.yw, lanes), message, mes...  11.1 us
    ppermute x5, starting transfers between devices, along_x(): lax.ppermute(cells_out, 'gx', [(i, (i + step) % 4) for i in range(4)])  8.88 us
    unnamed x30, local copies, waits for them, and re-layouts  8 us
    pallas_call x1, Pallas kernels, spread_weights(): pl.pallas_call(body, name='spread_weights', out_shape=(dense,) * 4 + (sin...  5.84 us
    ppermute x5, waiting for transfers between devices, along_x(): lax.ppermute(cells_out, 'gx', [(i, (i + step) % 4) for i in range(4)])  4.56 us
    all_to_all x1, waiting for transfers between devices, split_pairs(): lax.all_to_all(jnp.broadcast_to(sums[None], (16, SUMS, 128)), axes, 0, 0,...  3.87 us
    all_to_all x1, starting transfers between devices, split_pairs(): lax.all_to_all(jnp.broadcast_to(sums[None], (16, SUMS, 128)), axes, 0, 0,...  3.51 us
  transfers between devices with their start and end apart: 13, of which 6 were waited for; matrix products, arithmetic and copies ran while one was open for 6% of the time, Pallas kernels for 8%

profile of v1, /device:TPU:0, one launch (start us, length us, event | category | flops | bytes accessed | tf_op | source)
XLA Modules:
  0.0 77.4 jit_solution(14634305708175799522)
XLA Ops:
  0.6 0.8 %fusion = (f32[6,4,128]{2,1,0:T(4,128)S(1)}, f32[6,4,128]{2,1,0:T(4,128)S(1)}) fusion(f32[8,4,128]{2,1,0:T(4,128)} %param.6), kind=kLoop, calls=%fused_computation.5 | loop fusion | bytes 49152 | tf_op jit(solution)/shard_map/slice | solution.py:487
  1.4 3.0 %collective-permute-start = (f32[6,4,128]{2,1,0:T(4,128)S(1)}, f32[6,4,128]{2,1,0:T(4,128)S(1)}, u32[]{:S(2)}, u32[]{:S(2)}) collective-permute-start(f32[6,4,128]{2,1,0:T(4,128)S(1)} %get-tuple-element.61), channel_id=1, source_target_pairs={{0,4},{4,8},{8,12},{12,0},{1,5},{5,9},{9,13},{13,1},{2,6},{6,10},{... | collective-permute-start | bytes 36872 | tf_op jit(solution)/shard_map/ppermute | solution.py:472
  4.4 2.0 %collective-permute-start.1 = (f32[6,4,128]{2,1,0:T(4,128)S(1)}, f32[6,4,128]{2,1,0:T(4,128)S(1)}, u32[]{:S(2)}, u32[]{:S(2)}) collective-permute-start(f32[6,4,128]{2,1,0:T(4,128)S(1)} %get-tuple-element.60), channel_id=1, source_target_pairs={{0,12},{4,0},{8,4},{12,8},{1,13},{5,1},{9,5},{13,9},{2,14},{6,2},{... | collective-permute-start | bytes 36872 | tf_op jit(solution)/shard_map/ppermute | solution.py:472
  6.5 1.8 %copy.13 = bf16[27,32,32]{1,2,0:T(8,128)(2,1)} copy(bf16[27,32,32]{2,1,0:T(8,128)(2,1)} %d.1) | data formatting | bytes 110592 | tf_op args[3]
  8.2 1.8 %copy.14 = bf16[27,32,32]{1,2,0:T(8,128)(2,1)} copy(bf16[27,32,32]{2,1,0:T(8,128)(2,1)} %c.1) | data formatting | bytes 110592 | tf_op args[4]
  10.0 0.0 collective-permute-done
  10.0 0.7 constant_dynamic-update-slice_fusion.2
  10.7 0.0 collective-permute-done.1
  10.7 0.7 constant_dynamic-update-slice_fusion.own
  11.5 1.7 %collective-permute-start.2 = (f32[28,4,128]{2,1,0:T(4,128)S(1)}, f32[28,4,128]{2,1,0:T(4,128)S(1)}, u32[]{:S(2)}, u32[]{:S(2)}) collective-permute-start(f32[28,4,128]{2,1,0:T(4,128)S(1)} %constant_dynamic-update-slice_fusion.own), channel_id=1, source_target_pairs={{0,2},{2,0},{1,3},{3,1},{4,6},{6,4},{5,7},{7,5},{8,10},{10,8},{9,1... | collective-permute-start | bytes 172040 | tf_op jit(solution)/shard_map/ppermute | solution.py:492
  13.2 0.0 collective-permute-start.3
  13.2 0.4 collective-permute-start.4
  13.6 5.8 %spread_weights.1 = (bf16[9,256,256]{2,1,0:T(8,128)(2,1)}, bf16[9,256,256]{2,1,0:T(8,128)(2,1)}, bf16[9,256,256]{2,1,0:T(8,128)(2,1)}, bf16[9,256,256]{2,1,0:T(8...) custom-call(bf16[27,32,32]{2,1,0:T(8,128)(2,1)} %bitcast.3, ...), custom_call_target="tpu_custom_call" | custom-call | flops 3623878656 | bytes 6291456 | tf_op jit(solution)/shard_map/spread_weights/pallas_call | solution.py:142
  19.4 0.0 copy-done.5
  19.4 0.0 collective-permute-done.2.y
  19.5 0.0 copy-start.6
  19.5 0.0 collective-permute-done.3.z
  19.5 0.0 collective-permute-done.4.yz
  19.5 0.6 copy-done.6
  20.1 0.1 copy-done.7
  20.1 11.1 %update_one.1 = (f32[8,8,128]{2,1,0:T(8,128)}, f32[8,8,128]{2,1,0:T(8,128)}, f32[8,8,128]{2,1,0:T(8,128)}, f32[8,8,128]{2,1,0:T(8,128)}) custom-call(s32[1]{0:T(128)} %bitcast.where_ref, f32[28,4,128]{2,1,0:T(4,128)} %copy-done.5, f32[28,4,128]{2,1,0:T(4,128)} %copy-done.6, f32[28,4,128]{2,1,0:T(4,128)} %copy-done.7, f32[28,4,128]{2,1,0:T(4,128)} %copy-done.8, ...), custom_call_target="tpu_custom_call" | custom-call | flops 4907335680 | bytes 6291456 | tf_op jit(solution)/shard_map/update_one/pallas_call | solution.py:529
  31.2 0.0 collective-permute-start.5
  31.2 3.8 %collective-permute-start.6 = (f32[8,8,128]{2,1,0:T(8,128)}, f32[8,8,128]{2,1,0:T(8,128)S(1)}, u32[]{:S(2)}, u32[]{:S(2)}) collective-permute-start(f32[8,8,128]{2,1,0:T(8,128)} %get-tuple-element.37.low_ref), channel_id=1, source_target_pairs={{0,12},{4,0},{8,4},{12,8},{1,13},{5,1},{9,5},{13,9},{2,14},{6,2},{... | collective-permute-start | bytes 98312 | tf_op jit(solution)/shard_map/ppermute | solution.py:472
  35.0 0.7 slice.14
  35.7 0.0 collective-permute-start.7
  35.7 4.5 %collective-permute-done.7.far_ref = f32[2,8,128]{2,1,0:T(8,128)S(1)} collective-permute-done((f32[2,8,128]{2,1,0:T(8,128)S(1)}, f32[2,8,128]{2,1,0:T(8,128)S(1)}, u32[]{:S(2)}, u32[]{:S(2)}) %collective-permute-start.7) | collective-permute-done | bytes 8224 | tf_op jit(solution)/shard_map/ppermute | solution.py:472
  40.3 0.0 collective-permute-done.5.left_ref
  40.3 0.0 collective-permute-done.6.right_ref
  40.3 0.6 copy-done.4
  40.9 0.0 copy-done.1
  40.9 1.5 %join.1 = (f32[20,8,128]{2,1,0:T(8,128)}, f32[5,8,128]{2,1,0:T(8,128)}, f32[5,8,128]{2,1,0:T(8,128)}, f32[2,8,128]{2,1,0:T(8,128)}) custom-call(f32[8,8,128]{2,1,0:T(8,128)} %get-tuple-element.36.own_ref, f32[8,8,128]{2,1,0:T(8,128)} %get-tuple-element.37.low_ref, f32[8,8,128]{2,1,0:T(8,128)} %copy-done.1, f32[8,8,128]{2,1,0:T(8,128)} %copy-done.2, ...), custom_call_target="tpu_custom_call" | custom-call | tf_op jit(solution)/shard_map/join/pallas_call | solution.py:561
  42.4 1.7 %collective-permute-start.8 = (f32[5,8,128]{2,1,0:T(8,128)}, f32[5,8,128]{2,1,0:T(8,128)S(1)}, u32[]{:S(2)}, u32[]{:S(2)}) collective-permute-start(f32[5,8,128]{2,1,0:T(8,128)} %get-tuple-element.40), channel_id=1, source_target_pairs={{0,2},{2,1},{1,3},{3,0},{4,6},{6,5},{5,7},{7,4},{8,10},{10,9},{9,1... | collective-permute-start | bytes 61448 | tf_op jit(solution)/shard_map/ppermute | solution.py:479
  44.2 0.0 collective-permute-start.9
  44.2 0.3 collective-permute-start.10
  44.5 1.1 %collective-permute-done.10.across_ref = f32[2,8,128]{2,1,0:T(8,128)S(1)} collective-permute-done((f32[2,8,128]{2,1,0:T(8,128)}, f32[2,8,128]{2,1,0:T(8,128)S(1)}, u32[]{:S(2)}, u32[]{:S(2)}) %collective-permute-start.10) | collective-permute-done | bytes 8224 | tf_op jit(solution)/shard_map/ppermute | solution.py:570
  45.6 0.3 collective-permute-done.8.below_ref
  45.9 2.3 %collective-permute-done.9.above_ref = f32[5,8,128]{2,1,0:T(8,128)S(1)} collective-permute-done((f32[5,8,128]{2,1,0:T(8,128)}, f32[5,8,128]{2,1,0:T(8,128)S(1)}, u32[]{:S(2)}, u32[]{:S(2)}) %collective-permute-start.9) | collective-permute-done | bytes 20512 | tf_op jit(solution)/shard_map/ppermute | solution.py:479
  48.2 0.6 copy-done.10
  48.7 11.1 %update_two.1 = (f32[8,4,128]{2,1,0:T(4,128)}, f32[8,4,128]{2,1,0:T(4,128)}, f32[16,128]{1,0:T(8,128)}, f32[2,8,128]{2,1,0:T(8,128)}) custom-call(s32[1]{0:T(128)} %bitcast.where_ref, f32[20,8,128]{2,1,0:T(8,128)} %get-tuple-element.39.tile_ref, f32[5,8,128]{2,1,0:T(8,128)} %copy-done.9, f32[5,8,128]{2,1,0:T(8,128)} %copy-done.10, ...), custom_call_target="tpu_custom_call" | custom-call | flops 4907335680 | bytes 6291456 | tf_op jit(solution)/shard_map/update_two/pallas_call | solution.py:597
  59.8 1.4 %broadcast_in_dim.2 = f32[16,16,128]{2,1,0:T(8,128)} broadcast(f32[16,128]{1,0:T(8,128)} %get-tuple-element.46), dimensions={1,2} | broadcast | bytes 139264 | tf_op jit(solution)/shard_map/broadcast_in_dim | solution.py:609
  61.2 3.5 %all-to-all-start = ((f32[16,16,128]{2,1,0:T(8,128)}), f32[16,16,128]{2,1,0:T(8,128)S(1)}, u32[]{:S(2)}, u32[]{:S(2)}) async-start(f32[16,16,128]{2,1,0:T(8,128)} %broadcast_in_dim.2), calls=%async_computation | async-start | bytes 262144 | tf_op jit(solution)/shard_map/all_to_all | solution.py:608
  64.7 1.8 %collective-permute-start.11 = (f32[8,4,128]{2,1,0:T(4,128)}, f32[8,4,128]{2,1,0:T(4,128)S(1)}, u32[]{:S(2)}, u32[]{:S(2)}) collective-permute-start(f32[8,4,128]{2,1,0:T(4,128)} %get-tuple-element.45), channel_id=1, source_target_pairs={{0,2},{2,0},{1,3},{3,1},{4,6},{6,4},{5,7},{7,5},{8,10},{10,8},{9,1... | collective-permute-start | bytes 49160 | tf_op jit(solution)/shard_map/ppermute | solution.py:607
  66.5 2.2 %collective-permute-done.11.other_ref = f32[8,4,128]{2,1,0:T(4,128)S(1)} collective-permute-done((f32[8,4,128]{2,1,0:T(4,128)}, f32[8,4,128]{2,1,0:T(4,128)S(1)}, u32[]{:S(2)}, u32[]{:S(2)}) %collective-permute-start.11) | collective-permute-done | bytes 16416 | tf_op jit(solution)/shard_map/ppermute | solution.py:607
  68.7 3.9 %all-to-all-done.all_ref = f32[16,16,128]{2,1,0:T(8,128)S(1)} async-done(((f32[16,16,128]{2,1,0:T(8,128)}), f32[16,16,128]{2,1,0:T(8,128)S(1)}, u32[]{:S(2)}, u32[]{:S(2)}) %all-to-all-start) | async-done | bytes 131104 | tf_op jit(solution)/shard_map/all_to_all | solution.py:608
  72.6 0.6 copy-done
  73.3 1.6 %finish.1 = (f32[8,4,128]{2,1,0:T(4,128)}, f32[8,4,128]{2,1,0:T(4,128)}, f32[2,128]{1,0:T(2,128)}, f32[2,3,3]{2,1,0:T(4,128)}) custom-call(s32[1]{0:T(128)} %bitcast.where_ref, f32[8,4,128]{2,1,0:T(4,128)} %get-tuple-element.44.keep_ref, f32[8,4,128]{2,1,0:T(4,128)} %copy-done.3, f32[16,16,128]{2,1,0:T(8,128)} %copy-done, ...), custom_call_target="tpu_custom_call" | custom-call | tf_op jit(solution)/shard_map/finish/pallas_call | solution.py:634
  74.9 1.3 %copy.15 = f32[2,3,3]{2,0,1:T(2,128)} copy(f32[2,3,3]{2,1,0:T(4,128)} %get-tuple-element.59) | data formatting | bytes 144
  76.1 1.2 %slice_reduce_fusion = f32[2]{0:T(128)} fusion(f32[2,128]{1,0:T(2,128)} %get-tuple-element.50), kind=kLoop, calls=%fused_computation.4 | loop fusion | bytes 16 | tf_op jit(solution)/shard_map/slice | solution.py:641
  (18 shorter events, 0.0 us)
Async XLA Ops:
  1.4 8.6 %collective-permute-start = (f32[6,4,128]{2,1,0:T(4,128)S(1)}, f32[6,4,128]{2,1,0:T(4,128)S(1)}, u32[]{:S(2)}, u32[]{:S(2)}) collective-permute-start(f32[6,4,128]{2,1,0:T(4,128)S(1)} %get-tuple-element.61), channel_id=1, source_target_pairs={{0,4},{4,8},{8,12},{12,0},{1,5},{5,9},{9,13},{13,1},{2,6},{6,10},{... | collective-permute-start | bytes 36872 | tf_op jit(solution)/shard_map/ppermute | solution.py:472
  4.4 6.3 %collective-permute-start.1 = (f32[6,4,128]{2,1,0:T(4,128)S(1)}, f32[6,4,128]{2,1,0:T(4,128)S(1)}, u32[]{:S(2)}, u32[]{:S(2)}) collective-permute-start(f32[6,4,128]{2,1,0:T(4,128)S(1)} %get-tuple-element.60), channel_id=1, source_target_pairs={{0,12},{4,0},{8,4},{12,8},{1,13},{5,1},{9,5},{13,9},{2,14},{6,2},{... | collective-permute-start | bytes 36872 | tf_op jit(solution)/shard_map/ppermute | solution.py:472
  11.5 8.0 %copy-start.5 = (f32[28,4,128]{2,1,0:T(4,128)}, f32[28,4,128]{2,1,0:T(4,128)S(1)}, u32[]{:S(2)}) copy-start(f32[28,4,128]{2,1,0:T(4,128)S(1)} %constant_dynamic-update-slice_fusion.own) | copy-start | bytes 172036
  11.5 8.0 %collective-permute-start.2 = (f32[28,4,128]{2,1,0:T(4,128)S(1)}, f32[28,4,128]{2,1,0:T(4,128)S(1)}, u32[]{:S(2)}, u32[]{:S(2)}) collective-permute-start(f32[28,4,128]{2,1,0:T(4,128)S(1)} %constant_dynamic-update-slice_fusion.own), channel_id=1, source_target_pairs={{0,2},{2,0},{1,3},{3,1},{4,6},{6,4},{5,7},{7,5},{8,10},{10,8},{9,1... | collective-permute-start | bytes 172040 | tf_op jit(solution)/shard_map/ppermute | solution.py:492
  13.2 6.3 %collective-permute-start.3 = (f32[28,4,128]{2,1,0:T(4,128)S(1)}, f32[28,4,128]{2,1,0:T(4,128)S(1)}, u32[]{:S(2)}, u32[]{:S(2)}) collective-permute-start(f32[28,4,128]{2,1,0:T(4,128)S(1)} %constant_dynamic-update-slice_fusion.own), channel_id=1, source_target_pairs={{0,1},{1,0},{2,3},{3,2},{4,5},{5,4},{6,7},{7,6},{8,9},{9,8},{10,11... | collective-permute-start | bytes 172040 | tf_op jit(solution)/shard_map/ppermute | solution.py:493
  13.2 6.3 %collective-permute-start.4 = (f32[28,4,128]{2,1,0:T(4,128)S(1)}, f32[28,4,128]{2,1,0:T(4,128)S(1)}, u32[]{:S(2)}, u32[]{:S(2)}) collective-permute-start(f32[28,4,128]{2,1,0:T(4,128)S(1)} %constant_dynamic-update-slice_fusion.own), channel_id=1, source_target_pairs={{0,3},{1,2},{2,1},{3,0},{4,7},{5,6},{6,5},{7,4},{8,11},{9,10},{10,... | collective-permute-start | bytes 172040 | tf_op jit(solution)/shard_map/ppermute | solution.py:494
  19.5 0.6 copy-start.6
  19.5 0.6 copy-start.7
  19.5 0.6 copy-start.8
  31.2 9.1 %collective-permute-start.5 = (f32[8,8,128]{2,1,0:T(8,128)}, f32[8,8,128]{2,1,0:T(8,128)S(1)}, u32[]{:S(2)}, u32[]{:S(2)}) collective-permute-start(f32[8,8,128]{2,1,0:T(8,128)} %get-tuple-element.38), channel_id=1, source_target_pairs={{0,4},{4,8},{8,12},{12,0},{1,5},{5,9},{9,13},{13,1},{2,6},{6,10},{... | collective-permute-start | bytes 98312 | tf_op jit(solution)/shard_map/ppermute | solution.py:472
  31.2 9.1 %collective-permute-start.6 = (f32[8,8,128]{2,1,0:T(8,128)}, f32[8,8,128]{2,1,0:T(8,128)S(1)}, u32[]{:S(2)}, u32[]{:S(2)}) collective-permute-start(f32[8,8,128]{2,1,0:T(8,128)} %get-tuple-element.37.low_ref), channel_id=1, source_target_pairs={{0,12},{4,0},{8,4},{12,8},{1,13},{5,1},{9,5},{13,9},{2,14},{6,2},{... | collective-permute-start | bytes 98312 | tf_op jit(solution)/shard_map/ppermute | solution.py:472
  35.7 4.5 %collective-permute-start.7 = (f32[2,8,128]{2,1,0:T(8,128)S(1)}, f32[2,8,128]{2,1,0:T(8,128)S(1)}, u32[]{:S(2)}, u32[]{:S(2)}) collective-permute-start(f32[2,8,128]{2,1,0:T(8,128)S(1)} %slice.14), channel_id=1, source_target_pairs={{0,8},{4,12},{8,0},{12,4},{1,9},{5,13},{9,1},{13,5},{2,10},{6,14},... | collective-permute-start | bytes 24584 | tf_op jit(solution)/shard_map/ppermute | solution.py:472
  40.3 0.6 copy-start.4
  40.3 0.6 copy-start.1
  40.3 0.6 copy-start.2
  42.4 3.4 %collective-permute-start.8 = (f32[5,8,128]{2,1,0:T(8,128)}, f32[5,8,128]{2,1,0:T(8,128)S(1)}, u32[]{:S(2)}, u32[]{:S(2)}) collective-permute-start(f32[5,8,128]{2,1,0:T(8,128)} %get-tuple-element.40), channel_id=1, source_target_pairs={{0,2},{2,1},{1,3},{3,0},{4,6},{6,5},{5,7},{7,4},{8,10},{10,9},{9,1... | collective-permute-start | bytes 61448 | tf_op jit(solution)/shard_map/ppermute | solution.py:479
  44.2 4.0 %collective-permute-start.9 = (f32[5,8,128]{2,1,0:T(8,128)}, f32[5,8,128]{2,1,0:T(8,128)S(1)}, u32[]{:S(2)}, u32[]{:S(2)}) collective-permute-start(f32[5,8,128]{2,1,0:T(8,128)} %get-tuple-element.41), channel_id=1, source_target_pairs={{0,3},{2,0},{1,2},{3,1},{4,7},{6,4},{5,6},{7,5},{8,11},{10,8},{9,1... | collective-permute-start | bytes 61448 | tf_op jit(solution)/shard_map/ppermute | solution.py:479
  44.2 1.4 %collective-permute-start.10 = (f32[2,8,128]{2,1,0:T(8,128)}, f32[2,8,128]{2,1,0:T(8,128)S(1)}, u32[]{:S(2)}, u32[]{:S(2)}) collective-permute-start(f32[2,8,128]{2,1,0:T(8,128)} %get-tuple-element.42.sums_ref), channel_id=1, source_target_pairs={{0,1},{1,0},{2,3},{3,2},{4,5},{5,4},{6,7},{7,6},{8,9},{9,8},{10,11... | collective-permute-start | bytes 24584 | tf_op jit(solution)/shard_map/ppermute | solution.py:570
  45.6 2.6 %copy-start.11 = (f32[2,8,128]{2,1,0:T(8,128)}, f32[2,8,128]{2,1,0:T(8,128)S(1)}, u32[]{:S(2)}) copy-start(f32[2,8,128]{2,1,0:T(8,128)S(1)} %collective-permute-done.10.across_ref) | copy-start | bytes 24580
  45.9 2.3 %copy-start.9 = (f32[5,8,128]{2,1,0:T(8,128)}, f32[5,8,128]{2,1,0:T(8,128)S(1)}, u32[]{:S(2)}) copy-start(f32[5,8,128]{2,1,0:T(8,128)S(1)} %collective-permute-done.8.below_ref) | copy-start | bytes 61444
  48.1 0.6 copy-start.10
  61.2 11.4 %all-to-all-start = ((f32[16,16,128]{2,1,0:T(8,128)}), f32[16,16,128]{2,1,0:T(8,128)S(1)}, u32[]{:S(2)}, u32[]{:S(2)}) async-start(f32[16,16,128]{2,1,0:T(8,128)} %broadcast_in_dim.2), calls=%async_computation | async-start | bytes 262144 | tf_op jit(solution)/shard_map/all_to_all | solution.py:608
  64.7 4.0 %collective-permute-start.11 = (f32[8,4,128]{2,1,0:T(4,128)}, f32[8,4,128]{2,1,0:T(4,128)S(1)}, u32[]{:S(2)}, u32[]{:S(2)}) collective-permute-start(f32[8,4,128]{2,1,0:T(4,128)} %get-tuple-element.45), channel_id=1, source_target_pairs={{0,2},{2,0},{1,3},{3,1},{4,6},{6,4},{5,7},{7,5},{8,10},{10,8},{9,1... | collective-permute-start | bytes 49160 | tf_op jit(solution)/shard_map/ppermute | solution.py:607
  68.7 3.9 %copy-start.3 = (f32[8,4,128]{2,1,0:T(4,128)}, f32[8,4,128]{2,1,0:T(4,128)S(1)}, u32[]{:S(2)}) copy-start(f32[8,4,128]{2,1,0:T(4,128)S(1)} %collective-permute-done.11.other_ref) | copy-start | bytes 49156
  72.6 0.7 copy-start

commit v2 on v1

--- a/solution.py
+++ b/solution.py
@@ -15,7 +15,6 @@
 STRIPS = 16
 GROUP = 4
 SUMS = 16
-LIMIT = 60 << 20
 BF = jnp.bfloat16
 F32 = jnp.float32
 VM = pl.BlockSpec(memory_space=pltpu.VMEM)
@@ -43,8 +42,9 @@
 
 
 class Plan:
-    def __init__(self, xo, yw, own_y, ny, zo, ch):
+    def __init__(self, xo, yw, own_y, ny, zo, ch, limit):
         self.xo, self.yw, self.own_y, self.ny, self.zo, self.ch = xo, yw, own_y, ny, zo, ch
+        self.limit = limit << 20
         self.xe = xo + 2 * REACH
         self.ze = up(zo + 2 * REACH, STRIPS)
         self.zh = (self.ze - zo) // 2
@@ -56,29 +56,24 @@
         self.narrow = up(GROUP * self.fields, 128)
 
 
-def tap_no(tx, ty, tz, direction):
-    number = 9 * tx + 3 * ty + tz
-    return number if direction > 0 else 26 - number
-
-
 def weights_kernel(p, dense_in, single_in, dense_out, first_out, last_out):
     ch, yw, lanes = p.ch, p.yw, p.lanes
 
-    for ref_in, ref_out, direction in zip(dense_in, dense_out, (1, 1, -1, -1)):
+    for ref_in, ref_out in zip(dense_in, dense_out):
         taps = []
         for ty in range(3):
             taps.append(
                 jnp.concatenate(
-                    [ref_in[tap_no(t // 3, ty, t % 3, direction)] for t in range(9)], axis=0
+                    [ref_in[26 - (9 * (t // 3) + 3 * ty + t % 3)] for t in range(9)], axis=0
                 )
             )
+        taps = jnp.concatenate(taps, axis=1)
+        row, column = iota((3 * ch, lanes), 0), iota((3 * ch, lanes), 1)
+        ty = lax.div(row, ch)
         for yi in range(yw):
-            spread = None
-            for ty in range(3):
-                yo = (yi - ty + 1) % yw
-                place = (iota((ch, lanes), 1) == iota((ch, lanes), 0) + yo * ch).astype(F32)
-                part = dot(taps[ty], place.astype(BF))
-                spread = part if spread is None else spread + part
+            yo = lax.rem(yi + 1 - ty + yw, yw)
+            place = jnp.where(column == row + (yo - ty) * ch, 1.0, 0.0).astype(BF)
+            spread = dot(taps, place)
             ref_out[:, yi * ch : (yi + 1) * ch, :] = spread.astype(BF).reshape(9, ch, lanes)
 
     tile = (
@@ -130,31 +125,24 @@
 
 
 def spread_weights(p, w_first, w_second, w_third, w_last):
-    def body(a, b, c, d, first, last, oa, ob, oc, od, o_first, o_back, o_last, o_cot):
+    def body(second, third, first, last, o_second, o_third, o_first, o_back, o_last, o_cot):
         weights_kernel(
-            p, (a, b, c, d), (first, last), (oa, ob, oc, od), (o_first, o_back), (o_last, o_cot)
+            p, (second, third), (first, last), (o_second, o_third), (o_first, o_back), (o_last, o_cot)
         )
 
     dense = jax.ShapeDtypeStruct((9, p.lanes, p.lanes), BF)
     single = jax.ShapeDtypeStruct((18 * p.yw, p.lanes), BF)
     narrow = jax.ShapeDtypeStruct((3, p.narrow, p.lanes), BF)
-    flops = 2 * 4 * 9 * 3 * p.lanes * p.lanes * p.lanes
+    flops = 2 * 2 * 9 * 3 * p.ch * p.lanes * p.lanes
     return pl.pallas_call(
         body,
         name="spread_weights",
-        out_shape=(dense,) * 4 + (single,) * 2 + (narrow,) * 2,
-        in_specs=[VM] * 6,
-        out_specs=(VM,) * 8,
-        compiler_params=pltpu.CompilerParams(vmem_limit_bytes=LIMIT),
-        cost_estimate=pl.CostEstimate(flops=flops, bytes_accessed=6 << 20, transcendentals=0),
-    )(
-        jnp.swapaxes(w_second, 1, 2),
-        jnp.swapaxes(w_third, 1, 2),
-        w_third,
-        w_second,
-        w_first,
-        w_last,
-    )
+        out_shape=(dense,) * 2 + (single,) * 2 + (narrow,) * 2,
+        in_specs=[VM] * 4,
+        out_specs=(VM,) * 6,
+        compiler_params=pltpu.CompilerParams(vmem_limit_bytes=p.limit),
+        cost_estimate=pl.CostEstimate(flops=flops, bytes_accessed=3 << 20, transcendentals=0),
+    )(w_second, w_third, w_first, w_last)
 
 
 def cube_root(value):
@@ -173,12 +161,13 @@
     return [(start, min(size, total - start)) for start in range(0, total, size)]
 
 
-def dense_planes(p, ref, w_ref, start, count):
+def dense_planes(p, ref, w_ref, start, count, forward):
     total = None
     for t in range(9):
         tx, tz = divmod(t, 3)
         rows = ref[start + tx : start + tx + count, tz : tz + p.lo]
-        part = dot(rows.reshape(count * p.ze, p.lanes), w_ref[t])
+        rows = rows.reshape(count * p.ze, p.lanes)
+        part = dot_nt(rows, w_ref[8 - t]) if forward else dot(rows, w_ref[t])
         total = part if total is None else total + part
     return total
 
@@ -243,8 +232,8 @@
 
 
 def update_kernel(p, current, external, weights, scratch):
-    w_two, w_three, w_three_back, w_two_back, w_one, w_source, w_enhance, w_lever = weights
-    planes, act_a, act_b, act_c, slope_one, slope_two, slope_three, narrow = scratch
+    w_two, w_three, w_one, w_source, w_enhance, w_lever = weights
+    planes, act_a, act_b, act_c, slope_one, slope_two, narrow = scratch
 
     current = jnp.where(iota(current.shape, 2) < p.ze, current, 1.0)
     cube = cube_root(current)
@@ -270,7 +259,7 @@
             slope_one[x - 4] = slope_of(value, logistic, act)
 
     for start, count in blocks(p.xo + 8, 4):
-        values = dense_planes(p, act_a, w_two, start, count)
+        values = dense_planes(p, act_a, w_two, start, count, True)
         for k in range(count):
             x = start + k
             value = values[k * p.ze : (k + 1) * p.ze]
@@ -281,7 +270,7 @@
 
     to_planes(p, source, spread, planes)
     for start, count in blocks(p.xo + 6, 7):
-        values = dense_planes(p, act_b, w_three, start, count)
+        values = dense_planes(p, act_b, w_three, start, count, True)
         for k in range(count):
             x = start + k
             value = values[k * p.ze : (k + 1) * p.ze]
@@ -294,13 +283,13 @@
     enhance = narrow_fold(p, act_c, w_enhance, narrow, back)[:, 0]
 
     for start, count in blocks(p.xo + 4, 4):
-        values = dense_planes(p, act_a, w_three_back, start, count)
+        values = dense_planes(p, act_a, w_three, start, count, False)
         for k in range(count):
             x = start + k
             store_edges(p, act_b, x, values[k * p.ze : (k + 1) * p.ze] * slope_two[x])
 
     for start, count in blocks(p.xo + 2, 5):
-        values = dense_planes(p, act_b, w_two_back, start, count)
+        values = dense_planes(p, act_b, w_two, start, count, False)
         for k in range(count):
             x = start + k
             store_edges(p, act_c, x, values[k * p.ze : (k + 1) * p.ze] * slope_one[x])
@@ -340,7 +329,13 @@
         rows.append(jnp.sum(jnp.where(own, jnp.sum(term, axis=0), 0.0), axis=0, keepdims=True))
     rows.append(jnp.zeros((SUMS - len(rows), p.zq), F32))
     sums = jnp.sum(jnp.concatenate(rows, axis=0), axis=1, keepdims=True)
-    return potential, weighted, jnp.broadcast_to(sums, (SUMS, 128))
+    onto = iota((SUMS, 128), 0) == iota((SUMS, 128), 1)
+    row = jnp.sum(jnp.where(onto, sums, 0.0), axis=0, keepdims=True)
+    return potential, weighted, jnp.broadcast_to(row, (8, 128))
+
+
+def pick(row, number):
+    return jnp.sum(jnp.where(iota(row.shape, 1) == number, row, 0.0), axis=1, keepdims=True)
 
 
 def update_scratch(p):
@@ -354,7 +349,6 @@
         acts(p.xo + 2),
         pltpu.VMEM((p.xo + 2, p.ze, p.lanes), F32),
         pltpu.VMEM((p.xo + 4, p.ze, p.lanes), F32),
-        pltpu.VMEM((8, 128), F32),
         pltpu.VMEM((p.xo + 2, p.ze, p.narrow), F32),
     ]
 
@@ -364,15 +358,15 @@
     return pl.CostEstimate(flops=flops, bytes_accessed=6 << 20, transcendentals=0)
 
 
-def kernel_call(name, body, out_shape, n_smem, n_vmem, scratch=(), cost=None):
+def kernel_call(p, name, body, out_shape, n_smem, n_vmem, scratch=(), cost=None):
     return pl.pallas_call(
         body,
         name=name,
         out_shape=out_shape,
         in_specs=[SM] * n_smem + [VM] * n_vmem,
-        out_specs=jax.tree.map(lambda _: VM, out_shape),
+        out_specs=tuple(SM if len(shape.shape) == 1 else VM for shape in out_shape),
         scratch_shapes=list(scratch),
-        compiler_params=pltpu.CompilerParams(vmem_limit_bytes=LIMIT),
+        compiler_params=pltpu.CompilerParams(vmem_limit_bytes=p.limit),
         cost_estimate=cost,
     )
 
@@ -415,25 +409,26 @@
     yw = up(ny + 2 * REACH, 8)
     own_y = (yw - ny) // 2
     xo = up(nx, GROUP)
-    p = Plan(xo, yw, own_y, ny, nz, ch)
+    p = Plan(xo, yw, own_y, ny, nz, ch, 60)
     weights = spread_weights(p, w_first, w_second, w_third, w_last)
     axes = ("gx", "gy", "gz")
     count = nx * ny * nz * lax.axis_size("gx") * lax.axis_size("gy") * lax.axis_size("gz")
     total_mass = lax.psum(jnp.sum(density), axes)
 
     def body(cur, ext, *refs):
-        weight_refs, (o_pot, o_weighted, o_sums), scratch = refs[:8], refs[8:11], refs[11:]
+        weight_refs, (o_pot, o_weighted, o_sums), scratch = refs[:6], refs[6:9], refs[9:]
         pot, weighted, sums = update_kernel(p, cur[...], ext[...], weight_refs, scratch)
         o_pot[...] = pot
         o_weighted[...] = weighted
         o_sums[...] = sums
 
     call = kernel_call(
+        p,
         "update",
         body,
-        (f32(xo, yw, p.zq), f32(xo, yw, p.zq), f32(SUMS, 128)),
+        (f32(xo, yw, p.zq), f32(xo, yw, p.zq), f32(8, 128)),
         0,
-        10,
+        8,
         update_scratch(p),
         update_cost(p),
     )
@@ -448,7 +443,7 @@
         tile = widen(tile, "gx", 0, REACH, REACH)
         tile = jnp.pad(tile, ((0, 0), (0, 0), (0, p.zp - p.ze)), constant_values=1.0)
         pot, weighted, sums = call(tile, ext, *weights)
-        totals = lax.psum(sums[:, 0], axes)
+        totals = lax.psum(sums[0, :SUMS], axes)
         chem.append(jnp.log(total_mass / totals[0]) / TAU)
         moments = totals[3:12].reshape(3, 3)
         stress.append((moments + jnp.eye(3, dtype=F32) * totals[2]) / count)
@@ -461,7 +456,7 @@
     nx, ny, nz = density.shape
     ch = w_first.shape[1]
     half = nz // 2
-    p = Plan(nx, 2 * ny, 0, 2 * ny, half, ch)
+    p = Plan(nx, 2 * ny, 0, 2 * ny, half, ch, 20)
     lanes = p.zp
     gy = lax.axis_index("gy")
     where = gy.astype(jnp.int32).reshape(1)
@@ -494,16 +489,8 @@
     from_yz = lax.ppermute(wide, ("gy", "gz"), [(i, 3 - i) for i in range(4)])
     planes = p.xe + nx
 
-    def emit(weighted, sums, o_own, o_low, o_high):
-        extra = sums.reshape(2, 8, 128)
-        o_own[...] = weighted
-        o_low[:REACH] = weighted[:REACH]
-        o_low[REACH:] = extra
-        o_high[:REACH] = weighted[nx - REACH :]
-        o_high[REACH:] = extra
-
     def first_body(where_ref, own, y, z, yz, *refs):
-        weight_refs, outs, tile, scratch = refs[:8], refs[8:12], refs[12], refs[13:]
+        weight_refs, outs, tile, scratch = refs[:6], refs[6:11], refs[11], refs[12:]
         second = where_ref[0] == 1
         shift = jnp.where(second, nz - half + p.zh, p.zh)
         lane = iota((planes, p.yw, lanes), 2)
@@ -522,29 +509,36 @@
         cur = tile[: p.xe]
         ext = pltpu.roll(tile[p.xe :], lanes - p.zh, 2)
         _, weighted, sums = update_kernel(p, cur, ext, weight_refs, scratch)
-        emit(weighted, sums, *outs[:3])
-        outs[3][...] = ext
-
-    message = f32(REACH + 2, p.yw, lanes)
-    own, low, high, ext = kernel_call(
+        o_own, o_low, o_high, o_ext, o_sums = outs
+        o_own[...] = weighted
+        o_low[:REACH] = weighted[:REACH]
+        o_low[REACH] = sums
+        o_high[:REACH] = weighted[nx - REACH :]
+        o_high[REACH] = sums
+        o_ext[...] = ext
+        o_sums[...] = sums
+
+    message = f32(REACH + 1, p.yw, lanes)
+    own, low, high, ext, sums = kernel_call(
+        p,
         "update_one",
         first_body,
-        (f32(nx, p.yw, lanes), message, message, f32(nx, p.yw, lanes)),
+        (f32(nx, p.yw, lanes), message, message, f32(nx, p.yw, lanes), f32(8, 128)),
         1,
-        12,
+        10,
         [pltpu.VMEM((planes, p.yw, lanes), F32)] + update_scratch(p),
         update_cost(p),
     )(where, wide, from_y, from_z, from_yz, *weights)
 
     left = along_x(high, 1)
     right = along_x(low, -1)
-    far = along_x(low[REACH:], 2)
+    far = along_x(sums, 2)
 
     packs = up(p.xe, 8) // 8
 
-    def join_body(own_ref, low_ref, left_ref, right_ref, far_ref, o_tile, o_down, o_up, o_sums):
+    def join_body(own_ref, sums_ref, left_ref, right_ref, far_ref, o_tile, o_down, o_up, o_sums):
         tile = jnp.concatenate([left_ref[:REACH], own_ref[...], right_ref[:REACH]], axis=0)
-        sums = low_ref[REACH:] + left_ref[REACH:] + right_ref[REACH:] + far_ref[...]
+        sums = sums_ref[...] + left_ref[REACH] + right_ref[REACH] + far_ref[...]
         o_tile[...] = tile
         o_sums[...] = sums
         lane = lax.div(iota((p.yw, lanes), 1), p.zh)
@@ -555,26 +549,27 @@
                     moved = pltpu.roll(tile[8 * pack + k], (k * p.zh - start) % lanes, 1)
                     joined = jnp.where(lane == k, moved, joined)
                 ref[pack] = joined
-            ref[packs:] = sums
-
-    edge = f32(packs + 2, p.yw, lanes)
+            ref[packs] = sums
+
+    edge = f32(packs + 1, p.yw, lanes)
     tile, down, upper, sums = kernel_call(
+        p,
         "join",
         join_body,
-        (f32(p.xe, p.yw, lanes), edge, edge, f32(2, 8, 128)),
+        (f32(p.xe, p.yw, lanes), edge, edge, f32(8, 128)),
         0,
         5,
-    )(own, low, left, right, far)
+    )(own, sums, left, right, far)
     below = along_z(upper, 1)
     above = along_z(down, -1)
     across = lax.ppermute(sums, "gz", [(0, 1), (1, 0)])
 
     def second_body(where_ref, tile_ref, below_ref, above_ref, sums_ref, across_ref, ext_ref, *refs):
-        weight_refs, outs, cur, scratch = refs[:8], refs[8:12], refs[12], refs[13:]
+        weight_refs, outs, cur, scratch = refs[:6], refs[6:10], refs[10], refs[11:]
         o_keep, o_send, o_sums, o_totals = outs
-        totals = sums_ref[...] + across_ref[...] + below_ref[packs:] + above_ref[packs:]
+        totals = sums_ref[...] + across_ref[...] + below_ref[packs] + above_ref[packs]
         o_totals[...] = totals
-        scale = totals[0, 1:2, :] / totals[0, 0:1, :]
+        scale = pick(totals, 1) / pick(totals, 0)
         lane = iota((p.yw, lanes), 1)
         for x in range(p.xe):
             pack, k = divmod(x, 8)
@@ -584,7 +579,7 @@
             joined = jnp.where(lane < p.zh, lower, jnp.where(lane < p.zh + half, middle, top))
             cur[x] = joined * scale
         pot, weighted, sums_here = update_kernel(p, cur[...], ext_ref[...], weight_refs, scratch)
-        o_sums[...] = sums_here
+        o_sums[...] = jnp.broadcast_to(sums_here, (16, 8, 128))
         both = jnp.where(
             iota(pot.shape, 2) < half, pot, pltpu.roll(weighted, half, 2)
         )
@@ -595,50 +590,49 @@
 
     share = f32(nx, ny, lanes)
     keep, send, sums, totals = kernel_call(
+        p,
         "update_two",
         second_body,
-        (share, share, f32(SUMS, 128), f32(2, 8, 128)),
+        (share, share, f32(16, 8, 128), f32(8, 128)),
         1,
-        14,
+        12,
         [pltpu.VMEM((p.xe, p.yw, lanes), F32)] + update_scratch(p),
         update_cost(p),
     )(where, tile, below, above, sums, across, ext, *weights)
 
     other = lax.ppermute(send, "gy", [(0, 1), (1, 0)])
-    gathered = lax.all_to_all(
-        jnp.broadcast_to(sums[None], (16, SUMS, 128)), axes, 0, 0, tiled=True
-    )
+    gathered = lax.all_to_all(sums, axes, 0, 0, tiled=True)
 
     def last_body(where_ref, keep_ref, other_ref, all_ref, totals_ref, o_new, o_pot, o_chem, o_stress):
-        first = totals_ref[...].reshape(SUMS, 128)
+        first = totals_ref[...]
         last = jnp.sum(all_ref[...], axis=0)
-        mass = first[1:2]
-        scale = mass / last[0:1]
+        mass = pick(first, 1)
+        scale = mass / pick(last, 0)
         second = where_ref[0] == 1
         mine, theirs = keep_ref[...], other_ref[...]
         lower = jnp.where(second, theirs, mine)
         top = jnp.where(second, mine, theirs)
         lane = iota((nx, ny, nz), 2)
         o_pot[...] = jnp.where(lane < half, lower, pltpu.roll(top, half, 2))
-        o_new[...] = jnp.where(lane < half, pltpu.roll(lower, half, 2), top) * scale
-        row, column = iota((8, 128), 0), iota((8, 128), 1)
+        o_new[...] = jnp.where(lane < half, pltpu.roll(lower, half, 2), top) * scale[:ny]
+        lane = iota((8, 128), 1)
         for step, total in enumerate((first, last)):
-            o_chem[step : step + 1] = jnp.log(mass / total[0:1]) * (1.0 / TAU)
-            stress = jnp.where(row == column, total[2:3], 0.0)
+            chem = jnp.log(mass / pick(total, 0)) * (1.0 / TAU)
+            o_chem[step] = chem[0, 0]
             for a in range(3):
-                for b in range(3):
-                    k = 3 + 3 * a + b
-                    stress = stress + jnp.where((row == a) & (column == b), total[k : k + 1], 0.0)
-            o_stress[step] = stress[:3, :3] * (1.0 / cells)
+                moments = pltpu.roll(total, 128 - 3 - 3 * a, 1)
+                row = moments + jnp.where(lane == a, pick(total, 2), 0.0)
+                o_stress[a, step : step + 1] = row[:1, :3] * (1.0 / cells)
 
     new, potential, chem, stress = kernel_call(
+        p,
         "finish",
         last_body,
-        (f32(nx, ny, nz), f32(nx, ny, nz), f32(STEPS, 128), f32(STEPS, 3, 3)),
+        (f32(nx, ny, nz), f32(nx, ny, nz), f32(STEPS), f32(3, STEPS, 3)),
         1,
         4,
     )(where, keep, other, gathered, totals)
-    return new, potential, chem[:, 0], stress
+    return new, potential, chem, jnp.transpose(stress, (1, 0, 2))
 
 
 def on_device(density, external, w_first, w_second, w_third, w_last):

time: 78.2 us -> 59.1 us (0.76)
  Pallas kernels: 31.1 us -> 19 us
  local copies, waits for them, and re-layouts: 12.8 us -> 5.51 us
    pallas_call x5, Pallas kernels: 31.1 us -> 19 us  [the longest x1 8.59 us: split_pairs(): kernel_call(p, 'update_two', second_body, (share, share, f32(16, 8, 128),...]
    unnamed x30 -> x11, local copies, waits for them, and re-layouts: 8 us -> 4 us
    slice x2 -> x0, local copies, waits for them, and re-layouts: 1.97 us -> none  [the longest x1 1.24 us: split_pairs(): return (new, potential, chem[:, 0], stress)]
    ppermute x5, waiting for transfers between devices: 4.56 us -> 6.29 us  [along_x(): lax.ppermute(cells_out, 'gx', [(i, (i + step) % 4) for i in range(4)])]
    ppermute x1, starting transfers between devices: 0.01 us -> 1.72 us  [split_pairs(): from_z = lax.ppermute(wide, 'gz', [(0, 1), (1, 0)])]
    broadcast_in_dim x1 -> x0, local copies, waits for them, and re-layouts: 1.36 us -> none  [split_pairs(): jnp.broadcast_to(sums[None], (16, SUMS, 128))]
    ppermute x1, starting transfers between devices: 1.71 us -> 0.42 us  [split_pairs(): from_y = lax.ppermute(wide, 'gy', [(0, 1), (1, 0)])]
    all_to_all x1, waiting for transfers between devices: 3.87 us -> 3.04 us  [split_pairs(): gathered = lax.all_to_all(sums, axes, 0, 0, tiled=True)]
  transfers between devices with their start and end apart: 13 -> 13, of which waited for: 6 -> 7; matrix products, arithmetic and copies ran while one was open for 6% -> 1% of each run, Pallas kernels for 8% -> 3%
where the time goes in v2:
time: 59.1 us; the launch traced here: 58.4 us
  Pallas kernels  19 us (32%)
  starting transfers between devices  18.3 us (31%)
  waiting for transfers between devices  14.7 us (25%)
  local copies, waits for them, and re-layouts  5.51 us (9%)
  between operations  0.86 us (1%)
    ppermute x5, starting transfers between devices, along_x(): lax.ppermute(cells_out, 'gx', [(i, (i + step) % 4) for i in range(4)])  8.88 us
    pallas_call x1, Pallas kernels, split_pairs(): kernel_call(p, 'update_two', second_body, (share, share, f32(16, 8, 128),...  8.59 us
    pallas_call x1, Pallas kernels, split_pairs(): kernel_call(p, 'update_one', first_body, (f32(nx, p.yw, lanes), message,...  7.97 us
    ppermute x5, waiting for transfers between devices, along_x(): lax.ppermute(cells_out, 'gx', [(i, (i + step) % 4) for i in range(4)])  6.29 us
    unnamed x11, local copies, waits for them, and re-layouts  4 us
    all_to_all x1, starting transfers between devices, split_pairs(): gathered = lax.all_to_all(sums, axes, 0, 0, tiled=True)  3.49 us
    all_to_all x1, waiting for transfers between devices, split_pairs(): gathered = lax.all_to_all(sums, axes, 0, 0, tiled=True)  3.04 us
    ppermute x2, waiting for transfers between devices, along_z(): return lax.ppermute(cells_out, ('gy', 'gz'), pairs)  2.42 us
  transfers between devices with their start and end apart: 13, of which 7 were waited for; matrix products, arithmetic and copies ran while one was open for 1% of the time, Pallas kernels for 3%

profile of v2, /device:TPU:0, one launch (start us, length us, event | category | flops | bytes accessed | tf_op | source)
XLA Modules:
  0.0 58.4 jit_solution(1006141796350712234)
XLA Ops:
  0.6 0.8 %fusion = (f32[6,4,128]{2,1,0:T(4,128)S(1)}, f32[6,4,128]{2,1,0:T(4,128)S(1)}) fusion(f32[8,4,128]{2,1,0:T(4,128)} %param.6), kind=kLoop, calls=%fused_computation.4 | loop fusion | bytes 49152 | tf_op jit(solution)/shard_map/slice | solution.py:482
  1.4 3.0 %collective-permute-start = (f32[6,4,128]{2,1,0:T(4,128)S(1)}, f32[6,4,128]{2,1,0:T(4,128)S(1)}, u32[]{:S(2)}, u32[]{:S(2)}) collective-permute-start(f32[6,4,128]{2,1,0:T(4,128)S(1)} %get-tuple-element.51), channel_id=1, source_target_pairs={{0,4},{4,8},{8,12},{12,0},{1,5},{5,9},{9,13},{13,1},{2,6},{6,10},{... | collective-permute-start | bytes 36872 | tf_op jit(solution)/shard_map/ppermute | solution.py:467
  4.4 2.0 %collective-permute-start.1 = (f32[6,4,128]{2,1,0:T(4,128)S(1)}, f32[6,4,128]{2,1,0:T(4,128)S(1)}, u32[]{:S(2)}, u32[]{:S(2)}) collective-permute-start(f32[6,4,128]{2,1,0:T(4,128)S(1)} %get-tuple-element.50), channel_id=1, source_target_pairs={{0,12},{4,0},{8,4},{12,8},{1,13},{5,1},{9,5},{13,9},{2,14},{6,2},{... | collective-permute-start | bytes 36872 | tf_op jit(solution)/shard_map/ppermute | solution.py:467
  6.5 1.8 %collective-permute-done = f32[6,4,128]{2,1,0:T(4,128)S(1)} collective-permute-done((f32[6,4,128]{2,1,0:T(4,128)S(1)}, f32[6,4,128]{2,1,0:T(4,128)S(1)}, u32[]{:S(2)}, u32[]{:S(2)}) %collective-permute-start) | collective-permute-done | bytes 12320 | tf_op jit(solution)/shard_map/ppermute | solution.py:467
  8.2 0.7 %constant_dynamic-update-slice_fusion.2 = f32[28,4,128]{2,1,0:T(4,128)S(1)} fusion(f32[28,4,128]{2,1,0:T(4,128)S(1)} %constant_dynamic-update-slice_fusion.3, f32[8,4,128]{2,1,0:T(4,128)} %param.6), kind=kLoop, calls=%fused_computation.2 | loop fusion | bytes 32768
  9.0 0.0 collective-permute-done.1
  9.0 0.7 %constant_dynamic-update-slice_fusion.own = f32[28,4,128]{2,1,0:T(4,128)S(1)} fusion(f32[28,4,128]{2,1,0:T(4,128)S(1)} %constant_dynamic-update-slice_fusion.1, f32[8,4,128]{2,1,0:T(4,128)} %param.7), kind=kLoop, calls=%fused_computation | loop fusion | bytes 32768 | tf_op jit(solution)/shard_map/concatenate | solution.py:478
  9.7 0.0 collective-permute-start.4
  9.7 1.7 %collective-permute-start.3 = (f32[28,4,128]{2,1,0:T(4,128)S(1)}, f32[28,4,128]{2,1,0:T(4,128)S(1)}, u32[]{:S(2)}, u32[]{:S(2)}) collective-permute-start(f32[28,4,128]{2,1,0:T(4,128)S(1)} %constant_dynamic-update-slice_fusion.own), channel_id=1, source_target_pairs={{0,1},{1,0},{2,3},{3,2},{4,5},{5,4},{6,7},{7,6},{8,9},{9,8},{10,11... | collective-permute-start | bytes 172040 | tf_op jit(solution)/shard_map/ppermute | solution.py:488
  11.4 0.4 collective-permute-start.2
  11.9 0.0 copy-start
  11.9 0.9 %copy-done = bf16[27,32,32]{2,1,0:T(8,128)(2,1)S(1)} copy-done((bf16[27,32,32]{2,1,0:T(8,128)(2,1)S(1)}, bf16[27,32,32]{2,1,0:T(8,128)(2,1)}, u32[]{:S(2)}) %copy-start) | copy-done | bytes 55320
  12.8 0.0 copy-start.1
  12.8 0.9 %copy-done.1 = bf16[27,32,32]{2,1,0:T(8,128)(2,1)S(1)} copy-done((bf16[27,32,32]{2,1,0:T(8,128)(2,1)S(1)}, bf16[27,32,32]{2,1,0:T(8,128)(2,1)}, u32[]{:S(2)}) %copy-start.1) | copy-done | bytes 55320
  13.7 0.0 copy-start.2
  13.7 0.7 %copy-done.2 = bf16[27,32]{1,0:T(8,128)(2,1)S(1)} copy-done((bf16[27,32]{1,0:T(8,128)(2,1)S(1)}, bf16[27,32]{1,0:T(8,128)(2,1)}, u32[]{:S(2)}) %copy-start.2) | copy-done | bytes 1752
  14.4 0.0 copy-start.3
  14.4 0.7 %copy-done.3 = bf16[27,32]{1,0:T(8,128)(2,1)S(1)} copy-done((bf16[27,32]{1,0:T(8,128)(2,1)S(1)}, bf16[27,32]{1,0:T(8,128)(2,1)}, u32[]{:S(2)}) %copy-start.3) | copy-done | bytes 1752
  15.1 1.6 %spread_weights.1 = (bf16[9,256,256]{2,1,0:T(8,128)(2,1)S(1)}, bf16[9,256,256]{2,1,0:T(8,128)(2,1)S(1)}, bf16[144,256]{1,0:T(8,128)(2,1)S(1)}, bf16[144,256]{1,0...) custom-call(bf16[27,32,32]{2,1,0:T(8,128)(2,1)S(1)} %copy-done, ...), custom_call_target="tpu_custom_call" | custom-call | flops 226492416 | bytes 3145728 | tf_op jit(solution)/shard_map/spread_weights/pallas_call | solution.py:137
  16.7 0.0 collective-permute-done.4.yz
  16.7 0.0 collective-permute-done.3.z
  16.7 0.0 collective-permute-done.2.y
  16.7 8.0 %update_one.1 = (f32[8,8,128]{2,1,0:T(8,128)S(1)}, f32[7,8,128]{2,1,0:T(8,128)S(1)}, f32[7,8,128]{2,1,0:T(8,128)S(1)}, f32[8,8,128]{2,1,0:T(8,128)S(1)}, f32[8,128]{1,0:T(8,128)S(1)}) custom-call(s32[1]{0:T(128)} %bitcast.where_ref, f32[28,4,128]{2,1,0:T(4,128)S(1)} %constant_dynamic-update-slice_fusion.own, f32[28,4,128]{2,1,0:T(4,128)S(1)} %collective-permute-done.2.y, ...), custom_call_target="tpu_custom_call" | custom-call | flops 4907335680 | bytes 6291456 | tf_op jit(solution)/shard_map/update_one/pallas_call | solution.py:522
  24.7 0.7 %collective-permute-start.5 = (f32[7,8,128]{2,1,0:T(8,128)S(1)}, f32[7,8,128]{2,1,0:T(8,128)S(1)}, u32[]{:S(2)}, u32[]{:S(2)}) collective-permute-start(f32[7,8,128]{2,1,0:T(8,128)S(1)} %get-tuple-element.35), channel_id=1, source_target_pairs={{0,4},{4,8},{8,12},{12,0},{1,5},{5,9},{9,13},{13,1},{2,6},{6,10},{... | collective-permute-start | bytes 86024 | tf_op jit(solution)/shard_map/ppermute | solution.py:467
  25.4 3.1 %collective-permute-start.6 = (f32[7,8,128]{2,1,0:T(8,128)S(1)}, f32[7,8,128]{2,1,0:T(8,128)S(1)}, u32[]{:S(2)}, u32[]{:S(2)}) collective-permute-start(f32[7,8,128]{2,1,0:T(8,128)S(1)} %get-tuple-element.36), channel_id=1, source_target_pairs={{0,12},{4,0},{8,4},{12,8},{1,13},{5,1},{9,5},{13,9},{2,14},{6,2},{... | collective-permute-start | bytes 86024 | tf_op jit(solution)/shard_map/ppermute | solution.py:467
  28.5 0.0 collective-permute-start.7
  28.5 4.5 %collective-permute-done.7.far_ref = f32[8,128]{1,0:T(8,128)S(1)} collective-permute-done((f32[8,128]{1,0:T(8,128)S(1)}, f32[8,128]{1,0:T(8,128)S(1)}, u32[]{:S(2)}, u32[]{:S(2)}) %collective-permute-start.7) | collective-permute-done | bytes 4128 | tf_op jit(solution)/shard_map/ppermute | solution.py:467
  33.0 0.0 collective-permute-done.5.left_ref
  33.0 0.0 collective-permute-done.6.right_ref
  33.0 0.1 join.1
  33.2 1.7 %collective-permute-start.8 = (f32[4,8,128]{2,1,0:T(8,128)S(1)}, f32[4,8,128]{2,1,0:T(8,128)S(1)}, u32[]{:S(2)}, u32[]{:S(2)}) collective-permute-start(f32[4,8,128]{2,1,0:T(8,128)S(1)} %get-tuple-element.38), channel_id=1, source_target_pairs={{0,2},{2,1},{1,3},{3,0},{4,6},{6,5},{5,7},{7,4},{8,10},{10,9},{9,1... | collective-permute-start | bytes 49160 | tf_op jit(solution)/shard_map/ppermute | solution.py:474
  34.8 0.1 collective-permute-start.9
  35.0 0.2 collective-permute-start.10
  35.2 1.0 %collective-permute-done.10.across_ref = f32[8,128]{1,0:T(8,128)S(1)} collective-permute-done((f32[8,128]{1,0:T(8,128)S(1)}, f32[8,128]{1,0:T(8,128)S(1)}, u32[]{:S(2)}, u32[]{:S(2)}) %collective-permute-start.10) | collective-permute-done | bytes 4128 | tf_op jit(solution)/shard_map/ppermute | solution.py:565
  36.1 0.3 collective-permute-done.8.below_ref
  36.4 2.2 %collective-permute-done.9.above_ref = f32[4,8,128]{2,1,0:T(8,128)S(1)} collective-permute-done((f32[4,8,128]{2,1,0:T(8,128)S(1)}, f32[4,8,128]{2,1,0:T(8,128)S(1)}, u32[]{:S(2)}, u32[]{:S(2)}) %collective-permute-start.9) | collective-permute-done | bytes 16416 | tf_op jit(solution)/shard_map/ppermute | solution.py:474
  38.5 8.6 %update_two.1 = (f32[8,4,128]{2,1,0:T(4,128)S(1)}, f32[8,4,128]{2,1,0:T(4,128)S(1)}, f32[16,8,128]{2,1,0:T(8,128)}, f32[8,128]{1,0:T(8,128)S(1)}) custom-call(s32[1]{0:T(128)} %bitcast.where_ref, f32[20,8,128]{2,1,0:T(8,128)S(1)} %get-tuple-element.37.tile_ref, f32[4,8,128]{2,1,0:T(8,128)S(1)} %collective-permute-done.8.below_ref, ...), custom_call_target="tpu_custom_call" | custom-call | flops 4907335680 | bytes 6291456 | tf_op jit(solution)/shard_map/update_two/pallas_call | solution.py:592
  47.1 3.5 %all-to-all-start = ((f32[16,8,128]{2,1,0:T(8,128)}), f32[16,8,128]{2,1,0:T(8,128)S(1)}, u32[]{:S(2)}, u32[]{:S(2)}) async-start(f32[16,8,128]{2,1,0:T(8,128)} %get-tuple-element.44), calls=%async_computation | async-start | bytes 131072 | tf_op jit(solution)/shard_map/all_to_all | solution.py:604
  50.6 1.8 %collective-permute-start.11 = (f32[8,4,128]{2,1,0:T(4,128)S(1)}, f32[8,4,128]{2,1,0:T(4,128)S(1)}, u32[]{:S(2)}, u32[]{:S(2)}) collective-permute-start(f32[8,4,128]{2,1,0:T(4,128)S(1)} %get-tuple-element.43), channel_id=1, source_target_pairs={{0,2},{2,0},{1,3},{3,1},{4,6},{6,4},{5,7},{7,5},{8,10},{10,8},{9,1... | collective-permute-start | bytes 49160 | tf_op jit(solution)/shard_map/ppermute | solution.py:603
  52.4 2.0 %collective-permute-done.11.other_ref = f32[8,4,128]{2,1,0:T(4,128)S(1)} collective-permute-done((f32[8,4,128]{2,1,0:T(4,128)S(1)}, f32[8,4,128]{2,1,0:T(4,128)S(1)}, u32[]{:S(2)}, u32[]{:S(2)}) %collective-permute-start.11) | collective-permute-done | bytes 16416 | tf_op jit(solution)/shard_map/ppermute | solution.py:603
  54.5 3.0 %all-to-all-done.all_ref = f32[16,8,128]{2,1,0:T(8,128)S(1)} async-done(((f32[16,8,128]{2,1,0:T(8,128)}), f32[16,8,128]{2,1,0:T(8,128)S(1)}, u32[]{:S(2)}, u32[]{:S(2)}) %all-to-all-start) | async-done | bytes 65568 | tf_op jit(solution)/shard_map/all_to_all | solution.py:604
  57.5 0.8 %finish.1 = (f32[8,4,128]{2,1,0:T(4,128)}, f32[8,4,128]{2,1,0:T(4,128)}, f32[2]{0:T(128)}, f32[3,2,3]{2,1,0:T(2,128)}) custom-call(s32[1]{0:T(128)} %bitcast.where_ref, f32[8,4,128]{2,1,0:T(4,128)S(1)} %get-tuple-element.42.keep_ref, f32[8,4,128]{2,1,0:T(4,128)S(1)} %collective-permute-done.11.other_ref, f32[16,8,128]{2,1,0:T(8,128)S(1)} %all-to-all-done.all_ref, ...), custom_call_target="tpu_custom_call" | custom-call | tf_op jit(solution)/shard_map/finish/pallas_call | solution.py:627
  (2 shorter events, 0.0 us)
Async XLA Ops:
  1.4 6.8 %collective-permute-start = (f32[6,4,128]{2,1,0:T(4,128)S(1)}, f32[6,4,128]{2,1,0:T(4,128)S(1)}, u32[]{:S(2)}, u32[]{:S(2)}) collective-permute-start(f32[6,4,128]{2,1,0:T(4,128)S(1)} %get-tuple-element.51), channel_id=1, source_target_pairs={{0,4},{4,8},{8,12},{12,0},{1,5},{5,9},{9,13},{13,1},{2,6},{6,10},{... | collective-permute-start | bytes 36872 | tf_op jit(solution)/shard_map/ppermute | solution.py:467
  4.4 4.5 %collective-permute-start.1 = (f32[6,4,128]{2,1,0:T(4,128)S(1)}, f32[6,4,128]{2,1,0:T(4,128)S(1)}, u32[]{:S(2)}, u32[]{:S(2)}) collective-permute-start(f32[6,4,128]{2,1,0:T(4,128)S(1)} %get-tuple-element.50), channel_id=1, source_target_pairs={{0,12},{4,0},{8,4},{12,8},{1,13},{5,1},{9,5},{13,9},{2,14},{6,2},{... | collective-permute-start | bytes 36872 | tf_op jit(solution)/shard_map/ppermute | solution.py:467
  9.7 7.0 %collective-permute-start.4 = (f32[28,4,128]{2,1,0:T(4,128)S(1)}, f32[28,4,128]{2,1,0:T(4,128)S(1)}, u32[]{:S(2)}, u32[]{:S(2)}) collective-permute-start(f32[28,4,128]{2,1,0:T(4,128)S(1)} %constant_dynamic-update-slice_fusion.own), channel_id=1, source_target_pairs={{0,3},{1,2},{2,1},{3,0},{4,7},{5,6},{6,5},{7,4},{8,11},{9,10},{10,... | collective-permute-start | bytes 172040 | tf_op jit(solution)/shard_map/ppermute | solution.py:489
  9.7 7.0 %collective-permute-start.3 = (f32[28,4,128]{2,1,0:T(4,128)S(1)}, f32[28,4,128]{2,1,0:T(4,128)S(1)}, u32[]{:S(2)}, u32[]{:S(2)}) collective-permute-start(f32[28,4,128]{2,1,0:T(4,128)S(1)} %constant_dynamic-update-slice_fusion.own), channel_id=1, source_target_pairs={{0,1},{1,0},{2,3},{3,2},{4,5},{5,4},{6,7},{7,6},{8,9},{9,8},{10,11... | collective-permute-start | bytes 172040 | tf_op jit(solution)/shard_map/ppermute | solution.py:488
  11.4 5.3 %collective-permute-start.2 = (f32[28,4,128]{2,1,0:T(4,128)S(1)}, f32[28,4,128]{2,1,0:T(4,128)S(1)}, u32[]{:S(2)}, u32[]{:S(2)}) collective-permute-start(f32[28,4,128]{2,1,0:T(4,128)S(1)} %constant_dynamic-update-slice_fusion.own), channel_id=1, source_target_pairs={{0,2},{2,0},{1,3},{3,1},{4,6},{6,4},{5,7},{7,5},{8,10},{10,8},{9,1... | collective-permute-start | bytes 172040 | tf_op jit(solution)/shard_map/ppermute | solution.py:487
  11.9 0.9 %copy-start = (bf16[27,32,32]{2,1,0:T(8,128)(2,1)S(1)}, bf16[27,32,32]{2,1,0:T(8,128)(2,1)}, u32[]{:S(2)}) copy-start(bf16[27,32,32]{2,1,0:T(8,128)(2,1)} %second.1) | copy-start | bytes 165892
  12.8 0.9 %copy-start.1 = (bf16[27,32,32]{2,1,0:T(8,128)(2,1)S(1)}, bf16[27,32,32]{2,1,0:T(8,128)(2,1)}, u32[]{:S(2)}) copy-start(bf16[27,32,32]{2,1,0:T(8,128)(2,1)} %third.1) | copy-start | bytes 165892
  13.7 0.7 %copy-start.2 = (bf16[27,32]{1,0:T(8,128)(2,1)S(1)}, bf16[27,32]{1,0:T(8,128)(2,1)}, u32[]{:S(2)}) copy-start(bf16[27,32]{1,0:T(8,128)(2,1)} %first.1) | copy-start | bytes 5188
  14.4 0.7 %copy-start.3 = (bf16[27,32]{1,0:T(8,128)(2,1)S(1)}, bf16[27,32]{1,0:T(8,128)(2,1)}, u32[]{:S(2)}) copy-start(bf16[27,32]{1,0:T(8,128)(2,1)} %last.1) | copy-start | bytes 5188
  24.7 8.3 %collective-permute-start.5 = (f32[7,8,128]{2,1,0:T(8,128)S(1)}, f32[7,8,128]{2,1,0:T(8,128)S(1)}, u32[]{:S(2)}, u32[]{:S(2)}) collective-permute-start(f32[7,8,128]{2,1,0:T(8,128)S(1)} %get-tuple-element.35), channel_id=1, source_target_pairs={{0,4},{4,8},{8,12},{12,0},{1,5},{5,9},{9,13},{13,1},{2,6},{6,10},{... | collective-permute-start | bytes 86024 | tf_op jit(solution)/shard_map/ppermute | solution.py:467
  25.4 7.6 %collective-permute-start.6 = (f32[7,8,128]{2,1,0:T(8,128)S(1)}, f32[7,8,128]{2,1,0:T(8,128)S(1)}, u32[]{:S(2)}, u32[]{:S(2)}) collective-permute-start(f32[7,8,128]{2,1,0:T(8,128)S(1)} %get-tuple-element.36), channel_id=1, source_target_pairs={{0,12},{4,0},{8,4},{12,8},{1,13},{5,1},{9,5},{13,9},{2,14},{6,2},{... | collective-permute-start | bytes 86024 | tf_op jit(solution)/shard_map/ppermute | solution.py:467
  28.5 4.5 %collective-permute-start.7 = (f32[8,128]{1,0:T(8,128)S(1)}, f32[8,128]{1,0:T(8,128)S(1)}, u32[]{:S(2)}, u32[]{:S(2)}) collective-permute-start(f32[8,128]{1,0:T(8,128)S(1)} %get-tuple-element.34.sums_ref), channel_id=1, source_target_pairs={{0,8},{4,12},{8,0},{12,4},{1,9},{5,13},{9,1},{13,5},{2,10},{6,14},... | collective-permute-start | bytes 12296 | tf_op jit(solution)/shard_map/ppermute | solution.py:467
  33.2 3.2 %collective-permute-start.8 = (f32[4,8,128]{2,1,0:T(8,128)S(1)}, f32[4,8,128]{2,1,0:T(8,128)S(1)}, u32[]{:S(2)}, u32[]{:S(2)}) collective-permute-start(f32[4,8,128]{2,1,0:T(8,128)S(1)} %get-tuple-element.38), channel_id=1, source_target_pairs={{0,2},{2,1},{1,3},{3,0},{4,6},{6,5},{5,7},{7,4},{8,10},{10,9},{9,1... | collective-permute-start | bytes 49160 | tf_op jit(solution)/shard_map/ppermute | solution.py:474
  34.8 3.7 %collective-permute-start.9 = (f32[4,8,128]{2,1,0:T(8,128)S(1)}, f32[4,8,128]{2,1,0:T(8,128)S(1)}, u32[]{:S(2)}, u32[]{:S(2)}) collective-permute-start(f32[4,8,128]{2,1,0:T(8,128)S(1)} %get-tuple-element.39), channel_id=1, source_target_pairs={{0,3},{2,0},{1,2},{3,1},{4,7},{6,4},{5,6},{7,5},{8,11},{10,8},{9,1... | collective-permute-start | bytes 49160 | tf_op jit(solution)/shard_map/ppermute | solution.py:474
  35.0 1.2 %collective-permute-start.10 = (f32[8,128]{1,0:T(8,128)S(1)}, f32[8,128]{1,0:T(8,128)S(1)}, u32[]{:S(2)}, u32[]{:S(2)}) collective-permute-start(f32[8,128]{1,0:T(8,128)S(1)} %get-tuple-element.40.sums_ref), channel_id=1, source_target_pairs={{0,1},{1,0},{2,3},{3,2},{4,5},{5,4},{6,7},{7,6},{8,9},{9,8},{10,11... | collective-permute-start | bytes 12296 | tf_op jit(solution)/shard_map/ppermute | solution.py:565
  47.1 10.4 %all-to-all-start = ((f32[16,8,128]{2,1,0:T(8,128)}), f32[16,8,128]{2,1,0:T(8,128)S(1)}, u32[]{:S(2)}, u32[]{:S(2)}) async-start(f32[16,8,128]{2,1,0:T(8,128)} %get-tuple-element.44), calls=%async_computation | async-start | bytes 131072 | tf_op jit(solution)/shard_map/all_to_all | solution.py:604
  50.6 3.8 %collective-permute-start.11 = (f32[8,4,128]{2,1,0:T(4,128)S(1)}, f32[8,4,128]{2,1,0:T(4,128)S(1)}, u32[]{:S(2)}, u32[]{:S(2)}) collective-permute-start(f32[8,4,128]{2,1,0:T(4,128)S(1)} %get-tuple-element.43), channel_id=1, source_target_pairs={{0,2},{2,0},{1,3},{3,1},{4,6},{6,4},{5,7},{7,5},{8,10},{10,8},{9,1... | collective-permute-start | bytes 49160 | tf_op jit(solution)/shard_map/ppermute | solution.py:603

commit v3 on v2

--- a/solution.py
+++ b/solution.py
@@ -19,6 +19,7 @@
 F32 = jnp.float32
 VM = pl.BlockSpec(memory_space=pltpu.VMEM)
 SM = pl.BlockSpec(memory_space=pltpu.SMEM)
+HB = pl.BlockSpec(memory_space=pltpu.HBM)
 
 
 def up(number, unit):
@@ -125,10 +126,16 @@
 
 
 def spread_weights(p, w_first, w_second, w_third, w_last):
-    def body(second, third, first, last, o_second, o_third, o_first, o_back, o_last, o_cot):
-        weights_kernel(
-            p, (second, third), (first, last), (o_second, o_third), (o_first, o_back), (o_last, o_cot)
-        )
+    inputs = (w_second, w_third, w_first, w_last)
+
+    def body(*refs):
+        hbm, outs, held, sems = refs[:4], refs[4:10], refs[10:14], refs[14]
+        copies = [pltpu.make_async_copy(hbm[i], held[i], sems.at[i]) for i in range(4)]
+        for copy in copies:
+            copy.start()
+        for copy in copies:
+            copy.wait()
+        weights_kernel(p, held[:2], held[2:], outs[:2], outs[2:4], outs[4:])
 
     dense = jax.ShapeDtypeStruct((9, p.lanes, p.lanes), BF)
     single = jax.ShapeDtypeStruct((18 * p.yw, p.lanes), BF)
@@ -138,11 +145,13 @@
         body,
         name="spread_weights",
         out_shape=(dense,) * 2 + (single,) * 2 + (narrow,) * 2,
-        in_specs=[VM] * 4,
+        in_specs=[HB] * 4,
         out_specs=(VM,) * 6,
+        scratch_shapes=[pltpu.VMEM(a.shape, a.dtype) for a in inputs]
+        + [pltpu.SemaphoreType.DMA((4,))],
         compiler_params=pltpu.CompilerParams(vmem_limit_bytes=p.limit),
         cost_estimate=pl.CostEstimate(flops=flops, bytes_accessed=3 << 20, transcendentals=0),
-    )(w_second, w_third, w_first, w_last)
+    )(*[pltpu.with_memory_space_constraint(a, pltpu.HBM) for a in inputs])
 
 
 def cube_root(value):
@@ -195,10 +204,10 @@
     pieces = []
     for half in range(2):
         for tz in range(3):
-            piece = planes_ref[half, place : place + 3, :, tz * p.zp : (tz + 1) * p.zp]
-            pieces.append(piece.reshape(3 * p.yw, p.zp))
+            piece = planes_ref[half, place : place + 3, :, tz * p.zp : tz * p.zp + p.ze]
+            pieces.append(piece.reshape(3 * p.yw, p.ze))
     window = jnp.concatenate(pieces, axis=0).astype(BF)
-    return dot_tn(window, w_ref[...])[: p.ze]
+    return dot_tn(window, w_ref[...])
 
 
 def narrow_fold(p, ref, w_ref, planes_ref, back):
@@ -358,12 +367,12 @@
     return pl.CostEstimate(flops=flops, bytes_accessed=6 << 20, transcendentals=0)
 
 
-def kernel_call(p, name, body, out_shape, n_smem, n_vmem, scratch=(), cost=None):
+def kernel_call(p, name, body, out_shape, n_smem, n_vmem, scratch=(), cost=None, n_hbm=0):
     return pl.pallas_call(
         body,
         name=name,
         out_shape=out_shape,
-        in_specs=[SM] * n_smem + [VM] * n_vmem,
+        in_specs=[SM] * n_smem + [HB] * n_hbm + [VM] * n_vmem,
         out_specs=tuple(SM if len(shape.shape) == 1 else VM for shape in out_shape),
         scratch_shapes=list(scratch),
         compiler_params=pltpu.CompilerParams(vmem_limit_bytes=p.limit),
@@ -475,14 +484,31 @@
 
     weights = spread_weights(p, w_first, w_second, w_third, w_last)
 
-    wide = jnp.concatenate(
-        [
-            along_x(density[nx - REACH :], 1),
-            density,
-            along_x(density[:REACH], -1),
-            external,
-        ],
-        axis=0,
+    def widen_body(own_hbm, ext_hbm, left_ref, right_ref, o_wide, sems):
+        copies = [
+            pltpu.make_async_copy(own_hbm, o_wide.at[REACH : REACH + nx], sems.at[0]),
+            pltpu.make_async_copy(ext_hbm, o_wide.at[p.xe :], sems.at[1]),
+        ]
+        for copy in copies:
+            copy.start()
+        o_wide[:REACH] = left_ref[nx - REACH :]
+        o_wide[REACH + nx : p.xe] = right_ref[:REACH]
+        for copy in copies:
+            copy.wait()
+
+    (wide,) = kernel_call(
+        p,
+        "widen",
+        widen_body,
+        (f32(p.xe + nx, ny, nz),),
+        0,
+        2,
+        [pltpu.SemaphoreType.DMA((2,))],
+        n_hbm=2,
+    )(
+        *[pltpu.with_memory_space_constraint(a, pltpu.HBM) for a in (density, external)],
+        along_x(density, 1),
+        along_x(density, -1),
     )
     from_y = lax.ppermute(wide, "gy", [(0, 1), (1, 0)])
     from_z = lax.ppermute(wide, "gz", [(0, 1), (1, 0)])

time: 59.1 us -> 55.2 us (0.934)
  local copies, waits for them, and re-layouts: 5.51 us -> 0 us
  Pallas kernels: 19 us -> 20.4 us
  starting transfers between devices: 18.3 us -> 18.9 us
    unnamed x11 -> x0, local copies, waits for them, and re-layouts: 4 us -> none
    ppermute x2, waiting for transfers between devices: 2.42 us -> 1.36 us  [along_z(): return lax.ppermute(cells_out, ('gy', 'gz'), pairs)]
    pallas_call x1, Pallas kernels: 1.57 us -> 2.63 us  [spread_weights(): pl.pallas_call(body, name='spread_weights', out_shape=(dense,) * 2 + (sin...]
    ppermute x1, waiting for transfers between devices: 0.01 us -> 1.04 us  [split_pairs(): from_y = lax.ppermute(wide, 'gy', [(0, 1), (1, 0)])]
    slice x1 -> x0, local copies, waits for them, and re-layouts: 0.79 us -> none  [split_pairs(): density[:REACH]]
    pallas_call x0 -> x1, Pallas kernels: none -> 0.75 us  [split_pairs(): kernel_call(p, 'widen', widen_body, (f32(p.xe + nx, ny, nz),), 0, 2, [plt...]
    concatenate x1 -> x0, local copies, waits for them, and re-layouts: 0.73 us -> none  [split_pairs(): jnp.concatenate([along_x(density[nx - REACH:], 1), density, along_x(densi...]
    ppermute x5, starting transfers between devices: 8.88 us -> 9.56 us  [along_x(): lax.ppermute(cells_out, 'gx', [(i, (i + step) % 4) for i in range(4)])]
  transfers between devices with their start and end apart: 13 -> 13, of which waited for: 7 -> 9; matrix products, arithmetic and copies ran while one was open for 1% -> 0% of each run, Pallas kernels for 3% -> 5%
where the time goes in v3:
time: 55.2 us; the launch traced here: 54.8 us
  Pallas kernels  20.4 us (37%)
  starting transfers between devices  18.9 us (34%)
  waiting for transfers between devices  14.6 us (26%)
  between operations  0.86 us (2%)
    ppermute x5, starting transfers between devices, along_x(): lax.ppermute(cells_out, 'gx', [(i, (i + step) % 4) for i in range(4)])  9.56 us
    pallas_call x1, Pallas kernels, split_pairs(): kernel_call(p, 'update_two', second_body, (share, share, f32(16, 8, 128),...  8.42 us
    pallas_call x1, Pallas kernels, split_pairs(): kernel_call(p, 'update_one', first_body, (f32(nx, p.yw, lanes), message,...  7.79 us
    ppermute x5, waiting for transfers between devices, along_x(): lax.ppermute(cells_out, 'gx', [(i, (i + step) % 4) for i in range(4)])  6.03 us
    all_to_all x1, starting transfers between devices, split_pairs(): gathered = lax.all_to_all(sums, axes, 0, 0, tiled=True)  3.49 us
    all_to_all x1, waiting for transfers between devices, split_pairs(): gathered = lax.all_to_all(sums, axes, 0, 0, tiled=True)  2.99 us
    pallas_call x1, Pallas kernels, spread_weights(): pl.pallas_call(body, name='spread_weights', out_shape=(dense,) * 2 + (sin...  2.63 us
    ppermute x1, waiting for transfers between devices, split_pairs(): other = lax.ppermute(send, 'gy', [(0, 1), (1, 0)])  2.01 us
  transfers between devices with their start and end apart: 13, of which 9 were waited for; matrix products, arithmetic and copies ran while one was open for 0% of the time, Pallas kernels for 5%

profile of v3, /device:TPU:0, one launch (start us, length us, event | category | flops | bytes accessed | tf_op | source)
XLA Modules:
  0.0 54.8 jit_solution(10155015117683923124)
XLA Ops:
  0.6 3.1 %collective-permute-start = (f32[8,4,128]{2,1,0:T(4,128)}, f32[8,4,128]{2,1,0:T(4,128)S(1)}, u32[]{:S(2)}, u32[]{:S(2)}) collective-permute-start(f32[8,4,128]{2,1,0:T(4,128)} %own_hbm.1), channel_id=1, source_target_pairs={{0,4},{4,8},{8,12},{12,0},{1,5},{5,9},{9,13},{13,1},{2,6},{6,10},{... | collective-permute-start | bytes 49160 | tf_op jit(solution)/shard_map/ppermute | solution.py:476
  3.7 2.1 %collective-permute-start.1 = (f32[8,4,128]{2,1,0:T(4,128)}, f32[8,4,128]{2,1,0:T(4,128)S(1)}, u32[]{:S(2)}, u32[]{:S(2)}) collective-permute-start(f32[8,4,128]{2,1,0:T(4,128)} %own_hbm.1), channel_id=1, source_target_pairs={{0,12},{4,0},{8,4},{12,8},{1,13},{5,1},{9,5},{13,9},{2,14},{6,2},{... | collective-permute-start | bytes 49160 | tf_op jit(solution)/shard_map/ppermute | solution.py:476
  5.8 2.0 %collective-permute-done.left_ref = f32[8,4,128]{2,1,0:T(4,128)S(1)} collective-permute-done((f32[8,4,128]{2,1,0:T(4,128)}, f32[8,4,128]{2,1,0:T(4,128)S(1)}, u32[]{:S(2)}, u32[]{:S(2)}) %collective-permute-start) | collective-permute-done | bytes 16416 | tf_op jit(solution)/shard_map/ppermute | solution.py:476
  7.8 0.1 collective-permute-done.1.right_ref
  7.8 0.8 %widen.1.own = f32[28,4,128]{2,1,0:T(4,128)S(1)} custom-call(f32[8,4,128]{2,1,0:T(4,128)} %own_hbm.1, f32[8,4,128]{2,1,0:T(4,128)} %ext_hbm.1, f32[8,4,128]{2,1,0:T(4,128)S(1)} %collective-permute-done.left_ref, f32[8,4,128]{2,1,0:T(4,128)S(1)} %collective-permute-done.1.right_ref), custom_call_target="tpu_custom_call" | custom-call | tf_op jit(solution)/shard_map/widen/pallas_call | solution.py:499
  8.6 0.1 collective-permute-start.4
  8.7 1.6 %collective-permute-start.3 = (f32[28,4,128]{2,1,0:T(4,128)S(1)}, f32[28,4,128]{2,1,0:T(4,128)S(1)}, u32[]{:S(2)}, u32[]{:S(2)}) collective-permute-start(f32[28,4,128]{2,1,0:T(4,128)S(1)} %widen.1.own), channel_id=1, source_target_pairs={{0,1},{1,0},{2,3},{3,2},{4,5},{5,4},{6,7},{7,6},{8,9},{9,8},{10,11... | collective-permute-start | bytes 172040 | tf_op jit(solution)/shard_map/ppermute | solution.py:514
  10.3 0.5 collective-permute-start.2
  10.8 2.6 %spread_weights.1 = (bf16[9,256,256]{2,1,0:T(8,128)(2,1)S(1)}, bf16[9,256,256]{2,1,0:T(8,128)(2,1)S(1)}, bf16[144,256]{1,0:T(8,128)(2,1)S(1)}, bf16[144,256]{1,0...) custom-call(bf16[27,32,32]{2,1,0:T(8,128)(2,1)} %refs_0_.1, ...), custom_call_target="tpu_custom_call" | custom-call | flops 226492416 | bytes 3145728 | tf_op jit(solution)/shard_map/spread_weights/pallas_call | solution.py:144
  13.4 0.0 collective-permute-done.4.yz
  13.4 0.0 collective-permute-done.3.z
  13.5 1.0 %collective-permute-done.2.y = f32[28,4,128]{2,1,0:T(4,128)S(1)} collective-permute-done((f32[28,4,128]{2,1,0:T(4,128)S(1)}, f32[28,4,128]{2,1,0:T(4,128)S(1)}, u32[]{:S(2)}, u32[]{:S(2)}) %collective-permute-start.2) | collective-permute-done | bytes 57376 | tf_op jit(solution)/shard_map/ppermute | solution.py:513
  14.5 7.8 %update_one.1 = (f32[8,8,128]{2,1,0:T(8,128)S(1)}, f32[7,8,128]{2,1,0:T(8,128)S(1)}, f32[7,8,128]{2,1,0:T(8,128)S(1)}, f32[8,8,128]{2,1,0:T(8,128)S(1)}, f32[8,128]{1,0:T(8,128)S(1)}) custom-call(s32[1]{0:T(128)} %bitcast.where_ref, f32[28,4,128]{2,1,0:T(4,128)S(1)} %widen.1.own, f32[28,4,128]{2,1,0:T(4,128)S(1)} %collective-permute-done.2.y, ...), custom_call_target="tpu_custom_call" | custom-call | flops 4907335680 | bytes 6291456 | tf_op jit(solution)/shard_map/update_one/pallas_call | solution.py:548
  22.3 1.3 %collective-permute-start.5 = (f32[7,8,128]{2,1,0:T(8,128)S(1)}, f32[7,8,128]{2,1,0:T(8,128)S(1)}, u32[]{:S(2)}, u32[]{:S(2)}) collective-permute-start(f32[7,8,128]{2,1,0:T(8,128)S(1)} %get-tuple-element.35), channel_id=1, source_target_pairs={{0,4},{4,8},{8,12},{12,0},{1,5},{5,9},{9,13},{13,1},{2,6},{6,10},{... | collective-permute-start | bytes 86024 | tf_op jit(solution)/shard_map/ppermute | solution.py:476
  23.6 2.5 %collective-permute-start.6 = (f32[7,8,128]{2,1,0:T(8,128)S(1)}, f32[7,8,128]{2,1,0:T(8,128)S(1)}, u32[]{:S(2)}, u32[]{:S(2)}) collective-permute-start(f32[7,8,128]{2,1,0:T(8,128)S(1)} %get-tuple-element.36), channel_id=1, source_target_pairs={{0,12},{4,0},{8,4},{12,8},{1,13},{5,1},{9,5},{13,9},{2,14},{6,2},{... | collective-permute-start | bytes 86024 | tf_op jit(solution)/shard_map/ppermute | solution.py:476
  26.2 0.5 collective-permute-start.7
  26.7 4.0 %collective-permute-done.7.far_ref = f32[8,128]{1,0:T(8,128)S(1)} collective-permute-done((f32[8,128]{1,0:T(8,128)S(1)}, f32[8,128]{1,0:T(8,128)S(1)}, u32[]{:S(2)}, u32[]{:S(2)}) %collective-permute-start.7) | collective-permute-done | bytes 4128 | tf_op jit(solution)/shard_map/ppermute | solution.py:476
  30.7 0.0 collective-permute-done.5.left_ref
  30.7 0.0 collective-permute-done.6.right_ref
  30.7 0.1 join.1
  30.8 0.6 %collective-permute-start.8 = (f32[4,8,128]{2,1,0:T(8,128)S(1)}, f32[4,8,128]{2,1,0:T(8,128)S(1)}, u32[]{:S(2)}, u32[]{:S(2)}) collective-permute-start(f32[4,8,128]{2,1,0:T(8,128)S(1)} %get-tuple-element.38), channel_id=1, source_target_pairs={{0,2},{2,1},{1,3},{3,0},{4,6},{6,5},{5,7},{7,4},{8,10},{10,9},{9,1... | collective-permute-start | bytes 49160 | tf_op jit(solution)/shard_map/ppermute | solution.py:483
  31.4 1.2 %collective-permute-start.9 = (f32[4,8,128]{2,1,0:T(8,128)S(1)}, f32[4,8,128]{2,1,0:T(8,128)S(1)}, u32[]{:S(2)}, u32[]{:S(2)}) collective-permute-start(f32[4,8,128]{2,1,0:T(8,128)S(1)} %get-tuple-element.39), channel_id=1, source_target_pairs={{0,3},{2,0},{1,2},{3,1},{4,7},{6,4},{5,6},{7,5},{8,11},{10,8},{9,1... | collective-permute-start | bytes 49160 | tf_op jit(solution)/shard_map/ppermute | solution.py:483
  32.6 0.0 collective-permute-start.10
  32.6 1.2 %collective-permute-done.10.across_ref = f32[8,128]{1,0:T(8,128)S(1)} collective-permute-done((f32[8,128]{1,0:T(8,128)S(1)}, f32[8,128]{1,0:T(8,128)S(1)}, u32[]{:S(2)}, u32[]{:S(2)}) %collective-permute-start.10) | collective-permute-done | bytes 4128 | tf_op jit(solution)/shard_map/ppermute | solution.py:591
  33.7 0.2 collective-permute-done.8.below_ref
  34.0 1.1 %collective-permute-done.9.above_ref = f32[4,8,128]{2,1,0:T(8,128)S(1)} collective-permute-done((f32[4,8,128]{2,1,0:T(8,128)S(1)}, f32[4,8,128]{2,1,0:T(8,128)S(1)}, u32[]{:S(2)}, u32[]{:S(2)}) %collective-permute-start.9) | collective-permute-done | bytes 16416 | tf_op jit(solution)/shard_map/ppermute | solution.py:483
  35.1 8.4 %update_two.1 = (f32[8,4,128]{2,1,0:T(4,128)S(1)}, f32[8,4,128]{2,1,0:T(4,128)S(1)}, f32[16,8,128]{2,1,0:T(8,128)}, f32[8,128]{1,0:T(8,128)S(1)}) custom-call(s32[1]{0:T(128)} %bitcast.where_ref, f32[20,8,128]{2,1,0:T(8,128)S(1)} %get-tuple-element.37.tile_ref, f32[4,8,128]{2,1,0:T(8,128)S(1)} %collective-permute-done.8.below_ref, ...), custom_call_target="tpu_custom_call" | custom-call | flops 4907335680 | bytes 6291456 | tf_op jit(solution)/shard_map/update_two/pallas_call | solution.py:618
  43.5 3.5 %all-to-all-start = ((f32[16,8,128]{2,1,0:T(8,128)}), f32[16,8,128]{2,1,0:T(8,128)S(1)}, u32[]{:S(2)}, u32[]{:S(2)}) async-start(f32[16,8,128]{2,1,0:T(8,128)} %get-tuple-element.44), calls=%async_computation | async-start | bytes 131072 | tf_op jit(solution)/shard_map/all_to_all | solution.py:630
  47.0 1.9 %collective-permute-start.11 = (f32[8,4,128]{2,1,0:T(4,128)S(1)}, f32[8,4,128]{2,1,0:T(4,128)S(1)}, u32[]{:S(2)}, u32[]{:S(2)}) collective-permute-start(f32[8,4,128]{2,1,0:T(4,128)S(1)} %get-tuple-element.43), channel_id=1, source_target_pairs={{0,2},{2,0},{1,3},{3,1},{4,6},{6,4},{5,7},{7,5},{8,10},{10,8},{9,1... | collective-permute-start | bytes 49160 | tf_op jit(solution)/shard_map/ppermute | solution.py:629
  48.9 2.0 %collective-permute-done.11.other_ref = f32[8,4,128]{2,1,0:T(4,128)S(1)} collective-permute-done((f32[8,4,128]{2,1,0:T(4,128)S(1)}, f32[8,4,128]{2,1,0:T(4,128)S(1)}, u32[]{:S(2)}, u32[]{:S(2)}) %collective-permute-start.11) | collective-permute-done | bytes 16416 | tf_op jit(solution)/shard_map/ppermute | solution.py:629
  50.9 3.0 %all-to-all-done.all_ref = f32[16,8,128]{2,1,0:T(8,128)S(1)} async-done(((f32[16,8,128]{2,1,0:T(8,128)}), f32[16,8,128]{2,1,0:T(8,128)S(1)}, u32[]{:S(2)}, u32[]{:S(2)}) %all-to-all-start) | async-done | bytes 65568 | tf_op jit(solution)/shard_map/all_to_all | solution.py:630
  53.9 0.8 %finish.1 = (f32[8,4,128]{2,1,0:T(4,128)}, f32[8,4,128]{2,1,0:T(4,128)}, f32[2]{0:T(128)}, f32[3,2,3]{2,1,0:T(2,128)}) custom-call(s32[1]{0:T(128)} %bitcast.where_ref, f32[8,4,128]{2,1,0:T(4,128)S(1)} %get-tuple-element.42.keep_ref, f32[8,4,128]{2,1,0:T(4,128)S(1)} %collective-permute-done.11.other_ref, f32[16,8,128]{2,1,0:T(8,128)S(1)} %all-to-all-done.all_ref, ...), custom_call_target="tpu_custom_call" | custom-call | tf_op jit(solution)/shard_map/finish/pallas_call | solution.py:653
Async XLA Ops:
  0.6 7.1 %collective-permute-start = (f32[8,4,128]{2,1,0:T(4,128)}, f32[8,4,128]{2,1,0:T(4,128)S(1)}, u32[]{:S(2)}, u32[]{:S(2)}) collective-permute-start(f32[8,4,128]{2,1,0:T(4,128)} %own_hbm.1), channel_id=1, source_target_pairs={{0,4},{4,8},{8,12},{12,0},{1,5},{5,9},{9,13},{13,1},{2,6},{6,10},{... | collective-permute-start | bytes 49160 | tf_op jit(solution)/shard_map/ppermute | solution.py:476
  3.7 4.1 %collective-permute-start.1 = (f32[8,4,128]{2,1,0:T(4,128)}, f32[8,4,128]{2,1,0:T(4,128)S(1)}, u32[]{:S(2)}, u32[]{:S(2)}) collective-permute-start(f32[8,4,128]{2,1,0:T(4,128)} %own_hbm.1), channel_id=1, source_target_pairs={{0,12},{4,0},{8,4},{12,8},{1,13},{5,1},{9,5},{13,9},{2,14},{6,2},{... | collective-permute-start | bytes 49160 | tf_op jit(solution)/shard_map/ppermute | solution.py:476
  8.6 4.8 %collective-permute-start.4 = (f32[28,4,128]{2,1,0:T(4,128)S(1)}, f32[28,4,128]{2,1,0:T(4,128)S(1)}, u32[]{:S(2)}, u32[]{:S(2)}) collective-permute-start(f32[28,4,128]{2,1,0:T(4,128)S(1)} %widen.1.own), channel_id=1, source_target_pairs={{0,3},{1,2},{2,1},{3,0},{4,7},{5,6},{6,5},{7,4},{8,11},{9,10},{10,... | collective-permute-start | bytes 172040 | tf_op jit(solution)/shard_map/ppermute | solution.py:515
  8.7 4.8 %collective-permute-start.3 = (f32[28,4,128]{2,1,0:T(4,128)S(1)}, f32[28,4,128]{2,1,0:T(4,128)S(1)}, u32[]{:S(2)}, u32[]{:S(2)}) collective-permute-start(f32[28,4,128]{2,1,0:T(4,128)S(1)} %widen.1.own), channel_id=1, source_target_pairs={{0,1},{1,0},{2,3},{3,2},{4,5},{5,4},{6,7},{7,6},{8,9},{9,8},{10,11... | collective-permute-start | bytes 172040 | tf_op jit(solution)/shard_map/ppermute | solution.py:514
  10.3 4.2 %collective-permute-start.2 = (f32[28,4,128]{2,1,0:T(4,128)S(1)}, f32[28,4,128]{2,1,0:T(4,128)S(1)}, u32[]{:S(2)}, u32[]{:S(2)}) collective-permute-start(f32[28,4,128]{2,1,0:T(4,128)S(1)} %widen.1.own), channel_id=1, source_target_pairs={{0,2},{2,0},{1,3},{3,1},{4,6},{6,4},{5,7},{7,5},{8,10},{10,8},{9,1... | collective-permute-start | bytes 172040 | tf_op jit(solution)/shard_map/ppermute | solution.py:513
  22.3 8.4 %collective-permute-start.5 = (f32[7,8,128]{2,1,0:T(8,128)S(1)}, f32[7,8,128]{2,1,0:T(8,128)S(1)}, u32[]{:S(2)}, u32[]{:S(2)}) collective-permute-start(f32[7,8,128]{2,1,0:T(8,128)S(1)} %get-tuple-element.35), channel_id=1, source_target_pairs={{0,4},{4,8},{8,12},{12,0},{1,5},{5,9},{9,13},{13,1},{2,6},{6,10},{... | collective-permute-start | bytes 86024 | tf_op jit(solution)/shard_map/ppermute | solution.py:476
  23.6 7.0 %collective-permute-start.6 = (f32[7,8,128]{2,1,0:T(8,128)S(1)}, f32[7,8,128]{2,1,0:T(8,128)S(1)}, u32[]{:S(2)}, u32[]{:S(2)}) collective-permute-start(f32[7,8,128]{2,1,0:T(8,128)S(1)} %get-tuple-element.36), channel_id=1, source_target_pairs={{0,12},{4,0},{8,4},{12,8},{1,13},{5,1},{9,5},{13,9},{2,14},{6,2},{... | collective-permute-start | bytes 86024 | tf_op jit(solution)/shard_map/ppermute | solution.py:476
  26.2 4.5 %collective-permute-start.7 = (f32[8,128]{1,0:T(8,128)S(1)}, f32[8,128]{1,0:T(8,128)S(1)}, u32[]{:S(2)}, u32[]{:S(2)}) collective-permute-start(f32[8,128]{1,0:T(8,128)S(1)} %get-tuple-element.34.sums_ref), channel_id=1, source_target_pairs={{0,8},{4,12},{8,0},{12,4},{1,9},{5,13},{9,1},{13,5},{2,10},{6,14},... | collective-permute-start | bytes 12296 | tf_op jit(solution)/shard_map/ppermute | solution.py:476
  30.8 3.2 %collective-permute-start.8 = (f32[4,8,128]{2,1,0:T(8,128)S(1)}, f32[4,8,128]{2,1,0:T(8,128)S(1)}, u32[]{:S(2)}, u32[]{:S(2)}) collective-permute-start(f32[4,8,128]{2,1,0:T(8,128)S(1)} %get-tuple-element.38), channel_id=1, source_target_pairs={{0,2},{2,1},{1,3},{3,0},{4,6},{6,5},{5,7},{7,4},{8,10},{10,9},{9,1... | collective-permute-start | bytes 49160 | tf_op jit(solution)/shard_map/ppermute | solution.py:483
  31.4 3.7 %collective-permute-start.9 = (f32[4,8,128]{2,1,0:T(8,128)S(1)}, f32[4,8,128]{2,1,0:T(8,128)S(1)}, u32[]{:S(2)}, u32[]{:S(2)}) collective-permute-start(f32[4,8,128]{2,1,0:T(8,128)S(1)} %get-tuple-element.39), channel_id=1, source_target_pairs={{0,3},{2,0},{1,2},{3,1},{4,7},{6,4},{5,6},{7,5},{8,11},{10,8},{9,1... | collective-permute-start | bytes 49160 | tf_op jit(solution)/shard_map/ppermute | solution.py:483
  32.6 1.2 %collective-permute-start.10 = (f32[8,128]{1,0:T(8,128)S(1)}, f32[8,128]{1,0:T(8,128)S(1)}, u32[]{:S(2)}, u32[]{:S(2)}) collective-permute-start(f32[8,128]{1,0:T(8,128)S(1)} %get-tuple-element.40.sums_ref), channel_id=1, source_target_pairs={{0,1},{1,0},{2,3},{3,2},{4,5},{5,4},{6,7},{7,6},{8,9},{9,8},{10,11... | collective-permute-start | bytes 12296 | tf_op jit(solution)/shard_map/ppermute | solution.py:591
  43.5 10.4 %all-to-all-start = ((f32[16,8,128]{2,1,0:T(8,128)}), f32[16,8,128]{2,1,0:T(8,128)S(1)}, u32[]{:S(2)}, u32[]{:S(2)}) async-start(f32[16,8,128]{2,1,0:T(8,128)} %get-tuple-element.44), calls=%async_computation | async-start | bytes 131072 | tf_op jit(solution)/shard_map/all_to_all | solution.py:630
  47.0 3.9 %collective-permute-start.11 = (f32[8,4,128]{2,1,0:T(4,128)S(1)}, f32[8,4,128]{2,1,0:T(4,128)S(1)}, u32[]{:S(2)}, u32[]{:S(2)}) collective-permute-start(f32[8,4,128]{2,1,0:T(4,128)S(1)} %get-tuple-element.43), channel_id=1, source_target_pairs={{0,2},{2,0},{1,3},{3,1},{4,6},{6,4},{5,7},{7,5},{8,10},{10,8},{9,1... | collective-permute-start | bytes 49160 | tf_op jit(solution)/shard_map/ppermute | solution.py:629

commit v4 on v3

--- a/solution.py
+++ b/solution.py
@@ -14,6 +14,7 @@
 REACH = 6
 STRIPS = 16
 GROUP = 4
+PAIRS = 8
 SUMS = 16
 BF = jnp.bfloat16
 F32 = jnp.float32
@@ -57,8 +58,19 @@
         self.narrow = up(GROUP * self.fields, 128)
 
 
+PAIR_BLOCKS = (
+    (0, 0, 0, 0),
+    (0, 0, 1, 1),
+    (1, 0, 1, 0),
+    (1, 1, 0, 1),
+    (2, 1, 0, 0),
+    (2, 1, 1, 1),
+)
+
+
 def weights_kernel(p, dense_in, single_in, dense_out, first_out, last_out):
     ch, yw, lanes = p.ch, p.yw, p.lanes
+    half, wide = yw // 2, lanes // 2
 
     for ref_in, ref_out in zip(dense_in, dense_out):
         taps = []
@@ -71,11 +83,25 @@
         taps = jnp.concatenate(taps, axis=1)
         row, column = iota((3 * ch, lanes), 0), iota((3 * ch, lanes), 1)
         ty = lax.div(row, ch)
-        for yi in range(yw):
-            yo = lax.rem(yi + 1 - ty + yw, yw)
-            place = jnp.where(column == row + (yo - ty) * ch, 1.0, 0.0).astype(BF)
-            spread = dot(taps, place)
-            ref_out[:, yi * ch : (yi + 1) * ch, :] = spread.astype(BF).reshape(9, ch, lanes)
+        minus = column >= wide
+        for yi in range(half):
+            raw = yi + 1 - ty
+            wraps = (raw < 0) | (raw >= half)
+            yo = lax.rem(raw + half, half)
+            target = row + (yo - ty) * ch
+            match = jnp.where(minus, column - wide, column) == target
+            value = jnp.where(wraps & minus, -0.5, 0.5)
+            place = jnp.where(match, value, 0.0).astype(BF)
+            spread = dot(taps, place).astype(BF).reshape(3, 3, ch, lanes)
+            for sign in range(2):
+                for tx, step, x_in, x_out in PAIR_BLOCKS:
+                    begin = x_in * wide + yi * ch
+                    ref_out[
+                        sign, step, :, begin : begin + ch, x_out * wide : (x_out + 1) * wide
+                    ] = spread[tx, :, :, sign * wide : (sign + 1) * wide]
+        none = jnp.zeros((2, 3, wide, wide), BF)
+        ref_out[:, 0, :, :wide, wide:] = none
+        ref_out[:, 1, :, wide:, :wide] = none
 
     tile = (
         jnp.bitwise_and(iota((ch, lanes), 1), ch - 1) == iota((ch, lanes), 0)
@@ -88,14 +114,14 @@
     tx = lax.rem(lax.div(row, yw), 3)
     tz = lax.rem(lax.div(row, 3 * yw), 3)
     yo = lax.div(iota((rows, lanes), 1), ch)
-    for wide, ref_out, direction in zip(tiled, first_out, (1, -1)):
+    for single, ref_out, direction in zip(tiled, first_out, (1, -1)):
         total = jnp.zeros((rows, lanes), F32)
         for ty in range(3):
             number = 9 * tx + 3 * ty + tz
             number = number if direction > 0 else 26 - number
             pick = (iota((rows, 27), 1) == number).astype(F32).astype(BF)
             here = lax.rem(yo + (ty - 1 + yw), yw) == yi
-            total = total + jnp.where(here, dot(pick, wide), 0.0)
+            total = total + jnp.where(here, dot(pick, single), 0.0)
         ref_out[...] = total.astype(BF)
 
     rows = p.narrow
@@ -104,7 +130,7 @@
     field = lax.rem(lax.div(row, yw), 4)
     tx = lax.div(row, 4 * yw)
     yi = lax.div(iota((rows, lanes), 1), ch)
-    for wide, ref_out, direction in zip(tiled[::-1], last_out, (1, -1)):
+    for single, ref_out, direction in zip(tiled[::-1], last_out, (1, -1)):
         for tz in range(3):
             total = jnp.zeros((rows, lanes), F32)
             for ty in range(3):
@@ -121,7 +147,7 @@
                 factor = jnp.where(tx < 3, factor, 0).astype(F32)
                 pick = (iota((rows, 27), 1) == number).astype(F32).astype(BF)
                 here = lax.rem(yo + (ty - 1 + yw), yw) == yi
-                total = total + jnp.where(here, dot(pick, wide), 0.0) * factor
+                total = total + jnp.where(here, dot(pick, single), 0.0) * factor
             ref_out[tz] = total.astype(BF)
 
 
@@ -137,7 +163,7 @@
             copy.wait()
         weights_kernel(p, held[:2], held[2:], outs[:2], outs[2:4], outs[4:])
 
-    dense = jax.ShapeDtypeStruct((9, p.lanes, p.lanes), BF)
+    dense = jax.ShapeDtypeStruct((2, 2, 3, p.lanes, p.lanes), BF)
     single = jax.ShapeDtypeStruct((18 * p.yw, p.lanes), BF)
     narrow = jax.ShapeDtypeStruct((3, p.narrow, p.lanes), BF)
     flops = 2 * 2 * 9 * 3 * p.ch * p.lanes * p.lanes
@@ -170,15 +196,40 @@
     return [(start, min(size, total - start)) for start in range(0, total, size)]
 
 
+def store_pairs(p, ref, place, value):
+    wide = p.lanes // 2
+    first, second = value[:, :wide], value[:, wide:]
+    pair, side = divmod(place, 2)
+    lanes = slice(side * wide, (side + 1) * wide)
+    for sign, part in enumerate((first + second, first - second)):
+        tiles = part.reshape(p.lo, STRIPS, wide)
+        ref[sign, pair, 1 : p.lo + 1, :, lanes] = tiles.astype(BF)
+        ref[sign, pair, 0, :, lanes] = pltpu.roll(tiles[p.lo - 1], 1, 0).astype(BF)
+        ref[sign, pair, p.lo + 1, :, lanes] = pltpu.roll(tiles[0], STRIPS - 1, 0).astype(BF)
+
+
 def dense_planes(p, ref, w_ref, start, count, forward):
-    total = None
-    for t in range(9):
-        tx, tz = divmod(t, 3)
-        rows = ref[start + tx : start + tx + count, tz : tz + p.lo]
-        rows = rows.reshape(count * p.ze, p.lanes)
-        part = dot_nt(rows, w_ref[8 - t]) if forward else dot(rows, w_ref[t])
-        total = part if total is None else total + part
-    return total
+    halves = []
+    for sign in range(2):
+        total = None
+        for step in range(2):
+            for tz in range(3):
+                rows = ref[sign, start + step : start + step + count, tz : tz + p.lo]
+                rows = rows.reshape(count * p.ze, p.lanes)
+                if forward:
+                    part = dot_nt(rows, w_ref[sign, 1 - step, 2 - tz])
+                else:
+                    part = dot(rows, w_ref[sign, step, tz])
+                total = part if total is None else total + part
+        halves.append(total)
+    wide = p.lanes // 2
+    planes = []
+    for k in range(2 * count):
+        rows = slice(k // 2 * p.ze, (k // 2 + 1) * p.ze)
+        lanes = slice(k % 2 * wide, (k % 2 + 1) * wide)
+        plus, minus = halves[0][rows, lanes], halves[1][rows, lanes]
+        planes.append(jnp.concatenate([plus + minus, plus - minus], axis=1))
+    return planes
 
 
 def gate(value):
@@ -263,45 +314,37 @@
     for x in range(p.xo + 10):
         value = single_plane(p, planes, x, w_one)
         logistic, act = gate(value)
-        store_edges(p, act_a, x, act)
+        store_pairs(p, act_a, x, act)
         if 4 <= x < p.xo + 6:
             slope_one[x - 4] = slope_of(value, logistic, act)
 
-    for start, count in blocks(p.xo + 8, 4):
-        values = dense_planes(p, act_a, w_two, start, count, True)
-        for k in range(count):
-            x = start + k
-            value = values[k * p.ze : (k + 1) * p.ze]
+    for start, count in blocks((p.xo + 8) // 2, PAIRS):
+        for k, value in enumerate(dense_planes(p, act_a, w_two, start, count, True)):
+            x = 2 * start + k
             logistic, act = gate(value)
-            store_edges(p, act_b, x, act)
+            store_pairs(p, act_b, x, act)
             if 2 <= x < p.xo + 6:
                 slope_two[x - 2] = slope_of(value, logistic, act)
 
     to_planes(p, source, spread, planes)
-    for start, count in blocks(p.xo + 6, 7):
-        values = dense_planes(p, act_b, w_three, start, count, True)
-        for k in range(count):
-            x = start + k
-            value = values[k * p.ze : (k + 1) * p.ze]
+    for start, count in blocks((p.xo + 6) // 2, PAIRS):
+        for k, value in enumerate(dense_planes(p, act_b, w_three, start, count, True)):
+            x = 2 * start + k
             logistic, act = gate(value)
             if 2 <= x < p.xo + 4:
                 store_edges(p, act_c, x - 2, act)
             slope = slope_of(value, logistic, act)
-            store_edges(p, act_a, x, single_plane(p, planes, x + 2, w_source) * slope)
+            store_pairs(p, act_a, x, single_plane(p, planes, x + 2, w_source) * slope)
 
     enhance = narrow_fold(p, act_c, w_enhance, narrow, back)[:, 0]
 
-    for start, count in blocks(p.xo + 4, 4):
-        values = dense_planes(p, act_a, w_three, start, count, False)
-        for k in range(count):
-            x = start + k
-            store_edges(p, act_b, x, values[k * p.ze : (k + 1) * p.ze] * slope_two[x])
-
-    for start, count in blocks(p.xo + 2, 5):
-        values = dense_planes(p, act_b, w_two, start, count, False)
-        for k in range(count):
-            x = start + k
-            store_edges(p, act_c, x, values[k * p.ze : (k + 1) * p.ze] * slope_one[x])
+    for start, count in blocks((p.xo + 4) // 2, PAIRS):
+        for k, value in enumerate(dense_planes(p, act_a, w_three, start, count, False)):
+            store_pairs(p, act_b, 2 * start + k, value * slope_two[2 * start + k])
+
+    for start, count in blocks((p.xo + 2) // 2, PAIRS):
+        for k, value in enumerate(dense_planes(p, act_b, w_two, start, count, False)):
+            store_edges(p, act_c, 2 * start + k, value * slope_one[2 * start + k])
 
     levers = narrow_fold(p, act_c, w_lever, narrow, back)
 
@@ -348,14 +391,14 @@
 
 
 def update_scratch(p):
-    def acts(planes):
-        return pltpu.VMEM((planes, p.lo + 2, STRIPS, p.lanes), BF)
+    def pairs(planes):
+        return pltpu.VMEM((2, planes // 2, p.lo + 2, STRIPS, p.lanes), BF)
 
     return [
         pltpu.VMEM((2, p.xe, p.yw, 3 * p.zp), F32),
-        acts(p.xo + 10),
-        acts(p.xo + 8),
-        acts(p.xo + 2),
+        pairs(p.xo + 10),
+        pairs(p.xo + 8),
+        pltpu.VMEM((p.xo + 2, p.lo + 2, STRIPS, p.lanes), BF),
         pltpu.VMEM((p.xo + 2, p.ze, p.lanes), F32),
         pltpu.VMEM((p.xo + 4, p.ze, p.lanes), F32),
         pltpu.VMEM((p.xo + 2, p.ze, p.narrow), F32),
@@ -363,7 +406,7 @@
 
 
 def update_cost(p):
-    flops = 2 * 9 * p.lanes * p.lanes * p.ze * (4 * p.xo + 20)
+    flops = 2 * 6 * p.lanes * p.lanes * p.ze * (4 * p.xo + 20)
     return pl.CostEstimate(flops=flops, bytes_accessed=6 << 20, transcendentals=0)
 
 
@@ -467,8 +510,6 @@
     half = nz // 2
     p = Plan(nx, 2 * ny, 0, 2 * ny, half, ch, 20)
     lanes = p.zp
-    gy = lax.axis_index("gy")
-    where = gy.astype(jnp.int32).reshape(1)
     cells = nx * ny * nz * 16
     axes = ("gx", "gy", "gz")
 
@@ -515,9 +556,9 @@
     from_yz = lax.ppermute(wide, ("gy", "gz"), [(i, 3 - i) for i in range(4)])
     planes = p.xe + nx
 
-    def first_body(where_ref, own, y, z, yz, *refs):
+    def first_body(own, y, z, yz, *refs):
         weight_refs, outs, tile, scratch = refs[:6], refs[6:11], refs[11], refs[12:]
-        second = where_ref[0] == 1
+        second = lax.axis_index("gy") == 1
         shift = jnp.where(second, nz - half + p.zh, p.zh)
         lane = iota((planes, p.yw, lanes), 2)
         for ref, other in ((own, y), (z, yz)):
@@ -550,11 +591,11 @@
         "update_one",
         first_body,
         (f32(nx, p.yw, lanes), message, message, f32(nx, p.yw, lanes), f32(8, 128)),
-        1,
+        0,
         10,
         [pltpu.VMEM((planes, p.yw, lanes), F32)] + update_scratch(p),
         update_cost(p),
-    )(where, wide, from_y, from_z, from_yz, *weights)
+    )(wide, from_y, from_z, from_yz, *weights)
 
     left = along_x(high, 1)
     right = along_x(low, -1)
@@ -590,7 +631,7 @@
     above = along_z(down, -1)
     across = lax.ppermute(sums, "gz", [(0, 1), (1, 0)])
 
-    def second_body(where_ref, tile_ref, below_ref, above_ref, sums_ref, across_ref, ext_ref, *refs):
+    def second_body(tile_ref, below_ref, above_ref, sums_ref, across_ref, ext_ref, *refs):
         weight_refs, outs, cur, scratch = refs[:6], refs[6:10], refs[10], refs[11:]
         o_keep, o_send, o_sums, o_totals = outs
         totals = sums_ref[...] + across_ref[...] + below_ref[packs] + above_ref[packs]
@@ -609,7 +650,7 @@
         both = jnp.where(
             iota(pot.shape, 2) < half, pot, pltpu.roll(weighted, half, 2)
         )
-        second = where_ref[0] == 1
+        second = lax.axis_index("gy") == 1
         lower, top = both[:, :ny], both[:, ny:]
         o_keep[...] = jnp.where(second, top, lower)
         o_send[...] = jnp.where(second, lower, top)
@@ -620,21 +661,21 @@
         "update_two",
         second_body,
         (share, share, f32(16, 8, 128), f32(8, 128)),
-        1,
+        0,
         12,
         [pltpu.VMEM((p.xe, p.yw, lanes), F32)] + update_scratch(p),
         update_cost(p),
-    )(where, tile, below, above, sums, across, ext, *weights)
+    )(tile, below, above, sums, across, ext, *weights)
 
     other = lax.ppermute(send, "gy", [(0, 1), (1, 0)])
     gathered = lax.all_to_all(sums, axes, 0, 0, tiled=True)
 
-    def last_body(where_ref, keep_ref, other_ref, all_ref, totals_ref, o_new, o_pot, o_chem, o_stress):
+    def last_body(keep_ref, other_ref, all_ref, totals_ref, o_new, o_pot, o_chem, o_stress):
         first = totals_ref[...]
         last = jnp.sum(all_ref[...], axis=0)
         mass = pick(first, 1)
         scale = mass / pick(last, 0)
-        second = where_ref[0] == 1
+        second = lax.axis_index("gy") == 1
         mine, theirs = keep_ref[...], other_ref[...]
         lower = jnp.where(second, theirs, mine)
         top = jnp.where(second, mine, theirs)
@@ -655,9 +696,9 @@
         "finish",
         last_body,
         (f32(nx, ny, nz), f32(nx, ny, nz), f32(STEPS), f32(3, STEPS, 3)),
-        1,
+        0,
         4,
-    )(where, keep, other, gathered, totals)
+    )(keep, other, gathered, totals)
     return new, potential, chem, jnp.transpose(stress, (1, 0, 2))
 
 

time: 55.2 us -> 53 us (0.960)
  Pallas kernels: 20.4 us -> 18.1 us
    pallas_call x1, Pallas kernels: 7.79 us -> 6.7 us  [split_pairs(): kernel_call(p, 'update_one', first_body, (f32(nx, p.yw, lanes), message,...]
    pallas_call x1, Pallas kernels: 8.42 us -> 7.35 us  [split_pairs(): kernel_call(p, 'update_two', second_body, (share, share, f32(16, 8, 128),...]
where the time goes in v4:
time: 53 us; the launch traced here: 52.6 us
  starting transfers between devices  18.9 us (36%)
  Pallas kernels  18.1 us (34%)
  waiting for transfers between devices  14.8 us (28%)
  between operations  0.86 us (2%)
    ppermute x5, starting transfers between devices, along_x(): lax.ppermute(cells_out, 'gx', [(i, (i + step) % 4) for i in range(4)])  9.56 us
    pallas_call x1, Pallas kernels, split_pairs(): kernel_call(p, 'update_two', second_body, (share, share, f32(16, 8, 128),...  7.35 us
    pallas_call x1, Pallas kernels, split_pairs(): kernel_call(p, 'update_one', first_body, (f32(nx, p.yw, lanes), message,...  6.7 us
    ppermute x5, waiting for transfers between devices, along_x(): lax.ppermute(cells_out, 'gx', [(i, (i + step) % 4) for i in range(4)])  6.03 us
    all_to_all x1, starting transfers between devices, split_pairs(): gathered = lax.all_to_all(sums, axes, 0, 0, tiled=True)  3.49 us
    all_to_all x1, waiting for transfers between devices, split_pairs(): gathered = lax.all_to_all(sums, axes, 0, 0, tiled=True)  2.99 us
    pallas_call x1, Pallas kernels, spread_weights(): pl.pallas_call(body, name='spread_weights', out_shape=(dense,) * 2 + (sin...  2.41 us
    ppermute x1, waiting for transfers between devices, split_pairs(): other = lax.ppermute(send, 'gy', [(0, 1), (1, 0)])  2.01 us
  transfers between devices with their start and end apart: 13, of which 9 were waited for; matrix products, arithmetic and copies ran while one was open for 0% of the time, Pallas kernels for 5%

profile of v4, /device:TPU:0, one launch (start us, length us, event | category | flops | bytes accessed | tf_op | source)
XLA Modules:
  0.0 52.6 jit_solution(8467837650031490982)
XLA Ops:
  0.6 3.1 %collective-permute-start = (f32[8,4,128]{2,1,0:T(4,128)}, f32[8,4,128]{2,1,0:T(4,128)S(1)}, u32[]{:S(2)}, u32[]{:S(2)}) collective-permute-start(f32[8,4,128]{2,1,0:T(4,128)} %own_hbm.1), channel_id=1, source_target_pairs={{0,4},{4,8},{8,12},{12,0},{1,5},{5,9},{9,13},{13,1},{2,6},{6,10},{... | collective-permute-start | bytes 49160 | tf_op jit(solution)/shard_map/ppermute | solution.py:517
  3.7 2.1 %collective-permute-start.1 = (f32[8,4,128]{2,1,0:T(4,128)}, f32[8,4,128]{2,1,0:T(4,128)S(1)}, u32[]{:S(2)}, u32[]{:S(2)}) collective-permute-start(f32[8,4,128]{2,1,0:T(4,128)} %own_hbm.1), channel_id=1, source_target_pairs={{0,12},{4,0},{8,4},{12,8},{1,13},{5,1},{9,5},{13,9},{2,14},{6,2},{... | collective-permute-start | bytes 49160 | tf_op jit(solution)/shard_map/ppermute | solution.py:517
  5.8 2.0 %collective-permute-done.left_ref = f32[8,4,128]{2,1,0:T(4,128)S(1)} collective-permute-done((f32[8,4,128]{2,1,0:T(4,128)}, f32[8,4,128]{2,1,0:T(4,128)S(1)}, u32[]{:S(2)}, u32[]{:S(2)}) %collective-permute-start) | collective-permute-done | bytes 16416 | tf_op jit(solution)/shard_map/ppermute | solution.py:517
  7.8 0.1 collective-permute-done.1.right_ref
  7.8 0.8 %widen.1.own = f32[28,4,128]{2,1,0:T(4,128)S(1)} custom-call(f32[8,4,128]{2,1,0:T(4,128)} %own_hbm.1, f32[8,4,128]{2,1,0:T(4,128)} %ext_hbm.1, f32[8,4,128]{2,1,0:T(4,128)S(1)} %collective-permute-done.left_ref, f32[8,4,128]{2,1,0:T(4,128)S(1)} %collective-permute-done.1.right_ref), custom_call_target="tpu_custom_call" | custom-call | tf_op jit(solution)/shard_map/widen/pallas_call | solution.py:540
  8.6 0.1 collective-permute-start.4
  8.7 1.6 %collective-permute-start.3 = (f32[28,4,128]{2,1,0:T(4,128)S(1)}, f32[28,4,128]{2,1,0:T(4,128)S(1)}, u32[]{:S(2)}, u32[]{:S(2)}) collective-permute-start(f32[28,4,128]{2,1,0:T(4,128)S(1)} %widen.1.own), channel_id=1, source_target_pairs={{0,1},{1,0},{2,3},{3,2},{4,5},{5,4},{6,7},{7,6},{8,9},{9,8},{10,11... | collective-permute-start | bytes 172040 | tf_op jit(solution)/shard_map/ppermute | solution.py:555
  10.3 0.5 collective-permute-start.2
  10.8 2.4 %spread_weights.1 = (bf16[2,2,3,256,256]{4,3,2,1,0:T(8,128)(2,1)S(1)}, bf16[2,2,3,256,256]{4,3,2,1,0:T(8,128)(2,1)S(1)}, bf16[144,256]{1,0:T(8,128)(2,1)S(1)}, b...) custom-call(bf16[27,32,32]{2,1,0:T(8,128)(2,1)} %refs_0_.1, ...), custom_call_target="tpu_custom_call" | custom-call | flops 226492416 | bytes 3145728 | tf_op jit(solution)/shard_map/spread_weights/pallas_call | solution.py:170
  13.2 0.0 collective-permute-done.4.yz
  13.2 0.0 collective-permute-done.3.z
  13.2 1.3 %collective-permute-done.2.y = f32[28,4,128]{2,1,0:T(4,128)S(1)} collective-permute-done((f32[28,4,128]{2,1,0:T(4,128)S(1)}, f32[28,4,128]{2,1,0:T(4,128)S(1)}, u32[]{:S(2)}, u32[]{:S(2)}) %collective-permute-start.2) | collective-permute-done | bytes 57376 | tf_op jit(solution)/shard_map/ppermute | solution.py:554
  14.5 6.7 %update_one.1 = (f32[8,8,128]{2,1,0:T(8,128)S(1)}, f32[7,8,128]{2,1,0:T(8,128)S(1)}, f32[7,8,128]{2,1,0:T(8,128)S(1)}, f32[8,8,128]{2,1,0:T(8,128)S(1)}, f32[8,128]{1,0:T(8,128)S(1)}) custom-call(f32[28,4,128]{2,1,0:T(4,128)S(1)} %widen.1.own, f32[28,4,128]{2,1,0:T(4,128)S(1)} %collective-permute-done.2.y, f32[28,4,128]{2,1,0:T(4,128)S(1)} %collective-permute-done.3.z, ...), custom_call_target="tpu_custom_call" | custom-call | flops 3271557120 | bytes 6291456 | tf_op jit(solution)/shard_map/update_one/pallas_call | solution.py:589
  21.2 1.4 %collective-permute-start.5 = (f32[7,8,128]{2,1,0:T(8,128)S(1)}, f32[7,8,128]{2,1,0:T(8,128)S(1)}, u32[]{:S(2)}, u32[]{:S(2)}) collective-permute-start(f32[7,8,128]{2,1,0:T(8,128)S(1)} %get-tuple-element.35), channel_id=1, source_target_pairs={{0,4},{4,8},{8,12},{12,0},{1,5},{5,9},{9,13},{13,1},{2,6},{6,10},{... | collective-permute-start | bytes 86024 | tf_op jit(solution)/shard_map/ppermute | solution.py:517
  22.6 2.5 %collective-permute-start.6 = (f32[7,8,128]{2,1,0:T(8,128)S(1)}, f32[7,8,128]{2,1,0:T(8,128)S(1)}, u32[]{:S(2)}, u32[]{:S(2)}) collective-permute-start(f32[7,8,128]{2,1,0:T(8,128)S(1)} %get-tuple-element.36), channel_id=1, source_target_pairs={{0,12},{4,0},{8,4},{12,8},{1,13},{5,1},{9,5},{13,9},{2,14},{6,2},{... | collective-permute-start | bytes 86024 | tf_op jit(solution)/shard_map/ppermute | solution.py:517
  25.1 0.5 collective-permute-start.7
  25.6 4.0 %collective-permute-done.7.far_ref = f32[8,128]{1,0:T(8,128)S(1)} collective-permute-done((f32[8,128]{1,0:T(8,128)S(1)}, f32[8,128]{1,0:T(8,128)S(1)}, u32[]{:S(2)}, u32[]{:S(2)}) %collective-permute-start.7) | collective-permute-done | bytes 4128 | tf_op jit(solution)/shard_map/ppermute | solution.py:517
  29.6 0.0 collective-permute-done.5.left_ref
  29.6 0.0 collective-permute-done.6.right_ref
  29.6 0.1 join.1
  29.7 0.6 %collective-permute-start.8 = (f32[4,8,128]{2,1,0:T(8,128)S(1)}, f32[4,8,128]{2,1,0:T(8,128)S(1)}, u32[]{:S(2)}, u32[]{:S(2)}) collective-permute-start(f32[4,8,128]{2,1,0:T(8,128)S(1)} %get-tuple-element.38), channel_id=1, source_target_pairs={{0,2},{2,1},{1,3},{3,0},{4,6},{6,5},{5,7},{7,4},{8,10},{10,9},{9,1... | collective-permute-start | bytes 49160 | tf_op jit(solution)/shard_map/ppermute | solution.py:524
  30.3 1.2 %collective-permute-start.9 = (f32[4,8,128]{2,1,0:T(8,128)S(1)}, f32[4,8,128]{2,1,0:T(8,128)S(1)}, u32[]{:S(2)}, u32[]{:S(2)}) collective-permute-start(f32[4,8,128]{2,1,0:T(8,128)S(1)} %get-tuple-element.39), channel_id=1, source_target_pairs={{0,3},{2,0},{1,2},{3,1},{4,7},{6,4},{5,6},{7,5},{8,11},{10,8},{9,1... | collective-permute-start | bytes 49160 | tf_op jit(solution)/shard_map/ppermute | solution.py:524
  31.5 0.0 collective-permute-start.10
  31.5 1.2 %collective-permute-done.10.across_ref = f32[8,128]{1,0:T(8,128)S(1)} collective-permute-done((f32[8,128]{1,0:T(8,128)S(1)}, f32[8,128]{1,0:T(8,128)S(1)}, u32[]{:S(2)}, u32[]{:S(2)}) %collective-permute-start.10) | collective-permute-done | bytes 4128 | tf_op jit(solution)/shard_map/ppermute | solution.py:632
  32.7 0.2 collective-permute-done.8.below_ref
  32.9 1.1 %collective-permute-done.9.above_ref = f32[4,8,128]{2,1,0:T(8,128)S(1)} collective-permute-done((f32[4,8,128]{2,1,0:T(8,128)S(1)}, f32[4,8,128]{2,1,0:T(8,128)S(1)}, u32[]{:S(2)}, u32[]{:S(2)}) %collective-permute-start.9) | collective-permute-done | bytes 16416 | tf_op jit(solution)/shard_map/ppermute | solution.py:524
  34.0 7.3 %update_two.1 = (f32[8,4,128]{2,1,0:T(4,128)S(1)}, f32[8,4,128]{2,1,0:T(4,128)S(1)}, f32[16,8,128]{2,1,0:T(8,128)}, f32[8,128]{1,0:T(8,128)S(1)}) custom-call(f32[20,8,128]{2,1,0:T(8,128)S(1)} %get-tuple-element.37.tile_ref, f32[4,8,128]{2,1,0:T(8,128)S(1)} %collective-permute-done.8.below_ref, f32[4,8,128]{2,1,0:T(8,128)S(1)} %collective-permute-done.9.above_ref, ...), custom_call_target="tpu_custom_call" | custom-call | flops 3271557120 | bytes 6291456 | tf_op jit(solution)/shard_map/update_two/pallas_call | solution.py:659
  41.4 3.5 %all-to-all-start = ((f32[16,8,128]{2,1,0:T(8,128)}), f32[16,8,128]{2,1,0:T(8,128)S(1)}, u32[]{:S(2)}, u32[]{:S(2)}) async-start(f32[16,8,128]{2,1,0:T(8,128)} %get-tuple-element.44), calls=%async_computation | async-start | bytes 131072 | tf_op jit(solution)/shard_map/all_to_all | solution.py:671
  44.9 1.9 %collective-permute-start.11 = (f32[8,4,128]{2,1,0:T(4,128)S(1)}, f32[8,4,128]{2,1,0:T(4,128)S(1)}, u32[]{:S(2)}, u32[]{:S(2)}) collective-permute-start(f32[8,4,128]{2,1,0:T(4,128)S(1)} %get-tuple-element.43), channel_id=1, source_target_pairs={{0,2},{2,0},{1,3},{3,1},{4,6},{6,4},{5,7},{7,5},{8,10},{10,8},{9,1... | collective-permute-start | bytes 49160 | tf_op jit(solution)/shard_map/ppermute | solution.py:670
  46.7 2.0 %collective-permute-done.11.other_ref = f32[8,4,128]{2,1,0:T(4,128)S(1)} collective-permute-done((f32[8,4,128]{2,1,0:T(4,128)S(1)}, f32[8,4,128]{2,1,0:T(4,128)S(1)}, u32[]{:S(2)}, u32[]{:S(2)}) %collective-permute-start.11) | collective-permute-done | bytes 16416 | tf_op jit(solution)/shard_map/ppermute | solution.py:670
  48.7 3.0 %all-to-all-done.all_ref = f32[16,8,128]{2,1,0:T(8,128)S(1)} async-done(((f32[16,8,128]{2,1,0:T(8,128)}), f32[16,8,128]{2,1,0:T(8,128)S(1)}, u32[]{:S(2)}, u32[]{:S(2)}) %all-to-all-start) | async-done | bytes 65568 | tf_op jit(solution)/shard_map/all_to_all | solution.py:671
  51.7 0.8 %finish.1 = (f32[8,4,128]{2,1,0:T(4,128)}, f32[8,4,128]{2,1,0:T(4,128)}, f32[2]{0:T(128)}, f32[3,2,3]{2,1,0:T(2,128)}) custom-call(f32[8,4,128]{2,1,0:T(4,128)S(1)} %get-tuple-element.42.keep_ref, f32[8,4,128]{2,1,0:T(4,128)S(1)} %collective-permute-done.11.other_ref, f32[16,8,128]{2,1,0:T(8,128)S(1)} %all-to-all-done.all_ref, ...), custom_call_target="tpu_custom_call" | custom-call | tf_op jit(solution)/shard_map/finish/pallas_call | solution.py:694
Async XLA Ops:
  0.6 7.1 %collective-permute-start = (f32[8,4,128]{2,1,0:T(4,128)}, f32[8,4,128]{2,1,0:T(4,128)S(1)}, u32[]{:S(2)}, u32[]{:S(2)}) collective-permute-start(f32[8,4,128]{2,1,0:T(4,128)} %own_hbm.1), channel_id=1, source_target_pairs={{0,4},{4,8},{8,12},{12,0},{1,5},{5,9},{9,13},{13,1},{2,6},{6,10},{... | collective-permute-start | bytes 49160 | tf_op jit(solution)/shard_map/ppermute | solution.py:517
  3.7 4.1 %collective-permute-start.1 = (f32[8,4,128]{2,1,0:T(4,128)}, f32[8,4,128]{2,1,0:T(4,128)S(1)}, u32[]{:S(2)}, u32[]{:S(2)}) collective-permute-start(f32[8,4,128]{2,1,0:T(4,128)} %own_hbm.1), channel_id=1, source_target_pairs={{0,12},{4,0},{8,4},{12,8},{1,13},{5,1},{9,5},{13,9},{2,14},{6,2},{... | collective-permute-start | bytes 49160 | tf_op jit(solution)/shard_map/ppermute | solution.py:517
  8.6 4.6 %collective-permute-start.4 = (f32[28,4,128]{2,1,0:T(4,128)S(1)}, f32[28,4,128]{2,1,0:T(4,128)S(1)}, u32[]{:S(2)}, u32[]{:S(2)}) collective-permute-start(f32[28,4,128]{2,1,0:T(4,128)S(1)} %widen.1.own), channel_id=1, source_target_pairs={{0,3},{1,2},{2,1},{3,0},{4,7},{5,6},{6,5},{7,4},{8,11},{9,10},{10,... | collective-permute-start | bytes 172040 | tf_op jit(solution)/shard_map/ppermute | solution.py:556
  8.7 4.6 %collective-permute-start.3 = (f32[28,4,128]{2,1,0:T(4,128)S(1)}, f32[28,4,128]{2,1,0:T(4,128)S(1)}, u32[]{:S(2)}, u32[]{:S(2)}) collective-permute-start(f32[28,4,128]{2,1,0:T(4,128)S(1)} %widen.1.own), channel_id=1, source_target_pairs={{0,1},{1,0},{2,3},{3,2},{4,5},{5,4},{6,7},{7,6},{8,9},{9,8},{10,11... | collective-permute-start | bytes 172040 | tf_op jit(solution)/shard_map/ppermute | solution.py:555
  10.3 4.2 %collective-permute-start.2 = (f32[28,4,128]{2,1,0:T(4,128)S(1)}, f32[28,4,128]{2,1,0:T(4,128)S(1)}, u32[]{:S(2)}, u32[]{:S(2)}) collective-permute-start(f32[28,4,128]{2,1,0:T(4,128)S(1)} %widen.1.own), channel_id=1, source_target_pairs={{0,2},{2,0},{1,3},{3,1},{4,6},{6,4},{5,7},{7,5},{8,10},{10,8},{9,1... | collective-permute-start | bytes 172040 | tf_op jit(solution)/shard_map/ppermute | solution.py:554
  21.2 8.4 %collective-permute-start.5 = (f32[7,8,128]{2,1,0:T(8,128)S(1)}, f32[7,8,128]{2,1,0:T(8,128)S(1)}, u32[]{:S(2)}, u32[]{:S(2)}) collective-permute-start(f32[7,8,128]{2,1,0:T(8,128)S(1)} %get-tuple-element.35), channel_id=1, source_target_pairs={{0,4},{4,8},{8,12},{12,0},{1,5},{5,9},{9,13},{13,1},{2,6},{6,10},{... | collective-permute-start | bytes 86024 | tf_op jit(solution)/shard_map/ppermute | solution.py:517
  22.6 7.0 %collective-permute-start.6 = (f32[7,8,128]{2,1,0:T(8,128)S(1)}, f32[7,8,128]{2,1,0:T(8,128)S(1)}, u32[]{:S(2)}, u32[]{:S(2)}) collective-permute-start(f32[7,8,128]{2,1,0:T(8,128)S(1)} %get-tuple-element.36), channel_id=1, source_target_pairs={{0,12},{4,0},{8,4},{12,8},{1,13},{5,1},{9,5},{13,9},{2,14},{6,2},{... | collective-permute-start | bytes 86024 | tf_op jit(solution)/shard_map/ppermute | solution.py:517
  25.1 4.5 %collective-permute-start.7 = (f32[8,128]{1,0:T(8,128)S(1)}, f32[8,128]{1,0:T(8,128)S(1)}, u32[]{:S(2)}, u32[]{:S(2)}) collective-permute-start(f32[8,128]{1,0:T(8,128)S(1)} %get-tuple-element.34.sums_ref), channel_id=1, source_target_pairs={{0,8},{4,12},{8,0},{12,4},{1,9},{5,13},{9,1},{13,5},{2,10},{6,14},... | collective-permute-start | bytes 12296 | tf_op jit(solution)/shard_map/ppermute | solution.py:517
  29.7 3.2 %collective-permute-start.8 = (f32[4,8,128]{2,1,0:T(8,128)S(1)}, f32[4,8,128]{2,1,0:T(8,128)S(1)}, u32[]{:S(2)}, u32[]{:S(2)}) collective-permute-start(f32[4,8,128]{2,1,0:T(8,128)S(1)} %get-tuple-element.38), channel_id=1, source_target_pairs={{0,2},{2,1},{1,3},{3,0},{4,6},{6,5},{5,7},{7,4},{8,10},{10,9},{9,1... | collective-permute-start | bytes 49160 | tf_op jit(solution)/shard_map/ppermute | solution.py:524
  30.3 3.7 %collective-permute-start.9 = (f32[4,8,128]{2,1,0:T(8,128)S(1)}, f32[4,8,128]{2,1,0:T(8,128)S(1)}, u32[]{:S(2)}, u32[]{:S(2)}) collective-permute-start(f32[4,8,128]{2,1,0:T(8,128)S(1)} %get-tuple-element.39), channel_id=1, source_target_pairs={{0,3},{2,0},{1,2},{3,1},{4,7},{6,4},{5,6},{7,5},{8,11},{10,8},{9,1... | collective-permute-start | bytes 49160 | tf_op jit(solution)/shard_map/ppermute | solution.py:524
  31.5 1.2 %collective-permute-start.10 = (f32[8,128]{1,0:T(8,128)S(1)}, f32[8,128]{1,0:T(8,128)S(1)}, u32[]{:S(2)}, u32[]{:S(2)}) collective-permute-start(f32[8,128]{1,0:T(8,128)S(1)} %get-tuple-element.40.sums_ref), channel_id=1, source_target_pairs={{0,1},{1,0},{2,3},{3,2},{4,5},{5,4},{6,7},{7,6},{8,9},{9,8},{10,11... | collective-permute-start | bytes 12296 | tf_op jit(solution)/shard_map/ppermute | solution.py:632
  41.4 10.4 %all-to-all-start = ((f32[16,8,128]{2,1,0:T(8,128)}), f32[16,8,128]{2,1,0:T(8,128)S(1)}, u32[]{:S(2)}, u32[]{:S(2)}) async-start(f32[16,8,128]{2,1,0:T(8,128)} %get-tuple-element.44), calls=%async_computation | async-start | bytes 131072 | tf_op jit(solution)/shard_map/all_to_all | solution.py:671
  44.9 3.9 %collective-permute-start.11 = (f32[8,4,128]{2,1,0:T(4,128)S(1)}, f32[8,4,128]{2,1,0:T(4,128)S(1)}, u32[]{:S(2)}, u32[]{:S(2)}) collective-permute-start(f32[8,4,128]{2,1,0:T(4,128)S(1)} %get-tuple-element.43), channel_id=1, source_target_pairs={{0,2},{2,0},{1,3},{3,1},{4,6},{6,4},{5,7},{7,5},{8,10},{10,8},{9,1... | collective-permute-start | bytes 49160 | tf_op jit(solution)/shard_map/ppermute | solution.py:670

commit v5 on v4

--- a/solution.py
+++ b/solution.py
@@ -90,7 +90,7 @@
             yo = lax.rem(raw + half, half)
             target = row + (yo - ty) * ch
             match = jnp.where(minus, column - wide, column) == target
-            value = jnp.where(wraps & minus, -0.5, 0.5)
+            value = jnp.where(wraps & minus, -0.25, 0.25)
             place = jnp.where(match, value, 0.0).astype(BF)
             spread = dot(taps, place).astype(BF).reshape(3, 3, ch, lanes)
             for sign in range(2):
@@ -122,7 +122,7 @@
             pick = (iota((rows, 27), 1) == number).astype(F32).astype(BF)
             here = lax.rem(yo + (ty - 1 + yw), yw) == yi
             total = total + jnp.where(here, dot(pick, single), 0.0)
-        ref_out[...] = total.astype(BF)
+        ref_out[...] = (0.5 * total).astype(BF)
 
     rows = p.narrow
     row = iota((rows, 1), 0)
@@ -232,14 +232,14 @@
     return planes
 
 
-def gate(value):
-    logistic = 0.5 * jnp.tanh(0.5 * value) + 0.5
-    act = value * logistic
-    return logistic, act
-
-
-def slope_of(value, logistic, act):
-    return logistic * (1.0 + value - act)
+def gate(value, slope=True):
+    wave = jnp.tanh(value)
+    product = value * wave
+    act = value + product
+    if not slope:
+        return act, None
+    rise = 1.0 + wave
+    return act, rise + rise * (value - product)
 
 
 def to_planes(p, field, spread, planes_ref):
@@ -313,27 +313,28 @@
     to_planes(p, cube, spread, planes)
     for x in range(p.xo + 10):
         value = single_plane(p, planes, x, w_one)
-        logistic, act = gate(value)
+        inside = 4 <= x < p.xo + 6
+        act, slope = gate(value, inside)
         store_pairs(p, act_a, x, act)
-        if 4 <= x < p.xo + 6:
-            slope_one[x - 4] = slope_of(value, logistic, act)
+        if inside:
+            slope_one[x - 4] = slope
 
     for start, count in blocks((p.xo + 8) // 2, PAIRS):
         for k, value in enumerate(dense_planes(p, act_a, w_two, start, count, True)):
             x = 2 * start + k
-            logistic, act = gate(value)
+            inside = 2 <= x < p.xo + 6
+            act, slope = gate(value, inside)
             store_pairs(p, act_b, x, act)
-            if 2 <= x < p.xo + 6:
-                slope_two[x - 2] = slope_of(value, logistic, act)
+            if inside:
+                slope_two[x - 2] = slope
 
     to_planes(p, source, spread, planes)
     for start, count in blocks((p.xo + 6) // 2, PAIRS):
         for k, value in enumerate(dense_planes(p, act_b, w_three, start, count, True)):
             x = 2 * start + k
-            logistic, act = gate(value)
+            act, slope = gate(value)
             if 2 <= x < p.xo + 4:
                 store_edges(p, act_c, x - 2, act)
-            slope = slope_of(value, logistic, act)
             store_pairs(p, act_a, x, single_plane(p, planes, x + 2, w_source) * slope)
 
     enhance = narrow_fold(p, act_c, w_enhance, narrow, back)[:, 0]
@@ -646,7 +647,7 @@
             joined = jnp.where(lane < p.zh, lower, jnp.where(lane < p.zh + half, middle, top))
             cur[x] = joined * scale
         pot, weighted, sums_here = update_kernel(p, cur[...], ext_ref[...], weight_refs, scratch)
-        o_sums[...] = jnp.broadcast_to(sums_here, (16, 8, 128))
+        o_sums[...] = jnp.broadcast_to(sums_here[:4], (16, 4, 128))
         both = jnp.where(
             iota(pot.shape, 2) < half, pot, pltpu.roll(weighted, half, 2)
         )
@@ -660,7 +661,7 @@
         p,
         "update_two",
         second_body,
-        (share, share, f32(16, 8, 128), f32(8, 128)),
+        (share, share, f32(16, 4, 128), f32(8, 128)),
         0,
         12,
         [pltpu.VMEM((p.xe, p.yw, lanes), F32)] + update_scratch(p),
@@ -673,6 +674,7 @@
     def last_body(keep_ref, other_ref, all_ref, totals_ref, o_new, o_pot, o_chem, o_stress):
         first = totals_ref[...]
         last = jnp.sum(all_ref[...], axis=0)
+        last = jnp.concatenate([last, last], axis=0)
         mass = pick(first, 1)
         scale = mass / pick(last, 0)
         second = lax.axis_index("gy") == 1

time: 53 us -> 52.4 us (0.989)
  no operation moved by 1% of the time
where the time goes in v5:
time: 52.4 us; the launch traced here: 52 us
  starting transfers between devices  18.9 us (36%)
  Pallas kernels  17.7 us (34%)
  waiting for transfers between devices  14.5 us (28%)
  between operations  0.86 us (2%)
    ppermute x5, starting transfers between devices, along_x(): lax.ppermute(cells_out, 'gx', [(i, (i + step) % 4) for i in range(4)])  9.56 us
    pallas_call x1, Pallas kernels, split_pairs(): kernel_call(p, 'update_two', second_body, (share, share, f32(16, 4, 128),...  7.15 us
    pallas_call x1, Pallas kernels, split_pairs(): kernel_call(p, 'update_one', first_body, (f32(nx, p.yw, lanes), message,...  6.52 us
    ppermute x5, waiting for transfers between devices, along_x(): lax.ppermute(cells_out, 'gx', [(i, (i + step) % 4) for i in range(4)])  6.03 us
    all_to_all x1, starting transfers between devices, split_pairs(): gathered = lax.all_to_all(sums, axes, 0, 0, tiled=True)  3.49 us
    all_to_all x1, waiting for transfers between devices, split_pairs(): gathered = lax.all_to_all(sums, axes, 0, 0, tiled=True)  2.78 us
    pallas_call x1, Pallas kernels, spread_weights(): pl.pallas_call(body, name='spread_weights', out_shape=(dense,) * 2 + (sin...  2.42 us
    ppermute x1, waiting for transfers between devices, split_pairs(): other = lax.ppermute(send, 'gy', [(0, 1), (1, 0)])  1.96 us
  transfers between devices with their start and end apart: 13, of which 9 were waited for; matrix products, arithmetic and copies ran while one was open for 0% of the time, Pallas kernels for 5%

profile of v5, /device:TPU:0, one launch (start us, length us, event | category | flops | bytes accessed | tf_op | source)
XLA Modules:
  0.0 52.0 jit_solution(15156806196828021342)
XLA Ops:
  0.6 3.1 %collective-permute-start = (f32[8,4,128]{2,1,0:T(4,128)}, f32[8,4,128]{2,1,0:T(4,128)S(1)}, u32[]{:S(2)}, u32[]{:S(2)}) collective-permute-start(f32[8,4,128]{2,1,0:T(4,128)} %own_hbm.1), channel_id=1, source_target_pairs={{0,4},{4,8},{8,12},{12,0},{1,5},{5,9},{9,13},{13,1},{2,6},{6,10},{... | collective-permute-start | bytes 49160 | tf_op jit(solution)/shard_map/ppermute | solution.py:518
  3.7 2.1 %collective-permute-start.1 = (f32[8,4,128]{2,1,0:T(4,128)}, f32[8,4,128]{2,1,0:T(4,128)S(1)}, u32[]{:S(2)}, u32[]{:S(2)}) collective-permute-start(f32[8,4,128]{2,1,0:T(4,128)} %own_hbm.1), channel_id=1, source_target_pairs={{0,12},{4,0},{8,4},{12,8},{1,13},{5,1},{9,5},{13,9},{2,14},{6,2},{... | collective-permute-start | bytes 49160 | tf_op jit(solution)/shard_map/ppermute | solution.py:518
  5.8 2.0 %collective-permute-done.left_ref = f32[8,4,128]{2,1,0:T(4,128)S(1)} collective-permute-done((f32[8,4,128]{2,1,0:T(4,128)}, f32[8,4,128]{2,1,0:T(4,128)S(1)}, u32[]{:S(2)}, u32[]{:S(2)}) %collective-permute-start) | collective-permute-done | bytes 16416 | tf_op jit(solution)/shard_map/ppermute | solution.py:518
  7.8 0.1 collective-permute-done.1.right_ref
  7.8 0.8 %widen.1.own = f32[28,4,128]{2,1,0:T(4,128)S(1)} custom-call(f32[8,4,128]{2,1,0:T(4,128)} %own_hbm.1, f32[8,4,128]{2,1,0:T(4,128)} %ext_hbm.1, f32[8,4,128]{2,1,0:T(4,128)S(1)} %collective-permute-done.left_ref, f32[8,4,128]{2,1,0:T(4,128)S(1)} %collective-permute-done.1.right_ref), custom_call_target="tpu_custom_call" | custom-call | tf_op jit(solution)/shard_map/widen/pallas_call | solution.py:541
  8.6 0.1 collective-permute-start.4
  8.7 1.6 %collective-permute-start.3 = (f32[28,4,128]{2,1,0:T(4,128)S(1)}, f32[28,4,128]{2,1,0:T(4,128)S(1)}, u32[]{:S(2)}, u32[]{:S(2)}) collective-permute-start(f32[28,4,128]{2,1,0:T(4,128)S(1)} %widen.1.own), channel_id=1, source_target_pairs={{0,1},{1,0},{2,3},{3,2},{4,5},{5,4},{6,7},{7,6},{8,9},{9,8},{10,11... | collective-permute-start | bytes 172040 | tf_op jit(solution)/shard_map/ppermute | solution.py:556
  10.3 0.5 collective-permute-start.2
  10.8 2.4 %spread_weights.1 = (bf16[2,2,3,256,256]{4,3,2,1,0:T(8,128)(2,1)S(1)}, bf16[2,2,3,256,256]{4,3,2,1,0:T(8,128)(2,1)S(1)}, bf16[144,256]{1,0:T(8,128)(2,1)S(1)}, b...) custom-call(bf16[27,32,32]{2,1,0:T(8,128)(2,1)} %refs_0_.1, ...), custom_call_target="tpu_custom_call" | custom-call | flops 226492416 | bytes 3145728 | tf_op jit(solution)/shard_map/spread_weights/pallas_call | solution.py:170
  13.2 0.0 collective-permute-done.4.yz
  13.2 0.0 collective-permute-done.3.z
  13.3 1.2 %collective-permute-done.2.y = f32[28,4,128]{2,1,0:T(4,128)S(1)} collective-permute-done((f32[28,4,128]{2,1,0:T(4,128)S(1)}, f32[28,4,128]{2,1,0:T(4,128)S(1)}, u32[]{:S(2)}, u32[]{:S(2)}) %collective-permute-start.2) | collective-permute-done | bytes 57376 | tf_op jit(solution)/shard_map/ppermute | solution.py:555
  14.5 6.5 %update_one.1 = (f32[8,8,128]{2,1,0:T(8,128)S(1)}, f32[7,8,128]{2,1,0:T(8,128)S(1)}, f32[7,8,128]{2,1,0:T(8,128)S(1)}, f32[8,8,128]{2,1,0:T(8,128)S(1)}, f32[8,128]{1,0:T(8,128)S(1)}) custom-call(f32[28,4,128]{2,1,0:T(4,128)S(1)} %widen.1.own, f32[28,4,128]{2,1,0:T(4,128)S(1)} %collective-permute-done.2.y, f32[28,4,128]{2,1,0:T(4,128)S(1)} %collective-permute-done.3.z, ...), custom_call_target="tpu_custom_call" | custom-call | flops 3271557120 | bytes 6291456 | tf_op jit(solution)/shard_map/update_one/pallas_call | solution.py:590
  21.0 1.4 %collective-permute-start.5 = (f32[7,8,128]{2,1,0:T(8,128)S(1)}, f32[7,8,128]{2,1,0:T(8,128)S(1)}, u32[]{:S(2)}, u32[]{:S(2)}) collective-permute-start(f32[7,8,128]{2,1,0:T(8,128)S(1)} %get-tuple-element.35), channel_id=1, source_target_pairs={{0,4},{4,8},{8,12},{12,0},{1,5},{5,9},{9,13},{13,1},{2,6},{6,10},{... | collective-permute-start | bytes 86024 | tf_op jit(solution)/shard_map/ppermute | solution.py:518
  22.4 2.5 %collective-permute-start.6 = (f32[7,8,128]{2,1,0:T(8,128)S(1)}, f32[7,8,128]{2,1,0:T(8,128)S(1)}, u32[]{:S(2)}, u32[]{:S(2)}) collective-permute-start(f32[7,8,128]{2,1,0:T(8,128)S(1)} %get-tuple-element.36), channel_id=1, source_target_pairs={{0,12},{4,0},{8,4},{12,8},{1,13},{5,1},{9,5},{13,9},{2,14},{6,2},{... | collective-permute-start | bytes 86024 | tf_op jit(solution)/shard_map/ppermute | solution.py:518
  24.9 0.5 collective-permute-start.7
  25.4 4.0 %collective-permute-done.7.far_ref = f32[8,128]{1,0:T(8,128)S(1)} collective-permute-done((f32[8,128]{1,0:T(8,128)S(1)}, f32[8,128]{1,0:T(8,128)S(1)}, u32[]{:S(2)}, u32[]{:S(2)}) %collective-permute-start.7) | collective-permute-done | bytes 4128 | tf_op jit(solution)/shard_map/ppermute | solution.py:518
  29.4 0.0 collective-permute-done.5.left_ref
  29.4 0.0 collective-permute-done.6.right_ref
  29.4 0.1 join.1
  29.5 0.6 %collective-permute-start.8 = (f32[4,8,128]{2,1,0:T(8,128)S(1)}, f32[4,8,128]{2,1,0:T(8,128)S(1)}, u32[]{:S(2)}, u32[]{:S(2)}) collective-permute-start(f32[4,8,128]{2,1,0:T(8,128)S(1)} %get-tuple-element.38), channel_id=1, source_target_pairs={{0,2},{2,1},{1,3},{3,0},{4,6},{6,5},{5,7},{7,4},{8,10},{10,9},{9,1... | collective-permute-start | bytes 49160 | tf_op jit(solution)/shard_map/ppermute | solution.py:525
  30.1 1.2 %collective-permute-start.9 = (f32[4,8,128]{2,1,0:T(8,128)S(1)}, f32[4,8,128]{2,1,0:T(8,128)S(1)}, u32[]{:S(2)}, u32[]{:S(2)}) collective-permute-start(f32[4,8,128]{2,1,0:T(8,128)S(1)} %get-tuple-element.39), channel_id=1, source_target_pairs={{0,3},{2,0},{1,2},{3,1},{4,7},{6,4},{5,6},{7,5},{8,11},{10,8},{9,1... | collective-permute-start | bytes 49160 | tf_op jit(solution)/shard_map/ppermute | solution.py:525
  31.3 0.0 collective-permute-start.10
  31.3 1.2 %collective-permute-done.10.across_ref = f32[8,128]{1,0:T(8,128)S(1)} collective-permute-done((f32[8,128]{1,0:T(8,128)S(1)}, f32[8,128]{1,0:T(8,128)S(1)}, u32[]{:S(2)}, u32[]{:S(2)}) %collective-permute-start.10) | collective-permute-done | bytes 4128 | tf_op jit(solution)/shard_map/ppermute | solution.py:633
  32.5 0.2 collective-permute-done.8.below_ref
  32.7 1.1 %collective-permute-done.9.above_ref = f32[4,8,128]{2,1,0:T(8,128)S(1)} collective-permute-done((f32[4,8,128]{2,1,0:T(8,128)S(1)}, f32[4,8,128]{2,1,0:T(8,128)S(1)}, u32[]{:S(2)}, u32[]{:S(2)}) %collective-permute-start.9) | collective-permute-done | bytes 16416 | tf_op jit(solution)/shard_map/ppermute | solution.py:525
  33.8 7.2 %update_two.1 = (f32[8,4,128]{2,1,0:T(4,128)S(1)}, f32[8,4,128]{2,1,0:T(4,128)S(1)}, f32[16,4,128]{2,1,0:T(4,128)}, f32[8,128]{1,0:T(8,128)S(1)}) custom-call(f32[20,8,128]{2,1,0:T(8,128)S(1)} %get-tuple-element.37.tile_ref, f32[4,8,128]{2,1,0:T(8,128)S(1)} %collective-permute-done.8.below_ref, f32[4,8,128]{2,1,0:T(8,128)S(1)} %collective-permute-done.9.above_ref, ...), custom_call_target="tpu_custom_call" | custom-call | flops 3271557120 | bytes 6291456 | tf_op jit(solution)/shard_map/update_two/pallas_call | solution.py:660
  41.0 3.5 %all-to-all-start = ((f32[16,4,128]{2,1,0:T(4,128)}), f32[16,4,128]{2,1,0:T(4,128)S(1)}, u32[]{:S(2)}, u32[]{:S(2)}) async-start(f32[16,4,128]{2,1,0:T(4,128)} %get-tuple-element.44), calls=%async_computation | async-start | bytes 65536 | tf_op jit(solution)/shard_map/all_to_all | solution.py:672
  44.5 1.9 %collective-permute-start.11 = (f32[8,4,128]{2,1,0:T(4,128)S(1)}, f32[8,4,128]{2,1,0:T(4,128)S(1)}, u32[]{:S(2)}, u32[]{:S(2)}) collective-permute-start(f32[8,4,128]{2,1,0:T(4,128)S(1)} %get-tuple-element.43), channel_id=1, source_target_pairs={{0,2},{2,0},{1,3},{3,1},{4,6},{6,4},{5,7},{7,5},{8,10},{10,8},{9,1... | collective-permute-start | bytes 49160 | tf_op jit(solution)/shard_map/ppermute | solution.py:671
  46.3 2.0 %collective-permute-done.11.other_ref = f32[8,4,128]{2,1,0:T(4,128)S(1)} collective-permute-done((f32[8,4,128]{2,1,0:T(4,128)S(1)}, f32[8,4,128]{2,1,0:T(4,128)S(1)}, u32[]{:S(2)}, u32[]{:S(2)}) %collective-permute-start.11) | collective-permute-done | bytes 16416 | tf_op jit(solution)/shard_map/ppermute | solution.py:671
  48.3 2.8 %all-to-all-done.all_ref = f32[16,4,128]{2,1,0:T(4,128)S(1)} async-done(((f32[16,4,128]{2,1,0:T(4,128)}), f32[16,4,128]{2,1,0:T(4,128)S(1)}, u32[]{:S(2)}, u32[]{:S(2)}) %all-to-all-start) | async-done | bytes 32800 | tf_op jit(solution)/shard_map/all_to_all | solution.py:672
  51.1 0.8 %finish.1 = (f32[8,4,128]{2,1,0:T(4,128)}, f32[8,4,128]{2,1,0:T(4,128)}, f32[2]{0:T(128)}, f32[3,2,3]{2,1,0:T(2,128)}) custom-call(f32[8,4,128]{2,1,0:T(4,128)S(1)} %get-tuple-element.42.keep_ref, f32[8,4,128]{2,1,0:T(4,128)S(1)} %collective-permute-done.11.other_ref, f32[16,4,128]{2,1,0:T(4,128)S(1)} %all-to-all-done.all_ref, ...), custom_call_target="tpu_custom_call" | custom-call | tf_op jit(solution)/shard_map/finish/pallas_call | solution.py:696
Async XLA Ops:
  0.6 7.1 %collective-permute-start = (f32[8,4,128]{2,1,0:T(4,128)}, f32[8,4,128]{2,1,0:T(4,128)S(1)}, u32[]{:S(2)}, u32[]{:S(2)}) collective-permute-start(f32[8,4,128]{2,1,0:T(4,128)} %own_hbm.1), channel_id=1, source_target_pairs={{0,4},{4,8},{8,12},{12,0},{1,5},{5,9},{9,13},{13,1},{2,6},{6,10},{... | collective-permute-start | bytes 49160 | tf_op jit(solution)/shard_map/ppermute | solution.py:518
  3.7 4.1 %collective-permute-start.1 = (f32[8,4,128]{2,1,0:T(4,128)}, f32[8,4,128]{2,1,0:T(4,128)S(1)}, u32[]{:S(2)}, u32[]{:S(2)}) collective-permute-start(f32[8,4,128]{2,1,0:T(4,128)} %own_hbm.1), channel_id=1, source_target_pairs={{0,12},{4,0},{8,4},{12,8},{1,13},{5,1},{9,5},{13,9},{2,14},{6,2},{... | collective-permute-start | bytes 49160 | tf_op jit(solution)/shard_map/ppermute | solution.py:518
  8.6 4.6 %collective-permute-start.4 = (f32[28,4,128]{2,1,0:T(4,128)S(1)}, f32[28,4,128]{2,1,0:T(4,128)S(1)}, u32[]{:S(2)}, u32[]{:S(2)}) collective-permute-start(f32[28,4,128]{2,1,0:T(4,128)S(1)} %widen.1.own), channel_id=1, source_target_pairs={{0,3},{1,2},{2,1},{3,0},{4,7},{5,6},{6,5},{7,4},{8,11},{9,10},{10,... | collective-permute-start | bytes 172040 | tf_op jit(solution)/shard_map/ppermute | solution.py:557
  8.7 4.6 %collective-permute-start.3 = (f32[28,4,128]{2,1,0:T(4,128)S(1)}, f32[28,4,128]{2,1,0:T(4,128)S(1)}, u32[]{:S(2)}, u32[]{:S(2)}) collective-permute-start(f32[28,4,128]{2,1,0:T(4,128)S(1)} %widen.1.own), channel_id=1, source_target_pairs={{0,1},{1,0},{2,3},{3,2},{4,5},{5,4},{6,7},{7,6},{8,9},{9,8},{10,11... | collective-permute-start | bytes 172040 | tf_op jit(solution)/shard_map/ppermute | solution.py:556
  10.3 4.2 %collective-permute-start.2 = (f32[28,4,128]{2,1,0:T(4,128)S(1)}, f32[28,4,128]{2,1,0:T(4,128)S(1)}, u32[]{:S(2)}, u32[]{:S(2)}) collective-permute-start(f32[28,4,128]{2,1,0:T(4,128)S(1)} %widen.1.own), channel_id=1, source_target_pairs={{0,2},{2,0},{1,3},{3,1},{4,6},{6,4},{5,7},{7,5},{8,10},{10,8},{9,1... | collective-permute-start | bytes 172040 | tf_op jit(solution)/shard_map/ppermute | solution.py:555
  21.0 8.4 %collective-permute-start.5 = (f32[7,8,128]{2,1,0:T(8,128)S(1)}, f32[7,8,128]{2,1,0:T(8,128)S(1)}, u32[]{:S(2)}, u32[]{:S(2)}) collective-permute-start(f32[7,8,128]{2,1,0:T(8,128)S(1)} %get-tuple-element.35), channel_id=1, source_target_pairs={{0,4},{4,8},{8,12},{12,0},{1,5},{5,9},{9,13},{13,1},{2,6},{6,10},{... | collective-permute-start | bytes 86024 | tf_op jit(solution)/shard_map/ppermute | solution.py:518
  22.4 7.0 %collective-permute-start.6 = (f32[7,8,128]{2,1,0:T(8,128)S(1)}, f32[7,8,128]{2,1,0:T(8,128)S(1)}, u32[]{:S(2)}, u32[]{:S(2)}) collective-permute-start(f32[7,8,128]{2,1,0:T(8,128)S(1)} %get-tuple-element.36), channel_id=1, source_target_pairs={{0,12},{4,0},{8,4},{12,8},{1,13},{5,1},{9,5},{13,9},{2,14},{6,2},{... | collective-permute-start | bytes 86024 | tf_op jit(solution)/shard_map/ppermute | solution.py:518
  24.9 4.5 %collective-permute-start.7 = (f32[8,128]{1,0:T(8,128)S(1)}, f32[8,128]{1,0:T(8,128)S(1)}, u32[]{:S(2)}, u32[]{:S(2)}) collective-permute-start(f32[8,128]{1,0:T(8,128)S(1)} %get-tuple-element.34.sums_ref), channel_id=1, source_target_pairs={{0,8},{4,12},{8,0},{12,4},{1,9},{5,13},{9,1},{13,5},{2,10},{6,14},... | collective-permute-start | bytes 12296 | tf_op jit(solution)/shard_map/ppermute | solution.py:518
  29.5 3.2 %collective-permute-start.8 = (f32[4,8,128]{2,1,0:T(8,128)S(1)}, f32[4,8,128]{2,1,0:T(8,128)S(1)}, u32[]{:S(2)}, u32[]{:S(2)}) collective-permute-start(f32[4,8,128]{2,1,0:T(8,128)S(1)} %get-tuple-element.38), channel_id=1, source_target_pairs={{0,2},{2,1},{1,3},{3,0},{4,6},{6,5},{5,7},{7,4},{8,10},{10,9},{9,1... | collective-permute-start | bytes 49160 | tf_op jit(solution)/shard_map/ppermute | solution.py:525
  30.1 3.7 %collective-permute-start.9 = (f32[4,8,128]{2,1,0:T(8,128)S(1)}, f32[4,8,128]{2,1,0:T(8,128)S(1)}, u32[]{:S(2)}, u32[]{:S(2)}) collective-permute-start(f32[4,8,128]{2,1,0:T(8,128)S(1)} %get-tuple-element.39), channel_id=1, source_target_pairs={{0,3},{2,0},{1,2},{3,1},{4,7},{6,4},{5,6},{7,5},{8,11},{10,8},{9,1... | collective-permute-start | bytes 49160 | tf_op jit(solution)/shard_map/ppermute | solution.py:525
  31.3 1.2 %collective-permute-start.10 = (f32[8,128]{1,0:T(8,128)S(1)}, f32[8,128]{1,0:T(8,128)S(1)}, u32[]{:S(2)}, u32[]{:S(2)}) collective-permute-start(f32[8,128]{1,0:T(8,128)S(1)} %get-tuple-element.40.sums_ref), channel_id=1, source_target_pairs={{0,1},{1,0},{2,3},{3,2},{4,5},{5,4},{6,7},{7,6},{8,9},{9,8},{10,11... | collective-permute-start | bytes 12296 | tf_op jit(solution)/shard_map/ppermute | solution.py:633
  41.0 10.1 %all-to-all-start = ((f32[16,4,128]{2,1,0:T(4,128)}), f32[16,4,128]{2,1,0:T(4,128)S(1)}, u32[]{:S(2)}, u32[]{:S(2)}) async-start(f32[16,4,128]{2,1,0:T(4,128)} %get-tuple-element.44), calls=%async_computation | async-start | bytes 65536 | tf_op jit(solution)/shard_map/all_to_all | solution.py:672
  44.5 3.8 %collective-permute-start.11 = (f32[8,4,128]{2,1,0:T(4,128)S(1)}, f32[8,4,128]{2,1,0:T(4,128)S(1)}, u32[]{:S(2)}, u32[]{:S(2)}) collective-permute-start(f32[8,4,128]{2,1,0:T(4,128)S(1)} %get-tuple-element.43), channel_id=1, source_target_pairs={{0,2},{2,0},{1,3},{3,1},{4,6},{6,4},{5,7},{7,5},{8,10},{10,8},{9,1... | collective-permute-start | bytes 49160 | tf_op jit(solution)/shard_map/ppermute | solution.py:671

commit v6 on v5

--- a/solution.py
+++ b/solution.py
@@ -68,11 +68,59 @@
 )
 
 
-def weights_kernel(p, dense_in, single_in, dense_out, first_out, last_out):
+def weights_kernel(p, dense_in, single_in, dense_out, first_out, last_out, arrivals):
     ch, yw, lanes = p.ch, p.yw, p.lanes
     half, wide = yw // 2, lanes // 2
 
-    for ref_in, ref_out in zip(dense_in, dense_out):
+    tile = (
+        jnp.bitwise_and(iota((ch, lanes), 1), ch - 1) == iota((ch, lanes), 0)
+    ).astype(F32).astype(BF)
+    tiled = [dot(ref[...], tile).astype(BF) for ref in single_in]
+
+    rows = 18 * yw
+    row = iota((rows, 1), 0)
+    yi = lax.rem(row, yw)
+    tx = lax.rem(lax.div(row, yw), 3)
+    tz = lax.rem(lax.div(row, 3 * yw), 3)
+    yo = lax.div(iota((rows, lanes), 1), ch)
+    for single, ref_out, direction in zip(tiled, first_out, (1, -1)):
+        total = jnp.zeros((rows, lanes), F32)
+        for ty in range(3):
+            number = 9 * tx + 3 * ty + tz
+            number = number if direction > 0 else 26 - number
+            pick = (iota((rows, 27), 1) == number).astype(F32).astype(BF)
+            here = lax.rem(yo + (ty - 1 + yw), yw) == yi
+            total = total + jnp.where(here, dot(pick, single), 0.0)
+        ref_out[...] = (0.5 * total).astype(BF)
+
+    rows = p.narrow
+    row = iota((rows, 1), 0)
+    yo = lax.rem(row, yw)
+    field = lax.rem(lax.div(row, yw), 4)
+    tx = lax.div(row, 4 * yw)
+    yi = lax.div(iota((rows, lanes), 1), ch)
+    for single, ref_out, direction in zip(tiled[::-1], last_out, (1, -1)):
+        for tz in range(3):
+            total = jnp.zeros((rows, lanes), F32)
+            for ty in range(3):
+                number = 9 * tx + 3 * ty + tz
+                number = number if direction > 0 else 26 - number
+                if direction > 0:
+                    factor = jnp.where(field == 0, 1, 0)
+                else:
+                    factor = jnp.where(
+                        field == 0,
+                        1,
+                        jnp.where(field == 1, 1 - tx, jnp.where(field == 2, 1 - ty, 1 - tz)),
+                    )
+                factor = jnp.where(tx < 3, factor, 0).astype(F32)
+                pick = jnp.where(iota((rows, 27), 1) == number, factor, 0.0).astype(BF)
+                here = lax.rem(yo + (ty - 1 + yw), yw) == yi
+                total = total + jnp.where(here, dot(pick, single), 0.0)
+            ref_out[tz] = total.astype(BF)
+
+    for ref_in, ref_out, arrive in zip(dense_in, dense_out, arrivals):
+        arrive()
         taps = []
         for ty in range(3):
             taps.append(
@@ -103,53 +151,6 @@
         ref_out[:, 0, :, :wide, wide:] = none
         ref_out[:, 1, :, wide:, :wide] = none
 
-    tile = (
-        jnp.bitwise_and(iota((ch, lanes), 1), ch - 1) == iota((ch, lanes), 0)
-    ).astype(F32).astype(BF)
-    tiled = [dot(ref[...], tile).astype(BF) for ref in single_in]
-
-    rows = 18 * yw
-    row = iota((rows, 1), 0)
-    yi = lax.rem(row, yw)
-    tx = lax.rem(lax.div(row, yw), 3)
-    tz = lax.rem(lax.div(row, 3 * yw), 3)
-    yo = lax.div(iota((rows, lanes), 1), ch)
-    for single, ref_out, direction in zip(tiled, first_out, (1, -1)):
-        total = jnp.zeros((rows, lanes), F32)
-        for ty in range(3):
-            number = 9 * tx + 3 * ty + tz
-            number = number if direction > 0 else 26 - number
-            pick = (iota((rows, 27), 1) == number).astype(F32).astype(BF)
-            here = lax.rem(yo + (ty - 1 + yw), yw) == yi
-            total = total + jnp.where(here, dot(pick, single), 0.0)
-        ref_out[...] = (0.5 * total).astype(BF)
-
-    rows = p.narrow
-    row = iota((rows, 1), 0)
-    yo = lax.rem(row, yw)
-    field = lax.rem(lax.div(row, yw), 4)
-    tx = lax.div(row, 4 * yw)
-    yi = lax.div(iota((rows, lanes), 1), ch)
-    for single, ref_out, direction in zip(tiled[::-1], last_out, (1, -1)):
-        for tz in range(3):
-            total = jnp.zeros((rows, lanes), F32)
-            for ty in range(3):
-                number = 9 * tx + 3 * ty + tz
-                number = number if direction > 0 else 26 - number
-                if direction > 0:
-                    factor = jnp.where(field == 0, 1, 0)
-                else:
-                    factor = jnp.where(
-                        field == 0,
-                        1,
-                        jnp.where(field == 1, 1 - tx, jnp.where(field == 2, 1 - ty, 1 - tz)),
-                    )
-                factor = jnp.where(tx < 3, factor, 0).astype(F32)
-                pick = (iota((rows, 27), 1) == number).astype(F32).astype(BF)
-                here = lax.rem(yo + (ty - 1 + yw), yw) == yi
-                total = total + jnp.where(here, dot(pick, single), 0.0) * factor
-            ref_out[tz] = total.astype(BF)
-
 
 def spread_weights(p, w_first, w_second, w_third, w_last):
     inputs = (w_second, w_third, w_first, w_last)
@@ -157,11 +158,12 @@
     def body(*refs):
         hbm, outs, held, sems = refs[:4], refs[4:10], refs[10:14], refs[14]
         copies = [pltpu.make_async_copy(hbm[i], held[i], sems.at[i]) for i in range(4)]
-        for copy in copies:
+        for copy in copies[::-1]:
             copy.start()
-        for copy in copies:
+        for copy in copies[2:]:
             copy.wait()
-        weights_kernel(p, held[:2], held[2:], outs[:2], outs[2:4], outs[4:])
+        arrivals = [copy.wait for copy in copies[:2]]
+        weights_kernel(p, held[:2], held[2:], outs[:2], outs[2:4], outs[4:], arrivals)
 
     dense = jax.ShapeDtypeStruct((2, 2, 3, p.lanes, p.lanes), BF)
     single = jax.ShapeDtypeStruct((18 * p.yw, p.lanes), BF)
@@ -526,7 +528,7 @@
 
     weights = spread_weights(p, w_first, w_second, w_third, w_last)
 
-    def widen_body(own_hbm, ext_hbm, left_ref, right_ref, o_wide, sems):
+    def widen_body(own_hbm, ext_hbm, left_ref, right_ref, o_wide, o_cells, sems):
         copies = [
             pltpu.make_async_copy(own_hbm, o_wide.at[REACH : REACH + nx], sems.at[0]),
             pltpu.make_async_copy(ext_hbm, o_wide.at[p.xe :], sems.at[1]),
@@ -537,12 +539,13 @@
         o_wide[REACH + nx : p.xe] = right_ref[:REACH]
         for copy in copies:
             copy.wait()
-
-    (wide,) = kernel_call(
+        o_cells[...] = o_wide[: p.xe]
+
+    wide, cells_wide = kernel_call(
         p,
         "widen",
         widen_body,
-        (f32(p.xe + nx, ny, nz),),
+        (f32(p.xe + nx, ny, nz), f32(p.xe, ny, nz)),
         0,
         2,
         [pltpu.SemaphoreType.DMA((2,))],
@@ -553,15 +556,15 @@
         along_x(density, -1),
     )
     from_y = lax.ppermute(wide, "gy", [(0, 1), (1, 0)])
-    from_z = lax.ppermute(wide, "gz", [(0, 1), (1, 0)])
-    from_yz = lax.ppermute(wide, ("gy", "gz"), [(i, 3 - i) for i in range(4)])
+    from_z = lax.ppermute(cells_wide, "gz", [(0, 1), (1, 0)])
+    from_yz = lax.ppermute(cells_wide, ("gy", "gz"), [(i, 3 - i) for i in range(4)])
     planes = p.xe + nx
 
     def first_body(own, y, z, yz, *refs):
         weight_refs, outs, tile, scratch = refs[:6], refs[6:11], refs[11], refs[12:]
         second = lax.axis_index("gy") == 1
         shift = jnp.where(second, nz - half + p.zh, p.zh)
-        lane = iota((planes, p.yw, lanes), 2)
+        lane = iota((p.xe, p.yw, lanes), 2)
         for ref, other in ((own, y), (z, yz)):
             mine, theirs = ref[...], other[...]
             lower = jnp.where(second, theirs, mine)
@@ -573,7 +576,7 @@
             else:
                 begin = jnp.where(second, half + p.zh, 0)
                 end = jnp.where(second, lanes, p.zh)
-                tile[...] = jnp.where((lane >= begin) & (lane < end), moved, tile[...])
+                tile[: p.xe] = jnp.where((lane >= begin) & (lane < end), moved, tile[: p.xe])
         cur = tile[: p.xe]
         ext = pltpu.roll(tile[p.xe :], lanes - p.zh, 2)
         _, weighted, sums = update_kernel(p, cur, ext, weight_refs, scratch)

time: 52.4 us -> 52.1 us (level)
    ppermute x1, waiting for transfers between devices: 1.24 us -> 0.01 us  [split_pairs(): from_y = lax.ppermute(wide, 'gy', [(0, 1), (1, 0)])]
    ppermute x1, starting transfers between devices: 0.49 us -> 1.61 us  [split_pairs(): from_y = lax.ppermute(wide, 'gy', [(0, 1), (1, 0)])]
    ppermute x2, starting transfers between devices: 1.71 us -> 0.6 us  [the longest x1 0.6 us: split_pairs(): from_z = lax.ppermute(cells_wide, 'gz', [(0, 1), (1, 0)])]
    ppermute x2, waiting for transfers between devices: 0.01 us -> 0.64 us  [the longest x1 0.63 us: split_pairs(): lax.ppermute(cells_wide, ('gy', 'gz'), [(i, 3 - i) for i in range(4)])]
  transfers between devices with their start and end apart: 13 -> 13, of which waited for: 9 -> 9; matrix products, arithmetic and copies ran while one was open for 0% -> 0% of each run, Pallas kernels for 5% -> 4%
where the time goes in v6:
time: 52.1 us; the launch traced here: 51.6 us
  starting transfers between devices  18.9 us (36%)
  Pallas kernels  17.5 us (34%)
  waiting for transfers between devices  14.3 us (27%)
  between operations  0.84 us (2%)
    ppermute x5, starting transfers between devices, along_x(): lax.ppermute(cells_out, 'gx', [(i, (i + step) % 4) for i in range(4)])  9.61 us
    pallas_call x1, Pallas kernels, split_pairs(): kernel_call(p, 'update_two', second_body, (share, share, f32(16, 4, 128),...  7.14 us
    pallas_call x1, Pallas kernels, split_pairs(): kernel_call(p, 'update_one', first_body, (f32(nx, p.yw, lanes), message,...  6.5 us
    ppermute x5, waiting for transfers between devices, along_x(): lax.ppermute(cells_out, 'gx', [(i, (i + step) % 4) for i in range(4)])  5.93 us
    all_to_all x1, starting transfers between devices, split_pairs(): gathered = lax.all_to_all(sums, axes, 0, 0, tiled=True)  3.49 us
    all_to_all x1, waiting for transfers between devices, split_pairs(): gathered = lax.all_to_all(sums, axes, 0, 0, tiled=True)  2.79 us
    pallas_call x1, Pallas kernels, spread_weights(): pl.pallas_call(body, name='spread_weights', out_shape=(dense,) * 2 + (sin...  2.27 us
    ppermute x1, waiting for transfers between devices, split_pairs(): other = lax.ppermute(send, 'gy', [(0, 1), (1, 0)])  1.99 us
  transfers between devices with their start and end apart: 13, of which 9 were waited for; matrix products, arithmetic and copies ran while one was open for 0% of the time, Pallas kernels for 4%

profile of v6, /device:TPU:0, one launch (start us, length us, event | category | flops | bytes accessed | tf_op | source)
XLA Modules:
  0.0 51.6 jit_solution(13270845422448434769)
XLA Ops:
  0.6 3.1 %collective-permute-start = (f32[8,4,128]{2,1,0:T(4,128)}, f32[8,4,128]{2,1,0:T(4,128)S(1)}, u32[]{:S(2)}, u32[]{:S(2)}) collective-permute-start(f32[8,4,128]{2,1,0:T(4,128)} %own_hbm.1), channel_id=1, source_target_pairs={{0,4},{4,8},{8,12},{12,0},{1,5},{5,9},{9,13},{13,1},{2,6},{6,10},{... | collective-permute-start | bytes 49160 | tf_op jit(solution)/shard_map/ppermute | solution.py:520
  3.7 2.1 %collective-permute-start.1 = (f32[8,4,128]{2,1,0:T(4,128)}, f32[8,4,128]{2,1,0:T(4,128)S(1)}, u32[]{:S(2)}, u32[]{:S(2)}) collective-permute-start(f32[8,4,128]{2,1,0:T(4,128)} %own_hbm.1), channel_id=1, source_target_pairs={{0,12},{4,0},{8,4},{12,8},{1,13},{5,1},{9,5},{13,9},{2,14},{6,2},{... | collective-permute-start | bytes 49160 | tf_op jit(solution)/shard_map/ppermute | solution.py:520
  5.8 2.0 %collective-permute-done.left_ref = f32[8,4,128]{2,1,0:T(4,128)S(1)} collective-permute-done((f32[8,4,128]{2,1,0:T(4,128)}, f32[8,4,128]{2,1,0:T(4,128)S(1)}, u32[]{:S(2)}, u32[]{:S(2)}) %collective-permute-start) | collective-permute-done | bytes 16416 | tf_op jit(solution)/shard_map/ppermute | solution.py:520
  7.8 0.1 collective-permute-done.1.right_ref
  7.8 0.8 %widen.1 = (f32[28,4,128]{2,1,0:T(4,128)S(1)}, f32[20,4,128]{2,1,0:T(4,128)S(1)}) custom-call(f32[8,4,128]{2,1,0:T(4,128)} %own_hbm.1, f32[8,4,128]{2,1,0:T(4,128)} %ext_hbm.1, f32[8,4,128]{2,1,0:T(4,128)S(1)} %collective-permute-done.left_ref, f32[8,4,128]{2,1,0:T(4,128)S(1)} %collective-permute-done.1.right_ref), custom_call_target="tpu_custom_call" | custom-call | tf_op jit(solution)/shard_map/widen/pallas_call | solution.py:544
  8.6 1.6 %collective-permute-start.2 = (f32[28,4,128]{2,1,0:T(4,128)S(1)}, f32[28,4,128]{2,1,0:T(4,128)S(1)}, u32[]{:S(2)}, u32[]{:S(2)}) collective-permute-start(f32[28,4,128]{2,1,0:T(4,128)S(1)} %get-tuple-element.29.own), channel_id=1, source_target_pairs={{0,2},{2,0},{1,3},{3,1},{4,6},{6,4},{5,7},{7,5},{8,10},{10,8},{9,1... | collective-permute-start | bytes 172040 | tf_op jit(solution)/shard_map/ppermute | solution.py:558
  10.2 0.0 collective-permute-start.4
  10.2 0.6 %collective-permute-start.3 = (f32[20,4,128]{2,1,0:T(4,128)S(1)}, f32[20,4,128]{2,1,0:T(4,128)S(1)}, u32[]{:S(2)}, u32[]{:S(2)}) collective-permute-start(f32[20,4,128]{2,1,0:T(4,128)S(1)} %get-tuple-element.30), channel_id=1, source_target_pairs={{0,1},{1,0},{2,3},{3,2},{4,5},{5,4},{6,7},{7,6},{8,9},{9,8},{10,11... | collective-permute-start | bytes 122888 | tf_op jit(solution)/shard_map/ppermute | solution.py:559
  10.8 2.3 %spread_weights.1 = (bf16[2,2,3,256,256]{4,3,2,1,0:T(8,128)(2,1)S(1)}, bf16[2,2,3,256,256]{4,3,2,1,0:T(8,128)(2,1)S(1)}, bf16[144,256]{1,0:T(8,128)(2,1)S(1)}, b...) custom-call(bf16[27,32,32]{2,1,0:T(8,128)(2,1)} %refs_0_.1, ...), custom_call_target="tpu_custom_call" | custom-call | flops 226492416 | bytes 3145728 | tf_op jit(solution)/shard_map/spread_weights/pallas_call | solution.py:172
  13.1 0.6 %collective-permute-done.4.yz = f32[20,4,128]{2,1,0:T(4,128)S(1)} collective-permute-done((f32[20,4,128]{2,1,0:T(4,128)S(1)}, f32[20,4,128]{2,1,0:T(4,128)S(1)}, u32[]{:S(2)}, u32[]{:S(2)}) %collective-permute-start.4) | collective-permute-done | bytes 40992 | tf_op jit(solution)/shard_map/ppermute | solution.py:560
  13.7 0.0 collective-permute-done.3.z
  13.7 0.0 collective-permute-done.2.y
  13.7 6.5 %update_one.1 = (f32[8,8,128]{2,1,0:T(8,128)S(1)}, f32[7,8,128]{2,1,0:T(8,128)S(1)}, f32[7,8,128]{2,1,0:T(8,128)S(1)}, f32[8,8,128]{2,1,0:T(8,128)S(1)}, f32[8,128]{1,0:T(8,128)S(1)}) custom-call(f32[28,4,128]{2,1,0:T(4,128)S(1)} %get-tuple-element.29.own, f32[28,4,128]{2,1,0:T(4,128)S(1)} %collective-permute-done.2.y, ...), custom_call_target="tpu_custom_call" | custom-call | flops 3271557120 | bytes 6291456 | tf_op jit(solution)/shard_map/update_one/pallas_call | solution.py:593
  20.2 1.4 %collective-permute-start.5 = (f32[7,8,128]{2,1,0:T(8,128)S(1)}, f32[7,8,128]{2,1,0:T(8,128)S(1)}, u32[]{:S(2)}, u32[]{:S(2)}) collective-permute-start(f32[7,8,128]{2,1,0:T(8,128)S(1)} %get-tuple-element.39), channel_id=1, source_target_pairs={{0,4},{4,8},{8,12},{12,0},{1,5},{5,9},{9,13},{13,1},{2,6},{6,10},{... | collective-permute-start | bytes 86024 | tf_op jit(solution)/shard_map/ppermute | solution.py:520
  21.6 2.4 %collective-permute-start.6 = (f32[7,8,128]{2,1,0:T(8,128)S(1)}, f32[7,8,128]{2,1,0:T(8,128)S(1)}, u32[]{:S(2)}, u32[]{:S(2)}) collective-permute-start(f32[7,8,128]{2,1,0:T(8,128)S(1)} %get-tuple-element.40), channel_id=1, source_target_pairs={{0,12},{4,0},{8,4},{12,8},{1,13},{5,1},{9,5},{13,9},{2,14},{6,2},{... | collective-permute-start | bytes 86024 | tf_op jit(solution)/shard_map/ppermute | solution.py:520
  24.1 0.6 %collective-permute-start.7 = (f32[8,128]{1,0:T(8,128)S(1)}, f32[8,128]{1,0:T(8,128)S(1)}, u32[]{:S(2)}, u32[]{:S(2)}) collective-permute-start(f32[8,128]{1,0:T(8,128)S(1)} %get-tuple-element.38.sums_ref), channel_id=1, source_target_pairs={{0,8},{4,12},{8,0},{12,4},{1,9},{5,13},{9,1},{13,5},{2,10},{6,14},... | collective-permute-start | bytes 12296 | tf_op jit(solution)/shard_map/ppermute | solution.py:520
  24.7 3.9 %collective-permute-done.7.far_ref = f32[8,128]{1,0:T(8,128)S(1)} collective-permute-done((f32[8,128]{1,0:T(8,128)S(1)}, f32[8,128]{1,0:T(8,128)S(1)}, u32[]{:S(2)}, u32[]{:S(2)}) %collective-permute-start.7) | collective-permute-done | bytes 4128 | tf_op jit(solution)/shard_map/ppermute | solution.py:520
  28.6 0.0 collective-permute-done.5.left_ref
  28.6 0.0 collective-permute-done.6.right_ref
  28.6 0.1 join.1
  28.7 1.1 %collective-permute-start.8 = (f32[4,8,128]{2,1,0:T(8,128)S(1)}, f32[4,8,128]{2,1,0:T(8,128)S(1)}, u32[]{:S(2)}, u32[]{:S(2)}) collective-permute-start(f32[4,8,128]{2,1,0:T(8,128)S(1)} %get-tuple-element.42), channel_id=1, source_target_pairs={{0,2},{2,1},{1,3},{3,0},{4,6},{6,5},{5,7},{7,4},{8,10},{10,9},{9,1... | collective-permute-start | bytes 49160 | tf_op jit(solution)/shard_map/ppermute | solution.py:527
  29.7 0.7 %collective-permute-start.9 = (f32[4,8,128]{2,1,0:T(8,128)S(1)}, f32[4,8,128]{2,1,0:T(8,128)S(1)}, u32[]{:S(2)}, u32[]{:S(2)}) collective-permute-start(f32[4,8,128]{2,1,0:T(8,128)S(1)} %get-tuple-element.43), channel_id=1, source_target_pairs={{0,3},{2,0},{1,2},{3,1},{4,7},{6,4},{5,6},{7,5},{8,11},{10,8},{9,1... | collective-permute-start | bytes 49160 | tf_op jit(solution)/shard_map/ppermute | solution.py:527
  30.5 0.0 collective-permute-start.10
  30.5 1.2 %collective-permute-done.10.across_ref = f32[8,128]{1,0:T(8,128)S(1)} collective-permute-done((f32[8,128]{1,0:T(8,128)S(1)}, f32[8,128]{1,0:T(8,128)S(1)}, u32[]{:S(2)}, u32[]{:S(2)}) %collective-permute-start.10) | collective-permute-done | bytes 4128 | tf_op jit(solution)/shard_map/ppermute | solution.py:636
  31.6 0.2 collective-permute-done.8.below_ref
  31.9 1.6 %collective-permute-done.9.above_ref = f32[4,8,128]{2,1,0:T(8,128)S(1)} collective-permute-done((f32[4,8,128]{2,1,0:T(8,128)S(1)}, f32[4,8,128]{2,1,0:T(8,128)S(1)}, u32[]{:S(2)}, u32[]{:S(2)}) %collective-permute-start.9) | collective-permute-done | bytes 16416 | tf_op jit(solution)/shard_map/ppermute | solution.py:527
  33.5 7.1 %update_two.1 = (f32[8,4,128]{2,1,0:T(4,128)S(1)}, f32[8,4,128]{2,1,0:T(4,128)S(1)}, f32[16,4,128]{2,1,0:T(4,128)}, f32[8,128]{1,0:T(8,128)S(1)}) custom-call(f32[20,8,128]{2,1,0:T(8,128)S(1)} %get-tuple-element.41.tile_ref, f32[4,8,128]{2,1,0:T(8,128)S(1)} %collective-permute-done.8.below_ref, f32[4,8,128]{2,1,0:T(8,128)S(1)} %collective-permute-done.9.above_ref, ...), custom_call_target="tpu_custom_call" | custom-call | flops 3271557120 | bytes 6291456 | tf_op jit(solution)/shard_map/update_two/pallas_call | solution.py:663
  40.6 3.5 %all-to-all-start = ((f32[16,4,128]{2,1,0:T(4,128)}), f32[16,4,128]{2,1,0:T(4,128)S(1)}, u32[]{:S(2)}, u32[]{:S(2)}) async-start(f32[16,4,128]{2,1,0:T(4,128)} %get-tuple-element.48), calls=%async_computation | async-start | bytes 65536 | tf_op jit(solution)/shard_map/all_to_all | solution.py:675
  44.1 1.8 %collective-permute-start.11 = (f32[8,4,128]{2,1,0:T(4,128)S(1)}, f32[8,4,128]{2,1,0:T(4,128)S(1)}, u32[]{:S(2)}, u32[]{:S(2)}) collective-permute-start(f32[8,4,128]{2,1,0:T(4,128)S(1)} %get-tuple-element.47), channel_id=1, source_target_pairs={{0,2},{2,0},{1,3},{3,1},{4,6},{6,4},{5,7},{7,5},{8,10},{10,8},{9,1... | collective-permute-start | bytes 49160 | tf_op jit(solution)/shard_map/ppermute | solution.py:674
  45.9 2.0 %collective-permute-done.11.other_ref = f32[8,4,128]{2,1,0:T(4,128)S(1)} collective-permute-done((f32[8,4,128]{2,1,0:T(4,128)S(1)}, f32[8,4,128]{2,1,0:T(4,128)S(1)}, u32[]{:S(2)}, u32[]{:S(2)}) %collective-permute-start.11) | collective-permute-done | bytes 16416 | tf_op jit(solution)/shard_map/ppermute | solution.py:674
  47.9 2.8 %all-to-all-done.all_ref = f32[16,4,128]{2,1,0:T(4,128)S(1)} async-done(((f32[16,4,128]{2,1,0:T(4,128)}), f32[16,4,128]{2,1,0:T(4,128)S(1)}, u32[]{:S(2)}, u32[]{:S(2)}) %all-to-all-start) | async-done | bytes 32800 | tf_op jit(solution)/shard_map/all_to_all | solution.py:675
  50.7 0.8 %finish.1 = (f32[8,4,128]{2,1,0:T(4,128)}, f32[8,4,128]{2,1,0:T(4,128)}, f32[2]{0:T(128)}, f32[3,2,3]{2,1,0:T(2,128)}) custom-call(f32[8,4,128]{2,1,0:T(4,128)S(1)} %get-tuple-element.46.keep_ref, f32[8,4,128]{2,1,0:T(4,128)S(1)} %collective-permute-done.11.other_ref, f32[16,4,128]{2,1,0:T(4,128)S(1)} %all-to-all-done.all_ref, ...), custom_call_target="tpu_custom_call" | custom-call | tf_op jit(solution)/shard_map/finish/pallas_call | solution.py:699
Async XLA Ops:
  0.6 7.1 %collective-permute-start = (f32[8,4,128]{2,1,0:T(4,128)}, f32[8,4,128]{2,1,0:T(4,128)S(1)}, u32[]{:S(2)}, u32[]{:S(2)}) collective-permute-start(f32[8,4,128]{2,1,0:T(4,128)} %own_hbm.1), channel_id=1, source_target_pairs={{0,4},{4,8},{8,12},{12,0},{1,5},{5,9},{9,13},{13,1},{2,6},{6,10},{... | collective-permute-start | bytes 49160 | tf_op jit(solution)/shard_map/ppermute | solution.py:520
  3.7 4.1 %collective-permute-start.1 = (f32[8,4,128]{2,1,0:T(4,128)}, f32[8,4,128]{2,1,0:T(4,128)S(1)}, u32[]{:S(2)}, u32[]{:S(2)}) collective-permute-start(f32[8,4,128]{2,1,0:T(4,128)} %own_hbm.1), channel_id=1, source_target_pairs={{0,12},{4,0},{8,4},{12,8},{1,13},{5,1},{9,5},{13,9},{2,14},{6,2},{... | collective-permute-start | bytes 49160 | tf_op jit(solution)/shard_map/ppermute | solution.py:520
  8.6 5.1 %collective-permute-start.2 = (f32[28,4,128]{2,1,0:T(4,128)S(1)}, f32[28,4,128]{2,1,0:T(4,128)S(1)}, u32[]{:S(2)}, u32[]{:S(2)}) collective-permute-start(f32[28,4,128]{2,1,0:T(4,128)S(1)} %get-tuple-element.29.own), channel_id=1, source_target_pairs={{0,2},{2,0},{1,3},{3,1},{4,6},{6,4},{5,7},{7,5},{8,10},{10,8},{9,1... | collective-permute-start | bytes 172040 | tf_op jit(solution)/shard_map/ppermute | solution.py:558
  10.2 3.5 %collective-permute-start.4 = (f32[20,4,128]{2,1,0:T(4,128)S(1)}, f32[20,4,128]{2,1,0:T(4,128)S(1)}, u32[]{:S(2)}, u32[]{:S(2)}) collective-permute-start(f32[20,4,128]{2,1,0:T(4,128)S(1)} %get-tuple-element.30), channel_id=1, source_target_pairs={{0,3},{1,2},{2,1},{3,0},{4,7},{5,6},{6,5},{7,4},{8,11},{9,10},{10,... | collective-permute-start | bytes 122888 | tf_op jit(solution)/shard_map/ppermute | solution.py:560
  10.2 3.5 %collective-permute-start.3 = (f32[20,4,128]{2,1,0:T(4,128)S(1)}, f32[20,4,128]{2,1,0:T(4,128)S(1)}, u32[]{:S(2)}, u32[]{:S(2)}) collective-permute-start(f32[20,4,128]{2,1,0:T(4,128)S(1)} %get-tuple-element.30), channel_id=1, source_target_pairs={{0,1},{1,0},{2,3},{3,2},{4,5},{5,4},{6,7},{7,6},{8,9},{9,8},{10,11... | collective-permute-start | bytes 122888 | tf_op jit(solution)/shard_map/ppermute | solution.py:559
  20.2 8.3 %collective-permute-start.5 = (f32[7,8,128]{2,1,0:T(8,128)S(1)}, f32[7,8,128]{2,1,0:T(8,128)S(1)}, u32[]{:S(2)}, u32[]{:S(2)}) collective-permute-start(f32[7,8,128]{2,1,0:T(8,128)S(1)} %get-tuple-element.39), channel_id=1, source_target_pairs={{0,4},{4,8},{8,12},{12,0},{1,5},{5,9},{9,13},{13,1},{2,6},{6,10},{... | collective-permute-start | bytes 86024 | tf_op jit(solution)/shard_map/ppermute | solution.py:520
  21.6 6.9 %collective-permute-start.6 = (f32[7,8,128]{2,1,0:T(8,128)S(1)}, f32[7,8,128]{2,1,0:T(8,128)S(1)}, u32[]{:S(2)}, u32[]{:S(2)}) collective-permute-start(f32[7,8,128]{2,1,0:T(8,128)S(1)} %get-tuple-element.40), channel_id=1, source_target_pairs={{0,12},{4,0},{8,4},{12,8},{1,13},{5,1},{9,5},{13,9},{2,14},{6,2},{... | collective-permute-start | bytes 86024 | tf_op jit(solution)/shard_map/ppermute | solution.py:520
  24.1 4.5 %collective-permute-start.7 = (f32[8,128]{1,0:T(8,128)S(1)}, f32[8,128]{1,0:T(8,128)S(1)}, u32[]{:S(2)}, u32[]{:S(2)}) collective-permute-start(f32[8,128]{1,0:T(8,128)S(1)} %get-tuple-element.38.sums_ref), channel_id=1, source_target_pairs={{0,8},{4,12},{8,0},{12,4},{1,9},{5,13},{9,1},{13,5},{2,10},{6,14},... | collective-permute-start | bytes 12296 | tf_op jit(solution)/shard_map/ppermute | solution.py:520
  28.7 3.2 %collective-permute-start.8 = (f32[4,8,128]{2,1,0:T(8,128)S(1)}, f32[4,8,128]{2,1,0:T(8,128)S(1)}, u32[]{:S(2)}, u32[]{:S(2)}) collective-permute-start(f32[4,8,128]{2,1,0:T(8,128)S(1)} %get-tuple-element.42), channel_id=1, source_target_pairs={{0,2},{2,1},{1,3},{3,0},{4,6},{6,5},{5,7},{7,4},{8,10},{10,9},{9,1... | collective-permute-start | bytes 49160 | tf_op jit(solution)/shard_map/ppermute | solution.py:527
  29.7 3.7 %collective-permute-start.9 = (f32[4,8,128]{2,1,0:T(8,128)S(1)}, f32[4,8,128]{2,1,0:T(8,128)S(1)}, u32[]{:S(2)}, u32[]{:S(2)}) collective-permute-start(f32[4,8,128]{2,1,0:T(8,128)S(1)} %get-tuple-element.43), channel_id=1, source_target_pairs={{0,3},{2,0},{1,2},{3,1},{4,7},{6,4},{5,6},{7,5},{8,11},{10,8},{9,1... | collective-permute-start | bytes 49160 | tf_op jit(solution)/shard_map/ppermute | solution.py:527
  30.5 1.2 %collective-permute-start.10 = (f32[8,128]{1,0:T(8,128)S(1)}, f32[8,128]{1,0:T(8,128)S(1)}, u32[]{:S(2)}, u32[]{:S(2)}) collective-permute-start(f32[8,128]{1,0:T(8,128)S(1)} %get-tuple-element.44.sums_ref), channel_id=1, source_target_pairs={{0,1},{1,0},{2,3},{3,2},{4,5},{5,4},{6,7},{7,6},{8,9},{9,8},{10,11... | collective-permute-start | bytes 12296 | tf_op jit(solution)/shard_map/ppermute | solution.py:636
  40.6 10.1 %all-to-all-start = ((f32[16,4,128]{2,1,0:T(4,128)}), f32[16,4,128]{2,1,0:T(4,128)S(1)}, u32[]{:S(2)}, u32[]{:S(2)}) async-start(f32[16,4,128]{2,1,0:T(4,128)} %get-tuple-element.48), calls=%async_computation | async-start | bytes 65536 | tf_op jit(solution)/shard_map/all_to_all | solution.py:675
  44.1 3.8 %collective-permute-start.11 = (f32[8,4,128]{2,1,0:T(4,128)S(1)}, f32[8,4,128]{2,1,0:T(4,128)S(1)}, u32[]{:S(2)}, u32[]{:S(2)}) collective-permute-start(f32[8,4,128]{2,1,0:T(4,128)S(1)} %get-tuple-element.47), channel_id=1, source_target_pairs={{0,2},{2,0},{1,3},{3,1},{4,6},{6,4},{5,7},{7,5},{8,10},{10,8},{9,1... | collective-permute-start | bytes 49160 | tf_op jit(solution)/shard_map/ppermute | solution.py:674

commit v7 on v6

--- a/solution.py
+++ b/solution.py
@@ -650,7 +650,7 @@
             joined = jnp.where(lane < p.zh, lower, jnp.where(lane < p.zh + half, middle, top))
             cur[x] = joined * scale
         pot, weighted, sums_here = update_kernel(p, cur[...], ext_ref[...], weight_refs, scratch)
-        o_sums[...] = jnp.broadcast_to(sums_here[:4], (16, 4, 128))
+        o_sums[...] = jnp.broadcast_to(sums_here[:2], (16, 2, 128))
         both = jnp.where(
             iota(pot.shape, 2) < half, pot, pltpu.roll(weighted, half, 2)
         )
@@ -664,7 +664,7 @@
         p,
         "update_two",
         second_body,
-        (share, share, f32(16, 4, 128), f32(8, 128)),
+        (share, share, f32(16, 2, 128), f32(8, 128)),
         0,
         12,
         [pltpu.VMEM((p.xe, p.yw, lanes), F32)] + update_scratch(p),
@@ -677,7 +677,7 @@
     def last_body(keep_ref, other_ref, all_ref, totals_ref, o_new, o_pot, o_chem, o_stress):
         first = totals_ref[...]
         last = jnp.sum(all_ref[...], axis=0)
-        last = jnp.concatenate([last, last], axis=0)
+        last = jnp.concatenate([last] * 4, axis=0)
         mass = pick(first, 1)
         scale = mass / pick(last, 0)
         second = lax.axis_index("gy") == 1

time: 52.1 us -> 51.9 us (level)
  no operation moved by 1% of the time
where the time goes in v7:
time: 51.9 us; the launch traced here: 51.5 us
  starting transfers between devices  18.9 us (36%)
  Pallas kernels  17.5 us (34%)
  waiting for transfers between devices  14.2 us (27%)
  between operations  0.84 us (2%)
    ppermute x5, starting transfers between devices, along_x(): lax.ppermute(cells_out, 'gx', [(i, (i + step) % 4) for i in range(4)])  9.61 us
    pallas_call x1, Pallas kernels, split_pairs(): kernel_call(p, 'update_two', second_body, (share, share, f32(16, 2, 128),...  7.14 us
    pallas_call x1, Pallas kernels, split_pairs(): kernel_call(p, 'update_one', first_body, (f32(nx, p.yw, lanes), message,...  6.5 us
    ppermute x5, waiting for transfers between devices, along_x(): lax.ppermute(cells_out, 'gx', [(i, (i + step) % 4) for i in range(4)])  5.93 us
    all_to_all x1, starting transfers between devices, split_pairs(): gathered = lax.all_to_all(sums, axes, 0, 0, tiled=True)  3.49 us
    all_to_all x1, waiting for transfers between devices, split_pairs(): gathered = lax.all_to_all(sums, axes, 0, 0, tiled=True)  2.65 us
    pallas_call x1, Pallas kernels, spread_weights(): pl.pallas_call(body, name='spread_weights', out_shape=(dense,) * 2 + (sin...  2.27 us
    ppermute x1, waiting for transfers between devices, split_pairs(): other = lax.ppermute(send, 'gy', [(0, 1), (1, 0)])  1.99 us
  transfers between devices with their start and end apart: 13, of which 9 were waited for; matrix products, arithmetic and copies ran while one was open for 0% of the time, Pallas kernels for 4%

profile of v7, /device:TPU:0, one launch (start us, length us, event | category | flops | bytes accessed | tf_op | source)
XLA Modules:
  0.0 51.5 jit_solution(15403261269822866857)
XLA Ops:
  0.6 3.1 %collective-permute-start = (f32[8,4,128]{2,1,0:T(4,128)}, f32[8,4,128]{2,1,0:T(4,128)S(1)}, u32[]{:S(2)}, u32[]{:S(2)}) collective-permute-start(f32[8,4,128]{2,1,0:T(4,128)} %own_hbm.1), channel_id=1, source_target_pairs={{0,4},{4,8},{8,12},{12,0},{1,5},{5,9},{9,13},{13,1},{2,6},{6,10},{... | collective-permute-start | bytes 49160 | tf_op jit(solution)/shard_map/ppermute | solution.py:520
  3.7 2.1 %collective-permute-start.1 = (f32[8,4,128]{2,1,0:T(4,128)}, f32[8,4,128]{2,1,0:T(4,128)S(1)}, u32[]{:S(2)}, u32[]{:S(2)}) collective-permute-start(f32[8,4,128]{2,1,0:T(4,128)} %own_hbm.1), channel_id=1, source_target_pairs={{0,12},{4,0},{8,4},{12,8},{1,13},{5,1},{9,5},{13,9},{2,14},{6,2},{... | collective-permute-start | bytes 49160 | tf_op jit(solution)/shard_map/ppermute | solution.py:520
  5.8 2.0 %collective-permute-done.left_ref = f32[8,4,128]{2,1,0:T(4,128)S(1)} collective-permute-done((f32[8,4,128]{2,1,0:T(4,128)}, f32[8,4,128]{2,1,0:T(4,128)S(1)}, u32[]{:S(2)}, u32[]{:S(2)}) %collective-permute-start) | collective-permute-done | bytes 16416 | tf_op jit(solution)/shard_map/ppermute | solution.py:520
  7.8 0.1 collective-permute-done.1.right_ref
  7.8 0.8 %widen.1 = (f32[28,4,128]{2,1,0:T(4,128)S(1)}, f32[20,4,128]{2,1,0:T(4,128)S(1)}) custom-call(f32[8,4,128]{2,1,0:T(4,128)} %own_hbm.1, f32[8,4,128]{2,1,0:T(4,128)} %ext_hbm.1, f32[8,4,128]{2,1,0:T(4,128)S(1)} %collective-permute-done.left_ref, f32[8,4,128]{2,1,0:T(4,128)S(1)} %collective-permute-done.1.right_ref), custom_call_target="tpu_custom_call" | custom-call | tf_op jit(solution)/shard_map/widen/pallas_call | solution.py:544
  8.6 1.6 %collective-permute-start.2 = (f32[28,4,128]{2,1,0:T(4,128)S(1)}, f32[28,4,128]{2,1,0:T(4,128)S(1)}, u32[]{:S(2)}, u32[]{:S(2)}) collective-permute-start(f32[28,4,128]{2,1,0:T(4,128)S(1)} %get-tuple-element.29.own), channel_id=1, source_target_pairs={{0,2},{2,0},{1,3},{3,1},{4,6},{6,4},{5,7},{7,5},{8,10},{10,8},{9,1... | collective-permute-start | bytes 172040 | tf_op jit(solution)/shard_map/ppermute | solution.py:558
  10.2 0.0 collective-permute-start.4
  10.2 0.6 %collective-permute-start.3 = (f32[20,4,128]{2,1,0:T(4,128)S(1)}, f32[20,4,128]{2,1,0:T(4,128)S(1)}, u32[]{:S(2)}, u32[]{:S(2)}) collective-permute-start(f32[20,4,128]{2,1,0:T(4,128)S(1)} %get-tuple-element.30), channel_id=1, source_target_pairs={{0,1},{1,0},{2,3},{3,2},{4,5},{5,4},{6,7},{7,6},{8,9},{9,8},{10,11... | collective-permute-start | bytes 122888 | tf_op jit(solution)/shard_map/ppermute | solution.py:559
  10.8 2.3 %spread_weights.1 = (bf16[2,2,3,256,256]{4,3,2,1,0:T(8,128)(2,1)S(1)}, bf16[2,2,3,256,256]{4,3,2,1,0:T(8,128)(2,1)S(1)}, bf16[144,256]{1,0:T(8,128)(2,1)S(1)}, b...) custom-call(bf16[27,32,32]{2,1,0:T(8,128)(2,1)} %refs_0_.1, ...), custom_call_target="tpu_custom_call" | custom-call | flops 226492416 | bytes 3145728 | tf_op jit(solution)/shard_map/spread_weights/pallas_call | solution.py:172
  13.1 0.6 %collective-permute-done.4.yz = f32[20,4,128]{2,1,0:T(4,128)S(1)} collective-permute-done((f32[20,4,128]{2,1,0:T(4,128)S(1)}, f32[20,4,128]{2,1,0:T(4,128)S(1)}, u32[]{:S(2)}, u32[]{:S(2)}) %collective-permute-start.4) | collective-permute-done | bytes 40992 | tf_op jit(solution)/shard_map/ppermute | solution.py:560
  13.7 0.0 collective-permute-done.3.z
  13.7 0.0 collective-permute-done.2.y
  13.7 6.5 %update_one.1 = (f32[8,8,128]{2,1,0:T(8,128)S(1)}, f32[7,8,128]{2,1,0:T(8,128)S(1)}, f32[7,8,128]{2,1,0:T(8,128)S(1)}, f32[8,8,128]{2,1,0:T(8,128)S(1)}, f32[8,128]{1,0:T(8,128)S(1)}) custom-call(f32[28,4,128]{2,1,0:T(4,128)S(1)} %get-tuple-element.29.own, f32[28,4,128]{2,1,0:T(4,128)S(1)} %collective-permute-done.2.y, ...), custom_call_target="tpu_custom_call" | custom-call | flops 3271557120 | bytes 6291456 | tf_op jit(solution)/shard_map/update_one/pallas_call | solution.py:593
  20.2 1.4 %collective-permute-start.5 = (f32[7,8,128]{2,1,0:T(8,128)S(1)}, f32[7,8,128]{2,1,0:T(8,128)S(1)}, u32[]{:S(2)}, u32[]{:S(2)}) collective-permute-start(f32[7,8,128]{2,1,0:T(8,128)S(1)} %get-tuple-element.39), channel_id=1, source_target_pairs={{0,4},{4,8},{8,12},{12,0},{1,5},{5,9},{9,13},{13,1},{2,6},{6,10},{... | collective-permute-start | bytes 86024 | tf_op jit(solution)/shard_map/ppermute | solution.py:520
  21.6 2.4 %collective-permute-start.6 = (f32[7,8,128]{2,1,0:T(8,128)S(1)}, f32[7,8,128]{2,1,0:T(8,128)S(1)}, u32[]{:S(2)}, u32[]{:S(2)}) collective-permute-start(f32[7,8,128]{2,1,0:T(8,128)S(1)} %get-tuple-element.40), channel_id=1, source_target_pairs={{0,12},{4,0},{8,4},{12,8},{1,13},{5,1},{9,5},{13,9},{2,14},{6,2},{... | collective-permute-start | bytes 86024 | tf_op jit(solution)/shard_map/ppermute | solution.py:520
  24.1 0.6 %collective-permute-start.7 = (f32[8,128]{1,0:T(8,128)S(1)}, f32[8,128]{1,0:T(8,128)S(1)}, u32[]{:S(2)}, u32[]{:S(2)}) collective-permute-start(f32[8,128]{1,0:T(8,128)S(1)} %get-tuple-element.38.sums_ref), channel_id=1, source_target_pairs={{0,8},{4,12},{8,0},{12,4},{1,9},{5,13},{9,1},{13,5},{2,10},{6,14},... | collective-permute-start | bytes 12296 | tf_op jit(solution)/shard_map/ppermute | solution.py:520
  24.7 3.9 %collective-permute-done.7.far_ref = f32[8,128]{1,0:T(8,128)S(1)} collective-permute-done((f32[8,128]{1,0:T(8,128)S(1)}, f32[8,128]{1,0:T(8,128)S(1)}, u32[]{:S(2)}, u32[]{:S(2)}) %collective-permute-start.7) | collective-permute-done | bytes 4128 | tf_op jit(solution)/shard_map/ppermute | solution.py:520
  28.6 0.0 collective-permute-done.5.left_ref
  28.6 0.0 collective-permute-done.6.right_ref
  28.6 0.1 join.1
  28.7 1.1 %collective-permute-start.8 = (f32[4,8,128]{2,1,0:T(8,128)S(1)}, f32[4,8,128]{2,1,0:T(8,128)S(1)}, u32[]{:S(2)}, u32[]{:S(2)}) collective-permute-start(f32[4,8,128]{2,1,0:T(8,128)S(1)} %get-tuple-element.42), channel_id=1, source_target_pairs={{0,2},{2,1},{1,3},{3,0},{4,6},{6,5},{5,7},{7,4},{8,10},{10,9},{9,1... | collective-permute-start | bytes 49160 | tf_op jit(solution)/shard_map/ppermute | solution.py:527
  29.7 0.7 %collective-permute-start.9 = (f32[4,8,128]{2,1,0:T(8,128)S(1)}, f32[4,8,128]{2,1,0:T(8,128)S(1)}, u32[]{:S(2)}, u32[]{:S(2)}) collective-permute-start(f32[4,8,128]{2,1,0:T(8,128)S(1)} %get-tuple-element.43), channel_id=1, source_target_pairs={{0,3},{2,0},{1,2},{3,1},{4,7},{6,4},{5,6},{7,5},{8,11},{10,8},{9,1... | collective-permute-start | bytes 49160 | tf_op jit(solution)/shard_map/ppermute | solution.py:527
  30.5 0.0 collective-permute-start.10
  30.5 1.2 %collective-permute-done.10.across_ref = f32[8,128]{1,0:T(8,128)S(1)} collective-permute-done((f32[8,128]{1,0:T(8,128)S(1)}, f32[8,128]{1,0:T(8,128)S(1)}, u32[]{:S(2)}, u32[]{:S(2)}) %collective-permute-start.10) | collective-permute-done | bytes 4128 | tf_op jit(solution)/shard_map/ppermute | solution.py:636
  31.6 0.2 collective-permute-done.8.below_ref
  31.9 1.6 %collective-permute-done.9.above_ref = f32[4,8,128]{2,1,0:T(8,128)S(1)} collective-permute-done((f32[4,8,128]{2,1,0:T(8,128)S(1)}, f32[4,8,128]{2,1,0:T(8,128)S(1)}, u32[]{:S(2)}, u32[]{:S(2)}) %collective-permute-start.9) | collective-permute-done | bytes 16416 | tf_op jit(solution)/shard_map/ppermute | solution.py:527
  33.5 7.1 %update_two.1 = (f32[8,4,128]{2,1,0:T(4,128)S(1)}, f32[8,4,128]{2,1,0:T(4,128)S(1)}, f32[16,2,128]{2,1,0:T(2,128)}, f32[8,128]{1,0:T(8,128)S(1)}) custom-call(f32[20,8,128]{2,1,0:T(8,128)S(1)} %get-tuple-element.41.tile_ref, f32[4,8,128]{2,1,0:T(8,128)S(1)} %collective-permute-done.8.below_ref, f32[4,8,128]{2,1,0:T(8,128)S(1)} %collective-permute-done.9.above_ref, ...), custom_call_target="tpu_custom_call" | custom-call | flops 3271557120 | bytes 6291456 | tf_op jit(solution)/shard_map/update_two/pallas_call | solution.py:663
  40.6 3.5 %all-to-all-start = ((f32[16,2,128]{2,1,0:T(2,128)}), f32[16,2,128]{2,1,0:T(2,128)S(1)}, u32[]{:S(2)}, u32[]{:S(2)}) async-start(f32[16,2,128]{2,1,0:T(2,128)} %get-tuple-element.48), calls=%async_computation | async-start | bytes 32768 | tf_op jit(solution)/shard_map/all_to_all | solution.py:675
  44.1 1.8 %collective-permute-start.11 = (f32[8,4,128]{2,1,0:T(4,128)S(1)}, f32[8,4,128]{2,1,0:T(4,128)S(1)}, u32[]{:S(2)}, u32[]{:S(2)}) collective-permute-start(f32[8,4,128]{2,1,0:T(4,128)S(1)} %get-tuple-element.47), channel_id=1, source_target_pairs={{0,2},{2,0},{1,3},{3,1},{4,6},{6,4},{5,7},{7,5},{8,10},{10,8},{9,1... | collective-permute-start | bytes 49160 | tf_op jit(solution)/shard_map/ppermute | solution.py:674
  45.9 2.0 %collective-permute-done.11.other_ref = f32[8,4,128]{2,1,0:T(4,128)S(1)} collective-permute-done((f32[8,4,128]{2,1,0:T(4,128)S(1)}, f32[8,4,128]{2,1,0:T(4,128)S(1)}, u32[]{:S(2)}, u32[]{:S(2)}) %collective-permute-start.11) | collective-permute-done | bytes 16416 | tf_op jit(solution)/shard_map/ppermute | solution.py:674
  47.9 2.7 %all-to-all-done.all_ref = f32[16,2,128]{2,1,0:T(2,128)S(1)} async-done(((f32[16,2,128]{2,1,0:T(2,128)}), f32[16,2,128]{2,1,0:T(2,128)S(1)}, u32[]{:S(2)}, u32[]{:S(2)}) %all-to-all-start) | async-done | bytes 16416 | tf_op jit(solution)/shard_map/all_to_all | solution.py:675
  50.6 0.8 %finish.1 = (f32[8,4,128]{2,1,0:T(4,128)}, f32[8,4,128]{2,1,0:T(4,128)}, f32[2]{0:T(128)}, f32[3,2,3]{2,1,0:T(2,128)}) custom-call(f32[8,4,128]{2,1,0:T(4,128)S(1)} %get-tuple-element.46.keep_ref, f32[8,4,128]{2,1,0:T(4,128)S(1)} %collective-permute-done.11.other_ref, f32[16,2,128]{2,1,0:T(2,128)S(1)} %all-to-all-done.all_ref, ...), custom_call_target="tpu_custom_call" | custom-call | tf_op jit(solution)/shard_map/finish/pallas_call | solution.py:699
Async XLA Ops:
  0.6 7.1 %collective-permute-start = (f32[8,4,128]{2,1,0:T(4,128)}, f32[8,4,128]{2,1,0:T(4,128)S(1)}, u32[]{:S(2)}, u32[]{:S(2)}) collective-permute-start(f32[8,4,128]{2,1,0:T(4,128)} %own_hbm.1), channel_id=1, source_target_pairs={{0,4},{4,8},{8,12},{12,0},{1,5},{5,9},{9,13},{13,1},{2,6},{6,10},{... | collective-permute-start | bytes 49160 | tf_op jit(solution)/shard_map/ppermute | solution.py:520
  3.7 4.1 %collective-permute-start.1 = (f32[8,4,128]{2,1,0:T(4,128)}, f32[8,4,128]{2,1,0:T(4,128)S(1)}, u32[]{:S(2)}, u32[]{:S(2)}) collective-permute-start(f32[8,4,128]{2,1,0:T(4,128)} %own_hbm.1), channel_id=1, source_target_pairs={{0,12},{4,0},{8,4},{12,8},{1,13},{5,1},{9,5},{13,9},{2,14},{6,2},{... | collective-permute-start | bytes 49160 | tf_op jit(solution)/shard_map/ppermute | solution.py:520
  8.6 5.1 %collective-permute-start.2 = (f32[28,4,128]{2,1,0:T(4,128)S(1)}, f32[28,4,128]{2,1,0:T(4,128)S(1)}, u32[]{:S(2)}, u32[]{:S(2)}) collective-permute-start(f32[28,4,128]{2,1,0:T(4,128)S(1)} %get-tuple-element.29.own), channel_id=1, source_target_pairs={{0,2},{2,0},{1,3},{3,1},{4,6},{6,4},{5,7},{7,5},{8,10},{10,8},{9,1... | collective-permute-start | bytes 172040 | tf_op jit(solution)/shard_map/ppermute | solution.py:558
  10.2 3.5 %collective-permute-start.4 = (f32[20,4,128]{2,1,0:T(4,128)S(1)}, f32[20,4,128]{2,1,0:T(4,128)S(1)}, u32[]{:S(2)}, u32[]{:S(2)}) collective-permute-start(f32[20,4,128]{2,1,0:T(4,128)S(1)} %get-tuple-element.30), channel_id=1, source_target_pairs={{0,3},{1,2},{2,1},{3,0},{4,7},{5,6},{6,5},{7,4},{8,11},{9,10},{10,... | collective-permute-start | bytes 122888 | tf_op jit(solution)/shard_map/ppermute | solution.py:560
  10.2 3.5 %collective-permute-start.3 = (f32[20,4,128]{2,1,0:T(4,128)S(1)}, f32[20,4,128]{2,1,0:T(4,128)S(1)}, u32[]{:S(2)}, u32[]{:S(2)}) collective-permute-start(f32[20,4,128]{2,1,0:T(4,128)S(1)} %get-tuple-element.30), channel_id=1, source_target_pairs={{0,1},{1,0},{2,3},{3,2},{4,5},{5,4},{6,7},{7,6},{8,9},{9,8},{10,11... | collective-permute-start | bytes 122888 | tf_op jit(solution)/shard_map/ppermute | solution.py:559
  20.2 8.3 %collective-permute-start.5 = (f32[7,8,128]{2,1,0:T(8,128)S(1)}, f32[7,8,128]{2,1,0:T(8,128)S(1)}, u32[]{:S(2)}, u32[]{:S(2)}) collective-permute-start(f32[7,8,128]{2,1,0:T(8,128)S(1)} %get-tuple-element.39), channel_id=1, source_target_pairs={{0,4},{4,8},{8,12},{12,0},{1,5},{5,9},{9,13},{13,1},{2,6},{6,10},{... | collective-permute-start | bytes 86024 | tf_op jit(solution)/shard_map/ppermute | solution.py:520
  21.6 6.9 %collective-permute-start.6 = (f32[7,8,128]{2,1,0:T(8,128)S(1)}, f32[7,8,128]{2,1,0:T(8,128)S(1)}, u32[]{:S(2)}, u32[]{:S(2)}) collective-permute-start(f32[7,8,128]{2,1,0:T(8,128)S(1)} %get-tuple-element.40), channel_id=1, source_target_pairs={{0,12},{4,0},{8,4},{12,8},{1,13},{5,1},{9,5},{13,9},{2,14},{6,2},{... | collective-permute-start | bytes 86024 | tf_op jit(solution)/shard_map/ppermute | solution.py:520
  24.1 4.5 %collective-permute-start.7 = (f32[8,128]{1,0:T(8,128)S(1)}, f32[8,128]{1,0:T(8,128)S(1)}, u32[]{:S(2)}, u32[]{:S(2)}) collective-permute-start(f32[8,128]{1,0:T(8,128)S(1)} %get-tuple-element.38.sums_ref), channel_id=1, source_target_pairs={{0,8},{4,12},{8,0},{12,4},{1,9},{5,13},{9,1},{13,5},{2,10},{6,14},... | collective-permute-start | bytes 12296 | tf_op jit(solution)/shard_map/ppermute | solution.py:520
  28.7 3.2 %collective-permute-start.8 = (f32[4,8,128]{2,1,0:T(8,128)S(1)}, f32[4,8,128]{2,1,0:T(8,128)S(1)}, u32[]{:S(2)}, u32[]{:S(2)}) collective-permute-start(f32[4,8,128]{2,1,0:T(8,128)S(1)} %get-tuple-element.42), channel_id=1, source_target_pairs={{0,2},{2,1},{1,3},{3,0},{4,6},{6,5},{5,7},{7,4},{8,10},{10,9},{9,1... | collective-permute-start | bytes 49160 | tf_op jit(solution)/shard_map/ppermute | solution.py:527
  29.7 3.7 %collective-permute-start.9 = (f32[4,8,128]{2,1,0:T(8,128)S(1)}, f32[4,8,128]{2,1,0:T(8,128)S(1)}, u32[]{:S(2)}, u32[]{:S(2)}) collective-permute-start(f32[4,8,128]{2,1,0:T(8,128)S(1)} %get-tuple-element.43), channel_id=1, source_target_pairs={{0,3},{2,0},{1,2},{3,1},{4,7},{6,4},{5,6},{7,5},{8,11},{10,8},{9,1... | collective-permute-start | bytes 49160 | tf_op jit(solution)/shard_map/ppermute | solution.py:527
  30.5 1.2 %collective-permute-start.10 = (f32[8,128]{1,0:T(8,128)S(1)}, f32[8,128]{1,0:T(8,128)S(1)}, u32[]{:S(2)}, u32[]{:S(2)}) collective-permute-start(f32[8,128]{1,0:T(8,128)S(1)} %get-tuple-element.44.sums_ref), channel_id=1, source_target_pairs={{0,1},{1,0},{2,3},{3,2},{4,5},{5,4},{6,7},{7,6},{8,9},{9,8},{10,11... | collective-permute-start | bytes 12296 | tf_op jit(solution)/shard_map/ppermute | solution.py:636
  40.6 10.0 %all-to-all-start = ((f32[16,2,128]{2,1,0:T(2,128)}), f32[16,2,128]{2,1,0:T(2,128)S(1)}, u32[]{:S(2)}, u32[]{:S(2)}) async-start(f32[16,2,128]{2,1,0:T(2,128)} %get-tuple-element.48), calls=%async_computation | async-start | bytes 32768 | tf_op jit(solution)/shard_map/all_to_all | solution.py:675
  44.1 3.8 %collective-permute-start.11 = (f32[8,4,128]{2,1,0:T(4,128)S(1)}, f32[8,4,128]{2,1,0:T(4,128)S(1)}, u32[]{:S(2)}, u32[]{:S(2)}) collective-permute-start(f32[8,4,128]{2,1,0:T(4,128)S(1)} %get-tuple-element.47), channel_id=1, source_target_pairs={{0,2},{2,0},{1,3},{3,1},{4,6},{6,4},{5,7},{7,5},{8,10},{10,8},{9,1... | collective-permute-start | bytes 49160 | tf_op jit(solution)/shard_map/ppermute | solution.py:674
